TPU v7x, 32 devices: a whole 2x2x4 slice. The times are simulated.
32 devices in a mesh: group: 2 (over y), adapter: 8 (over z, core), tensor: 2 (over x), sub: 1.
Axes of the slice: x: 2, y: 2, z: 4, core: 2. Of those that a mesh axis runs over, the one named last changes fastest.
Arguments:
- tokens: bfloat16 [4096, 8192], P(('group', 'adapter'), ('tensor', 'sub')), parts along dimension 0, may hold values from -6 to 6
- token_adapter_index: int32 [4096], P(('group', 'adapter')), parts along dimension 0, may hold values from 0 to 63, as said below
- table: int32 [128], P('group'), parts along dimension 0, may hold values from 0 to 63, as said below
- value_matrix: bfloat16 [8192, 1024], P(('tensor', 'sub')), may hold values from -0.0625 to 0.0625
- shrink_weight: float32 [8192, 1024], P(('tensor', 'sub'), 'adapter'), may hold values from -0.0625 to 0.0625
- expand_weight: float32 [64, 16, 1024], P('adapter', None, ('tensor', 'sub')), may hold values from -1.5 to 1.5
Outputs:
- values: bfloat16 [4096, 1024], P(('group', 'adapter'), ('tensor', 'sub')), parts along dimension 0
There are 2 independent parts, one for each index of `group`. A program takes and returns all parts, laid end to end along the dimension named above; an argument that names none is the same for every part. Nothing has to cross between parts.
Inputs may be any that keep to these rules, and one draw needn't show every extreme that they name: A permutation: adapter a sits in slot table[a], which index table[a] // 8 of the adapter axis holds. `token_adapter_index`: among the 256 tokens of one index of the adapter axis, at most 128 use adapters held by any one index.
All inputs are finite; a program needn't handle non-finite values.
Results may differ from a plain program's by a relative error of at most 0.00115.
Values may be sent and summed in bfloat16 or wider, within the bound.
No kernel may reach another device: no remote copies, remote signals or barrier semaphores. Data moves between devices by JAX's collectives and lax.ppermute only.
A program may use at most 64 MiB of HBM per device.

v0:
```python
import jax
import jax.numpy as jnp
from jax import lax
from jax.sharding import PartitionSpec as P

SCALING = 0.5


def shrink_masked(fragments, shrink_weight, resident_count, rank_length):
    incoming, labels = fragments
    flattened = incoming.reshape(-1, incoming.shape[2])
    label_flat = labels.reshape(-1)
    item_total = flattened.shape[0]
    shrunk = jnp.dot(
        flattened,
        shrink_weight,
        precision=lax.Precision.HIGHEST,
        preferred_element_type=jnp.float32,
    )
    choose = (
        label_flat[:, None] == lax.broadcasted_iota(jnp.int32, (item_total, resident_count), 1)
    ).astype(jnp.float32)
    selected = shrunk.reshape(item_total, resident_count, rank_length) * choose[:, :, None]
    return selected.reshape(item_total, resident_count * rank_length)


def per_device(tokens, token_adapter_index, table, value_matrix, shrink_weight, expand_weight):
    row_count, feat_width = tokens.shape
    owner_count = lax.axis_size("adapter")
    resident_count, rank_length, column_span = expand_weight.shape
    capacity = 4 * row_count // owner_count
    slot_count = owner_count * capacity
    adapter_total = table.shape[0]
    matches = token_adapter_index[:, None] == lax.broadcasted_iota(
        jnp.int32, (row_count, adapter_total), 1
    )
    slot_number = jnp.sum(jnp.where(matches, table[None, :], 0), axis=1)
    owner_index = slot_number // resident_count
    held_index = slot_number % resident_count
    owner_match = (
        owner_index[:, None] == lax.broadcasted_iota(jnp.int32, (row_count, owner_count), 1)
    ).astype(jnp.int32)
    position = jnp.sum(jnp.cumsum(owner_match, axis=0) * owner_match, axis=1) - 1
    destination = owner_index * capacity + position
    source = (
        jnp.zeros((slot_count,), jnp.int32)
        .at[destination]
        .set(jnp.arange(row_count, dtype=jnp.int32))
    )
    filled = jnp.zeros((slot_count,), jnp.bool_).at[destination].set(True)
    packed = jnp.where(filled[:, None], tokens[source], jnp.zeros((), tokens.dtype))
    packed = packed.reshape(owner_count, capacity, feat_width)
    labels = jnp.where(filled, held_index[source], -1).reshape(owner_count, capacity)
    complete_expand = lax.all_gather(expand_weight, ("tensor", "sub"), axis=2, tiled=True)
    expand_matrix = complete_expand.reshape(resident_count * rank_length, complete_expand.shape[2])
    fragments = (
        lax.all_to_all(packed, "adapter", split_axis=0, concat_axis=0, tiled=True),
        lax.all_to_all(labels, "adapter", split_axis=0, concat_axis=0, tiled=True),
    )
    selected = shrink_masked(fragments, shrink_weight, resident_count, rank_length)
    outgoing = SCALING * jnp.dot(
        selected, expand_matrix, precision=lax.Precision.HIGHEST, preferred_element_type=jnp.float32
    )
    outgoing = outgoing.reshape(
        fragments[0].shape[0], fragments[0].shape[1], expand_matrix.shape[1]
    )
    gathered_output = lax.all_to_all(outgoing, "adapter", split_axis=0, concat_axis=0, tiled=True)
    adapter_update = gathered_output.reshape(slot_count, gathered_output.shape[2])[destination]
    matrix_product = lax.dot_general(
        value_matrix, tokens, (((0,), (1,)), ((), ())), preferred_element_type=jnp.float32
    )
    base_output = lax.psum_scatter(
        matrix_product + jnp.transpose(adapter_update),
        ("tensor", "sub"),
        scatter_dimension=0,
        tiled=True,
    )
    return jnp.transpose(base_output).astype(jnp.bfloat16)


def solution(mesh):
    placed = (
        P(("group", "adapter"), ("tensor", "sub")),
        P(("group", "adapter")),
        P("group"),
        P(("tensor", "sub"), None),
        P(("tensor", "sub"), "adapter"),
        P("adapter", None, ("tensor", "sub")),
    )
    return jax.shard_map(
        per_device,
        mesh=mesh,
        in_specs=placed,
        out_specs=P(("group", "adapter"), ("tensor", "sub")),
        check_vma=False,
    )
```

profile of v0, /device:TPU:0, one launch (start us, length us, event | category | flops | bytes accessed | tf_op | source)
XLA Modules:
  0.0 384.6 jit_solution(11274641833885576704)
XLA Ops:
  6.5 0.0 copy-start
  6.5 0.9 select_reduce_fusion
  7.5 0.6 reduce-window.6
  8.1 0.2 slice_reduce_fusion
  8.4 0.1 fusion.1
  8.5 1.4 scatter_custom_fusion.1
  9.9 1.5 scatter_custom_fusion
  11.4 6.8 %gather_fusion.1 = s32[1024]{0:T(1024)S(1)} fusion(s32[256]{0:T(256)S(1)} %get-tuple-element.5, s32[1024]{0:T(1024)S(1)} %fusion.3), kind=kCustom, calls=%fused_computation.1 | custom fusion | bytes 12288 | tf_op jit(solution)/shard_map/gather | solution.py:53
  18.3 0.6 broadcast_select_fusion.1
  18.9 6.3 %all-to-all-start.1 = ((s32[8,1,128]{2,1,0:T(1,128)}), s32[8,1,128]{2,1,0:T(1,128)S(1)}, u32[]{:S(2)}, u32[]{:S(2)}) async-start(s32[8,1,128]{2,1,0:T(1,128)} %bitcast.12), calls=%async_computation.1 | async-start | bytes 8192 | tf_op jit(solution)/shard_map/all_to_all | solution.py:58
  25.2 0.0 copy-done
  25.2 7.8 %gather_fusion = bf16[1024,4096]{1,0:T(8,128)(2,1)} fusion(bf16[256,4096]{1,0:T(8,128)(2,1)S(1)} %copy-done, s32[1024]{0:T(1024)S(1)} %fusion.3), kind=kCustom, calls=%fused_computation | custom fusion | bytes 16781312 | tf_op jit(solution)/shard_map/gather | solution.py:51
  33.0 7.2 %broadcast_select_fusion = bf16[8,128,4096]{2,1,0:T(8,128)(2,1)} fusion(bf16[8,128,4096]{2,1,0:T(8,128)(2,1)} %bitcast.41, pred[8,128]{1,0:T(8,128)(4,1)S(1)} %bitcast.46), kind=kLoop, calls=%fused_computation.5 | loop fusion | flops 4194304 | bytes 16778240 | tf_op jit(solution)/shard_map/jit(_where)/select_n | solution.py:51
  40.2 0.0 all-to-all-done.1
  40.2 5.1 %all-to-all-start = ((bf16[8,128,4096]{2,1,0:T(8,128)(2,1)}), bf16[8,128,4096]{2,1,0:T(8,128)(2,1)}, u32[]{:S(2)}, u32[]{:S(2)}) async-start(bf16[8,128,4096]{2,1,0:T(8,128)(2,1)} %broadcast_select_fusion), calls=%async_computation | async-start | bytes 16777216 | tf_op jit(solution)/shard_map/all_to_all | solution.py:57
  45.3 0.0 copy-start.1
  45.3 3.0 copy.12
  48.3 0.0 copy-done.1
  48.3 9.4 %all_gather.3 = f32[8,16,1024]{2,1,0:T(8,128)S(1)} all-gather(f32[8,16,512]{2,1,0:T(8,128)S(1)} %copy-done.1), channel_id=1, replica_groups=mesh['group'=2,'adapter'=8,'tensor'=2,'sub'=1] {'tensor','sub'}, dimensions={2}, use_global_device_ids=true | all-gather | bytes 786432 | tf_op jit(solution)/shard_map/all_gather | solution.py:54
  57.7 171.6 %all-to-all-done = bf16[8,128,4096]{2,1,0:T(8,128)(2,1)} async-done(((bf16[8,128,4096]{2,1,0:T(8,128)(2,1)}), bf16[8,128,4096]{2,1,0:T(8,128)(2,1)}, u32[]{:S(2)}, u32[]{:S(2)}) %all-to-all-start) | async-done | bytes 8388640 | tf_op jit(solution)/shard_map/all_to_all | solution.py:57
  229.3 11.4 %convolution_multiply_fusion = f32[1024,8,16]{0,2,1:T(8,128)S(1)} fusion(bf16[1024,4096,1]{1,0,2:T(8,128)(2,1)} %bitcast.9, f32[8,16,4096]{2,1,0:T(8,128)} %bitcast.43, f32[1024,8]{0,1:T(8,128)S(1)} %fusion), kind=kOutput, calls=%fused_computation.8 | convolution fusion | flops 6442582016 | bytes 11042816 | tf_op jit(solution)/shard_map/dot_general | solution.py:14
  240.7 5.1 %bitcast_multiply_fusion = f32[1024,1024]{1,0:T(8,128)} fusion(f32[1024,8,16]{0,2,1:T(8,128)S(1)} %convolution_multiply_fusion, f32[8,16,1024]{2,1,0:T(8,128)S(1)} %all_gather.3), kind=kOutput, calls=%fused_computation.6 | convolution fusion | flops 1611661312 | bytes 5242880 | tf_op jit(solution)/shard_map/dot_general | solution.py:61
  245.8 4.5 %all-to-all-start.2 = ((f32[8,128,1024]{2,1,0:T(8,128)}), f32[8,128,1024]{2,1,0:T(8,128)}, u32[]{:S(2)}, u32[]{:S(2)}) async-start(f32[8,128,1024]{2,1,0:T(8,128)} %bitcast.42), calls=%async_computation.2 | async-start | bytes 8388608 | tf_op jit(solution)/shard_map/all_to_all | solution.py:67
  250.4 0.2 reduce-scatter.2.cloned.1.call-start
  250.6 93.8 %all-to-all-done.2 = f32[8,128,1024]{2,1,0:T(8,128)} async-done(((f32[8,128,1024]{2,1,0:T(8,128)}), f32[8,128,1024]{2,1,0:T(8,128)}, u32[]{:S(2)}, u32[]{:S(2)}) %all-to-all-start.2) | async-done | bytes 4194336 | tf_op jit(solution)/shard_map/all_to_all | solution.py:67
  344.4 3.8 gather_fusion.2
  348.1 1.3 copy.13
  349.5 7.0 %convolution_add_fusion = f32[1024,256]{1,0:T(8,128)} fusion(bf16[4096,1024]{1,0:T(8,128)(2,1)} %param.9, bf16[256,4096]{1,0:T(8,128)(2,1)S(1)} %copy-done, f32[256,1024]{0,1:T(8,128)} %copy.13), kind=kOutput, calls=%fused_computation.7 | convolution fusion | flops 2147745792 | bytes 12582912 | tf_op jit(solution)/shard_map/dot_general | solution.py:69
  356.4 0.0 reduce-scatter.2.cloned.1.call-update
  356.5 19.4 %reduce-scatter.2.cloned.1.call-done = f32[512,256]{1,0:T(8,128)} async-done(((f32[1024,256]{1,0:T(8,128)}), f32[512,256]{1,0:T(8,128)}) %reduce-scatter.2.cloned.1.call-update) | async-done | bytes 524304 | tf_op jit(solution)/shard_map/reduce_scatter | solution.py:72
  375.8 1.1 convert_bitcast_fusion
  376.9 0.8 copy.14
  (12 shorter events, 0.1 us)
Async XLA Ops:
  6.5 18.6 %copy-start = (bf16[256,4096]{1,0:T(8,128)(2,1)S(1)}, bf16[256,4096]{1,0:T(8,128)(2,1)}, u32[]{:S(2)}) copy-start(bf16[256,4096]{1,0:T(8,128)(2,1)} %param.6) | copy-start | bytes 6291460
  18.9 21.4 %all-to-all-start.1 = ((s32[8,1,128]{2,1,0:T(1,128)}), s32[8,1,128]{2,1,0:T(1,128)S(1)}, u32[]{:S(2)}, u32[]{:S(2)}) async-start(s32[8,1,128]{2,1,0:T(1,128)} %bitcast.12), calls=%async_computation.1 | async-start | bytes 8192 | tf_op jit(solution)/shard_map/all_to_all | solution.py:58
  40.2 189.1 %all-to-all-start = ((bf16[8,128,4096]{2,1,0:T(8,128)(2,1)}), bf16[8,128,4096]{2,1,0:T(8,128)(2,1)}, u32[]{:S(2)}, u32[]{:S(2)}) async-start(bf16[8,128,4096]{2,1,0:T(8,128)(2,1)} %broadcast_select_fusion), calls=%async_computation | async-start | bytes 16777216 | tf_op jit(solution)/shard_map/all_to_all | solution.py:57
  45.3 3.0 copy-start.1
  245.8 98.6 %all-to-all-start.2 = ((f32[8,128,1024]{2,1,0:T(8,128)}), f32[8,128,1024]{2,1,0:T(8,128)}, u32[]{:S(2)}, u32[]{:S(2)}) async-start(f32[8,128,1024]{2,1,0:T(8,128)} %bitcast.42), calls=%async_computation.2 | async-start | bytes 8388608 | tf_op jit(solution)/shard_map/all_to_all | solution.py:67
  250.4 125.5 %reduce-scatter.2.cloned.1.call-start = ((), (), s32[]{:S(2)}) async-start(), calls=%async_computation.4 | async-start | bytes 1572864 | tf_op jit(solution)/shard_map/reduce_scatter | solution.py:72
Sparse Core Ops, SparseCore 0:
  356.6 19.1 reduce-scatter.1
where the time goes:
time: 385 us
  waiting for transfers between devices  285 us (74%)
  local copies, waits for them, and re-layouts  26.7 us (7%)
  matrix products  23.5 us (6%)
  starting transfers between devices  16.2 us (4%)
  between operations  13.5 us (4%)
  other arithmetic  10.6 us (3%)
  blocking collectives  9.37 us (2%)
    all_to_all x1, waiting for transfers between devices, per_device(): lax.all_to_all(packed, 'adapter', split_axis=0, concat_axis=0, tiled=True)  172 us
    all_to_all x1, waiting for transfers between devices, per_device(): lax.all_to_all(outgoing, 'adapter', split_axis=0, concat_axis=0, tiled=True)  93.8 us
    reduce_scatter x1, waiting for transfers between devices, per_device(): lax.psum_scatter(matrix_product + jnp.transpose(adapter_update), ('tensor...  19.4 us
    dot_general x1, matrix products, shrink_masked(): jnp.dot(flattened, shrink_weight, precision=lax.Precision.HIGHEST, prefer...  11.4 us
    all_gather x1, blocking collectives, per_device(): lax.all_gather(expand_weight, ('tensor', 'sub'), axis=2, tiled=True)  9.37 us
    gather x1, local copies, waits for them, and re-layouts, per_device(): tokens[source]  7.82 us
  transfers between devices with their start and end apart: 4, of which 3 were waited for; matrix products, arithmetic and copies ran while one was open for 5% of the time, Pallas kernels for 0%

commit v1 on v0

v1 whole, which is shorter than its diff:
```python
import jax
import jax.numpy as jnp
from jax import lax
from jax.sharding import PartitionSpec as P

SCALING = 0.5
SHRINK_GAIN = 2.0**19
EXPAND_GAIN = 2.0**14


def chain(piece, half, spots):
    def shift(value, step, senders):
        pairs = [(2 * s + c, 2 * (s + step) + c) for s in senders for c in range(2)]
        return lax.ppermute(value, "adapter", pairs)

    found = [(piece, half)]
    up = down = piece
    merged = None
    for step in range(1, spots):
        goes_up = list(range(step - 1, spots - 1))
        goes_down = list(range(1, spots - step + 1))
        source = jnp.where(half >= step, half - step, half + step)
        valid = (half >= step) | (half + step < spots)
        if 2 * step - 1 > spots:
            pairs = [(2 * s + c, 2 * (s + 1) + c) for s in goes_up for c in range(2)]
            pairs += [(2 * s + c, 2 * (s - 1) + c) for s in goes_down for c in range(2)]
            merged = lax.ppermute(merged, "adapter", pairs)
        else:
            up, down = shift(up, 1, goes_up), shift(down, -1, goes_down)
            if 2 * step > spots - 1:
                merged = jnp.where(half >= step, up, down)
            else:
                found.append((up, jnp.where(half >= step, half - step, -1)))
                found.append((down, jnp.where(half + step < spots, half + step, -1)))
                continue
        found.append((merged, jnp.where(valid, source, -1)))
    return found


def two_terms(value):
    wide = value.astype(jnp.float32)
    high = lax.reduce_precision(wide, exponent_bits=8, mantissa_bits=7)
    return high.astype(jnp.bfloat16), (wide - high).astype(jnp.bfloat16)


def per_device(tokens, token_adapter_index, table, value_matrix, shrink_weight, expand_weight):
    rows, width = tokens.shape
    resident, rank, span = expand_weight.shape
    held = resident * rank
    owners = lax.axis_size("adapter")
    spots = owners // 2
    quarter = width // 4
    g, a = lax.axis_index("group"), lax.axis_index("adapter")
    c, half = a % 2, a // 2
    core_pairs = [(i, i ^ 1) for i in range(owners)]
    swap = [(0, 1), (1, 0)]

    def over_core(value):
        return lax.ppermute(value, "adapter", core_pairs)

    def over_group(value):
        return lax.ppermute(value, "group", swap)

    flat_expand = expand_weight.reshape(held, span)

    def encoded(side):
        place = 2 * side + g
        shrink = lax.dynamic_slice_in_dim(shrink_weight, place * quarter, quarter, 0)
        expand = lax.dynamic_slice_in_dim(flat_expand, place * (span // 4), span // 4, 1)
        return jnp.concatenate(
            [
                (shrink * SHRINK_GAIN).astype(jnp.float16),
                (expand * EXPAND_GAIN).astype(jnp.float16).reshape(-1, held),
            ],
            axis=0,
        )

    given = over_core(encoded(1 - c))
    mine = encoded(c)
    chains = [(chain(mine, half, spots), c), (chain(given, half, spots), 1 - c)]

    matches = token_adapter_index[:, None] == lax.broadcasted_iota(
        jnp.int32, (rows, table.shape[0]), 1
    )
    slot = jnp.sum(jnp.where(matches, table[None, :], 0), axis=1)
    keep = lax.dynamic_slice_in_dim(tokens, c * 2 * quarter, 2 * quarter, 1)
    give = lax.dynamic_slice_in_dim(tokens, (1 - c) * 2 * quarter, 2 * quarter, 1)
    pair = jnp.concatenate([keep, over_core(give)], axis=0)
    pair_slot = jnp.concatenate([slot, over_core(slot)])
    own_part = lax.dynamic_slice_in_dim(pair, g * quarter, quarter, 1)
    other_part = lax.dynamic_slice_in_dim(pair, (1 - g) * quarter, quarter, 1)
    every = jnp.concatenate([own_part, over_group(other_part)], axis=0)
    every_slot = jnp.concatenate([pair_slot, over_group(pair_slot)])

    partial = jnp.dot(tokens, value_matrix, preferred_element_type=jnp.float32)
    axes = ("tensor", "sub")
    two = lax.axis_size("tensor") == 2 and lax.axis_size("sub") == 1
    if two:
        x = lax.axis_index("tensor")
        sent = lax.dynamic_slice_in_dim(partial, (1 - x) * span, span, 1)
        base = lax.dynamic_slice_in_dim(partial, x * span, span, 1) + lax.ppermute(
            sent, "tensor", swap
        )
    else:
        base = lax.psum_scatter(partial, axes, scatter_dimension=1, tiled=True)

    lane_slot = lax.broadcasted_iota(jnp.int32, (1, held), 1) // rank
    total = jnp.zeros((every.shape[0], held), jnp.float32)
    for pieces, side in chains:
        for piece, source in pieces:
            high, low = two_terms(piece[:quarter])
            product = jnp.dot(
                every, jnp.concatenate([high, low], axis=1), preferred_element_type=jnp.float32
            )
            first = jnp.where(source < 0, -(2**20), (2 * source + side) * resident)
            total = jnp.where(
                every_slot[:, None] == lane_slot + first,
                product[:, :held] + product[:, held:],
                total,
            )
    compact = jnp.sum(total.reshape(-1, resident, rank), axis=1)
    compact = jnp.transpose(compact)
    pair_sum = compact[:, : 2 * rows] + over_group(compact[:, 2 * rows :])
    own_sum = pair_sum[:, :rows] + over_core(pair_sum[:, rows:])
    if two:
        own_sum = own_sum + lax.ppermute(own_sum, "tensor", swap)
    else:
        own_sum = lax.psum(own_sum, axes)

    parts = [[piece[quarter:].reshape(held, span // 4) for piece, _ in pieces] for pieces, _ in chains]
    count = len(parts[0])
    quarter_rows = jnp.concatenate(parts[0] + parts[1], axis=0)
    other = over_group(quarter_rows)
    half_rows = jnp.concatenate(
        [jnp.where(g == 0, quarter_rows, other), jnp.where(g == 0, other, quarter_rows)], axis=1
    )
    came = over_core(half_rows)
    came = jnp.concatenate([came[count * held :], came[: count * held]], axis=0)
    whole = jnp.concatenate(
        [jnp.where(c == 0, half_rows, came), jnp.where(c == 0, came, half_rows)], axis=1
    )
    spread = jnp.tile(jnp.transpose(own_sum), (1, resident))
    masked = jnp.concatenate(
        [
            jnp.where(
                slot[:, None]
                == lane_slot + jnp.where(source < 0, -(2**20), (2 * source + side) * resident),
                spread,
                0.0,
            )
            for pieces, side in chains
            for _, source in pieces
        ],
        axis=1,
    )
    masked_high, masked_low = two_terms(masked)
    whole_high, whole_low = two_terms(whole)
    update = (
        jnp.dot(masked_high, whole_high, preferred_element_type=jnp.float32)
        + jnp.dot(masked_low, whole_high, preferred_element_type=jnp.float32)
        + jnp.dot(masked_high, whole_low, preferred_element_type=jnp.float32)
    )
    return (base + (SCALING / (SHRINK_GAIN * EXPAND_GAIN)) * update).astype(jnp.bfloat16)


def solution(mesh):
    placed = (
        P(("group", "adapter"), ("tensor", "sub")),
        P(("group", "adapter")),
        P("group"),
        P(("tensor", "sub"), None),
        P(("tensor", "sub"), "adapter"),
        P("adapter", None, ("tensor", "sub")),
    )
    return jax.shard_map(
        per_device,
        mesh=mesh,
        in_specs=placed,
        out_specs=P(("group", "adapter"), ("tensor", "sub")),
        check_vma=False,
    )
```

time: 385 us -> 117 us (0.30)
  waiting for transfers between devices: 285 us -> 51.1 us
  local copies, waits for them, and re-layouts: 26.7 us -> 3.96 us
  starting transfers between devices: 16.2 us -> 29.6 us
  between operations: 13.5 us -> 0.61 us
  blocking collectives: 9.37 us -> 0 us
  matrix products: 23.5 us -> 16.8 us
    all_to_all x3 -> x0, waiting for transfers between devices: 265 us -> none  [the longest x1 172 us: per_device(): lax.all_to_all(packed, 'adapter', split_axis=0, concat_axis=0, tiled=True)]
    ppermute x0 -> x21, waiting for transfers between devices: none -> 51.1 us  [the longest x4 22.7 us: over_group(): return lax.ppermute(value, 'group', swap)]
    ppermute x0 -> x21, starting transfers between devices: none -> 29.6 us  [the longest x8 16.7 us: shift(): return lax.ppermute(value, 'adapter', pairs)]
    gather x4 -> x0, local copies, waits for them, and re-layouts: 19.7 us -> none  [the longest x1 7.82 us: per_device(): tokens[source]]
    reduce_scatter x1 -> x0, waiting for transfers between devices: 19.4 us -> none  [per_device(): lax.psum_scatter(matrix_product + jnp.transpose(adapter_update), ('tensor...]
    all_to_all x3 -> x0, starting transfers between devices: 16 us -> none  [the longest x1 6.33 us: per_device(): lax.all_to_all(labels, 'adapter', split_axis=0, concat_axis=0, tiled=True)]
    all_gather x1 -> x0, blocking collectives: 9.37 us -> none  [per_device(): lax.all_gather(expand_weight, ('tensor', 'sub'), axis=2, tiled=True)]
    dot_general x3 -> x14, matrix products: 23.5 us -> 16.8 us  [the longest x10 7.59 us: per_device(): jnp.dot(every, jnp.concatenate([high, low], axis=1), preferred_element_ty...]
  transfers between devices with their start and end apart: 4 -> 21, of which waited for: 3 -> 8; matrix products, arithmetic and copies ran while one was open for 5% -> 25% of each run, Pallas kernels for 0% -> 0%
where the time goes in v1:
time: 117 us; the launch traced here: 116 us
  waiting for transfers between devices  51.1 us (44%)
  starting transfers between devices  29.6 us (25%)
  matrix products  16.8 us (14%)
  other arithmetic  14.3 us (12%)
  local copies, waits for them, and re-layouts  3.96 us (3%)
    ppermute x4, waiting for transfers between devices, over_group(): return lax.ppermute(value, 'group', swap)  22.7 us
    ppermute x8, waiting for transfers between devices, shift(): return lax.ppermute(value, 'adapter', pairs)  20.2 us
    ppermute x8, starting transfers between devices, shift(): return lax.ppermute(value, 'adapter', pairs)  16.7 us
    dot_general x10, matrix products, per_device(): jnp.dot(every, jnp.concatenate([high, low], axis=1), preferred_element_ty...  7.59 us
    dot_general x1, matrix products, per_device(): partial = jnp.dot(tokens, value_matrix, preferred_element_type=jnp.float32)  6.83 us
    convert_element_type x11, other arithmetic, two_terms(): return (high.astype(jnp.bfloat16), (wide - high).astype(jnp.bfloat16))  6.46 us
    ppermute x4, starting transfers between devices, over_group(): return lax.ppermute(value, 'group', swap)  6.32 us
    ppermute x1, waiting for transfers between devices, per_device(): own_sum = own_sum + lax.ppermute(own_sum, 'tensor', swap)  4.23 us
  transfers between devices with their start and end apart: 21, of which 8 were waited for; matrix products, arithmetic and copies ran while one was open for 25% of the time, Pallas kernels for 0%

profile of v1, /device:TPU:0, one launch (start us, length us, event | category | flops | bytes accessed | tf_op | source)
XLA Modules:
  0.0 116.3 jit_solution(3007497708796482669)
XLA Ops:
  0.0 1.6 %constant_dynamic-update-slice_fusion.19 = (f16[1280,128]{1,0:T(8,128)(2,1)}, f16[128,128]{1,0:T(8,128)(2,1)S(1)}) fusion(f32[128,512]{1,0:T(8,128)} %bitcast.21, s32[]{:T(128)S(6)} %select_n.292), kind=kLoop, calls=%fused_computation.155 | loop fusion | flops 32767 | bytes 131076
  1.6 2.0 %reduce-precision_convert_fusion.4 = (bf16[1024,128]{1,0:T(8,128)(2,1)}, f16[1024,128]{1,0:T(8,128)(2,1)S(1)}, f16[1024,128]{1,0:T(8,128)(2,1)S(1)}) fusion(f32[4096,128]{1,0:T(8,128)} %param.10, s32[]{:T(128)S(6)} %select_n.291, s32[]{:T(128)S(6)} %select_n.279), kind=kLoop, calls=%fused_computation.20 | loop fusion | flops 917504 | bytes 1835016 | tf_op jit(solution)/shard_map/convert_element_type | solution.py:43
  4.5 5.6 %collective-permute-start.11 = (f16[1152,128]{1,0:T(8,128)(2,1)}, f16[1152,128]{1,0:T(8,128)(2,1)}, u32[]{:S(2)}, u32[]{:S(2)}) collective-permute-start(f16[1152,128]{1,0:T(8,128)(2,1)} %pad_maximum_fusion.8), channel_id=1, source_target_pairs={{0,4},{2,6},{4,8},{6,10},{8,12},{10,14},{1,5},{3,7},{5,9},{7,11},{... | collective-permute-start | bytes 884744 | tf_op jit(solution)/shard_map/ppermute | solution.py:14
  10.1 1.3 %collective-permute-start.13 = (f16[1152,128]{1,0:T(8,128)(2,1)}, f16[1152,128]{1,0:T(8,128)(2,1)}, u32[]{:S(2)}, u32[]{:S(2)}) collective-permute-start(f16[1152,128]{1,0:T(8,128)(2,1)} %pad_maximum_fusion.8), channel_id=1, source_target_pairs={{4,0},{6,2},{8,4},{10,6},{12,8},{14,10},{5,1},{7,3},{9,5},{11,7},{... | collective-permute-start | bytes 884744 | tf_op jit(solution)/shard_map/ppermute | solution.py:14
  11.4 0.9 multiply_convert_fusion.3
  13.1 1.2 %constant_dynamic-slice_fusion = (bf16[256,2048]{1,0:T(8,128)(2,1)}, bf16[256,2048]{1,0:T(8,128)(2,1)S(1)}) fusion(bf16[256,4096]{1,0:T(8,128)(2,1)S(1)} %copy-done, s32[]{:T(128)S(6)} %select_n.275, s32[]{:T(128)S(6)} %select_n.274), kind=kLoop, calls=%fused_computation.160 | loop fusion | bytes 4194312 | tf_op jit(solution)/shard_map/dynamic_slice | solution.py:87
  15.7 6.8 %fusion.90 = f32[256,1024]{1,0:T(8,128)} fusion(bf16[256,4096]{1,0:T(8,128)(2,1)S(1)} %copy-done, bf16[4096,1024]{1,0:T(8,128)(2,1)} %param.9), kind=kOutput, calls=%fused_computation.192 | convolution fusion | flops 2147483648 | bytes 11534336 | tf_op jit(solution)/shard_map/dot_general | solution.py:95
  22.6 1.6 %collective-permute-start.2 = (s32[512]{0:T(512)S(1)}, s32[512]{0:T(512)S(1)}, u32[]{:S(2)}, u32[]{:S(2)}) collective-permute-start(s32[512]{0:T(512)S(1)} %pad_add_fusion.1), channel_id=1, source_target_pairs={{0,16},{16,0},{1,17},{17,1},{2,18},{18,2},{3,19},{19,3},{4,20},{20... | collective-permute-start | bytes 6152 | tf_op jit(solution)/shard_map/ppermute | solution.py:62
  24.2 2.1 %collective-permute-done.2 = s32[512]{0:T(512)S(1)} collective-permute-done((s32[512]{0:T(512)S(1)}, s32[512]{0:T(512)S(1)}, u32[]{:S(2)}, u32[]{:S(2)}) %collective-permute-start.2) | collective-permute-done | bytes 2080 | tf_op jit(solution)/shard_map/ppermute | solution.py:62
  26.3 4.6 %collective-permute-start.6 = (f16[1152,128]{1,0:T(8,128)(2,1)}, f16[1152,128]{1,0:T(8,128)(2,1)S(1)}, u32[]{:S(2)}, u32[]{:S(2)}) collective-permute-start(f16[1152,128]{1,0:T(8,128)(2,1)} %collective-permute-done.5), channel_id=1, source_target_pairs={{0,4},{2,6},{4,8},{6,10},{8,12},{10,14},{1,5},{3,7},{5,9},{7,11},{... | collective-permute-start | bytes 884744 | tf_op jit(solution)/shard_map/ppermute | solution.py:14
  30.8 1.3 %collective-permute-start.8 = (f16[1152,128]{1,0:T(8,128)(2,1)}, f16[1152,128]{1,0:T(8,128)(2,1)S(1)}, u32[]{:S(2)}, u32[]{:S(2)}) collective-permute-start(f16[1152,128]{1,0:T(8,128)(2,1)} %collective-permute-done.5), channel_id=1, source_target_pairs={{4,0},{6,2},{8,4},{10,6},{12,8},{14,10},{5,1},{7,3},{9,5},{11,7},{... | collective-permute-start | bytes 884744 | tf_op jit(solution)/shard_map/ppermute | solution.py:14
  32.8 1.0 reduce-precision_convert_fusion.5
  33.9 1.3 %collective-permute-start.14 = (f16[1152,128]{1,0:T(8,128)(2,1)}, f16[1152,128]{1,0:T(8,128)(2,1)S(1)}, u32[]{:S(2)}, u32[]{:S(2)}) collective-permute-start(f16[1152,128]{1,0:T(8,128)(2,1)} %collective-permute-done.13), channel_id=1, source_target_pairs={{4,0},{6,2},{8,4},{10,6},{5,1},{7,3},{9,5},{11,7},{20,16},{22,18},... | collective-permute-start | bytes 884744 | tf_op jit(solution)/shard_map/ppermute | solution.py:14
  35.2 1.0 reduce-precision_convert_fusion.6
  37.8 1.0 reduce-precision_convert_fusion.9
  38.8 8.4 %collective-permute-done.14 = f16[1152,128]{1,0:T(8,128)(2,1)S(1)} collective-permute-done((f16[1152,128]{1,0:T(8,128)(2,1)}, f16[1152,128]{1,0:T(8,128)(2,1)S(1)}, u32[]{:S(2)}, u32[]{:S(2)}) %collective-permute-start.14) | collective-permute-done | bytes 294944 | tf_op jit(solution)/shard_map/ppermute | solution.py:14
  47.3 1.3 %collective-permute-start.15 = (f16[1152,128]{1,0:T(8,128)(2,1)S(1)}, f16[1152,128]{1,0:T(8,128)(2,1)S(1)}, u32[]{:S(2)}, u32[]{:S(2)}) collective-permute-start(f16[1152,128]{1,0:T(8,128)(2,1)S(1)} %broadcast_select_fusion.4), channel_id=1, source_target_pairs={{8,12},{10,14},{4,0},{6,2},{9,13},{11,15},{5,1},{7,3},{24,28},{26,... | collective-permute-start | bytes 884744 | tf_op jit(solution)/shard_map/ppermute | solution.py:27
  49.5 1.3 %collective-permute-start.9 = (f16[1152,128]{1,0:T(8,128)(2,1)S(1)}, f16[1152,128]{1,0:T(8,128)(2,1)S(1)}, u32[]{:S(2)}, u32[]{:S(2)}) collective-permute-start(f16[1152,128]{1,0:T(8,128)(2,1)S(1)} %collective-permute-done.8), channel_id=1, source_target_pairs={{4,0},{6,2},{8,4},{10,6},{5,1},{7,3},{9,5},{11,7},{20,16},{22,18},... | collective-permute-start | bytes 884744 | tf_op jit(solution)/shard_map/ppermute | solution.py:14
  51.0 11.8 %collective-permute-done.9 = f16[1152,128]{1,0:T(8,128)(2,1)S(1)} collective-permute-done((f16[1152,128]{1,0:T(8,128)(2,1)S(1)}, f16[1152,128]{1,0:T(8,128)(2,1)S(1)}, u32[]{:S(2)}, u32[]{:S(2)}) %collective-permute-start.9) | collective-permute-done | bytes 294944 | tf_op jit(solution)/shard_map/ppermute | solution.py:14
  62.9 1.5 %collective-permute-start.10 = (f16[1152,128]{1,0:T(8,128)(2,1)S(1)}, f16[1152,128]{1,0:T(8,128)(2,1)S(1)}, u32[]{:S(2)}, u32[]{:S(2)}) collective-permute-start(f16[1152,128]{1,0:T(8,128)(2,1)S(1)} %broadcast_select_fusion.5), channel_id=1, source_target_pairs={{8,12},{10,14},{4,0},{6,2},{9,13},{11,15},{5,1},{7,3},{24,28},{26,... | collective-permute-start | bytes 884744 | tf_op jit(solution)/shard_map/ppermute | solution.py:27
  65.4 1.5 %fusion.12 = (bf16[512,1024]{1,0:T(8,128)(2,1)S(1)}, bf16[512,1024]{1,0:T(8,128)(2,1)S(1)}) fusion(s32[]{:T(128)S(6)} %select_n.276, bf16[256,2048]{1,0:T(8,128)(2,1)S(1)} %get-tuple-element.12, bf16[256,2048]{1,0:T(8,128)(2,1)} %collective-permute-done.3, s32[]{:T(128)S(6)} %select_n.277), kind=kLoop, calls=%fused_computation.18 | loop fusion | flops 4194304 | bytes 4194312 | tf_op jit(solution)/shard_map/concatenate | solution.py:88
  66.9 1.6 %collective-permute-start.4 = (bf16[512,1024]{1,0:T(8,128)(2,1)S(1)}, bf16[512,1024]{1,0:T(8,128)(2,1)S(1)}, u32[]{:S(2)}, u32[]{:S(2)}) collective-permute-start(bf16[512,1024]{1,0:T(8,128)(2,1)S(1)} %get-tuple-element.10), channel_id=1, source_target_pairs={{0,16},{16,0},{1,17},{17,1},{2,18},{18,2},{3,19},{19,3},{4,20},{20... | collective-permute-start | bytes 3145736 | tf_op jit(solution)/shard_map/ppermute | solution.py:62
  68.6 2.9 %collective-permute-done.10 = f16[1152,128]{1,0:T(8,128)(2,1)S(1)} collective-permute-done((f16[1152,128]{1,0:T(8,128)(2,1)S(1)}, f16[1152,128]{1,0:T(8,128)(2,1)S(1)}, u32[]{:S(2)}, u32[]{:S(2)}) %collective-permute-start.10) | collective-permute-done | bytes 294944 | tf_op jit(solution)/shard_map/ppermute | solution.py:27
  71.5 1.6 %collective-permute-start.19 = (f16[1280,128]{1,0:T(8,128)(2,1)S(1)}, f16[1280,128]{1,0:T(8,128)(2,1)S(1)}, u32[]{:S(2)}, u32[]{:S(2)}) collective-permute-start(f16[1280,128]{1,0:T(8,128)(2,1)S(1)} %constant_dynamic-update-slice_fusion.10), channel_id=1, source_target_pairs={{0,16},{16,0},{1,17},{17,1},{2,18},{18,2},{3,19},{19,3},{4,20},{20... | collective-permute-start | bytes 983048 | tf_op jit(solution)/shard_map/ppermute | solution.py:62
  73.2 19.8 %collective-permute-done.4 = bf16[512,1024]{1,0:T(8,128)(2,1)S(1)} collective-permute-done((bf16[512,1024]{1,0:T(8,128)(2,1)S(1)}, bf16[512,1024]{1,0:T(8,128)(2,1)S(1)}, u32[]{:S(2)}, u32[]{:S(2)}) %collective-permute-start.4) | collective-permute-done | bytes 1048608 | tf_op jit(solution)/shard_map/ppermute | solution.py:62
  100.7 0.8 fusion.33
  101.6 1.6 %collective-permute-start.16 = (f32[16,512]{1,0:T(8,128)S(1)}, f32[16,512]{1,0:T(8,128)S(1)}, u32[]{:S(2)}, u32[]{:S(2)}) collective-permute-start(f32[16,512]{1,0:T(8,128)S(1)} %slice.206), channel_id=1, source_target_pairs={{0,16},{16,0},{1,17},{17,1},{2,18},{18,2},{3,19},{19,3},{4,20},{20... | collective-permute-start | bytes 98312 | tf_op jit(solution)/shard_map/ppermute | solution.py:62
  103.3 1.6 %collective-permute-start = (f32[256,512]{1,0:T(8,128)S(1)}, f32[256,512]{1,0:T(8,128)S(1)}, u32[]{:S(2)}, u32[]{:S(2)}) collective-permute-start(f32[256,512]{1,0:T(8,128)S(1)} %constant_dynamic-slice_fusion.2), channel_id=1, source_target_pairs={{0,1},{1,0},{2,3},{3,2},{4,5},{5,4},{6,7},{7,6},{8,9},{9,8},{10,11... | collective-permute-start | bytes 1572872 | tf_op jit(solution)/shard_map/ppermute | solution.py:101
  105.9 1.0 collective-permute-done.17
  106.9 1.5 %collective-permute-start.18 = (f32[16,256]{1,0:T(8,128)S(1)}, f32[16,256]{1,0:T(8,128)S(1)}, u32[]{:S(2)}, u32[]{:S(2)}) collective-permute-start(f32[16,256]{1,0:T(8,128)S(1)} %slice_add_fusion.11), channel_id=1, source_target_pairs={{0,1},{1,0},{2,3},{3,2},{4,5},{5,4},{6,7},{7,6},{8,9},{9,8},{10,11... | collective-permute-start | bytes 49160 | tf_op jit(solution)/shard_map/ppermute | solution.py:126
  108.6 4.2 %collective-permute-done.18 = f32[16,256]{1,0:T(8,128)S(1)} collective-permute-done((f32[16,256]{1,0:T(8,128)S(1)}, f32[16,256]{1,0:T(8,128)S(1)}, u32[]{:S(2)}, u32[]{:S(2)}) %collective-permute-start.18) | collective-permute-done | bytes 16416 | tf_op jit(solution)/shard_map/ppermute | solution.py:126
  115.0 1.3 %add_convert_fusion = bf16[256,512]{1,0:T(8,128)(2,1)} fusion(f32[256,512]{1,0:T(8,128)S(1)} %collective-permute-done, f32[256,1024]{1,0:T(8,128)S(1)} %copy-done.4, s32[]{:T(128)S(6)} %select_n.264, f32[256,512]{1,0:T(8,128)S(1)} %convolution_add_fusion, f16[1280,256]{1,0:T(8,128)(2,1)S(1)} %get-tuple-element.15, ...), kind=kOutput, calls=%fused_computation.123 | convolution fusion | flops 340131840 | bytes 4456452 | tf_op jit(solution)/shard_map/dot_general | solution.py:161
  (97 shorter events, 18.6 us)
Async XLA Ops:
  0.0 13.0 %copy-start = (bf16[256,4096]{1,0:T(8,128)(2,1)S(1)}, bf16[256,4096]{1,0:T(8,128)(2,1)}, u32[]{:S(2)}) copy-start(bf16[256,4096]{1,0:T(8,128)(2,1)} %param.6) | copy-start | bytes 6291460
  4.5 27.7 %collective-permute-start.11 = (f16[1152,128]{1,0:T(8,128)(2,1)}, f16[1152,128]{1,0:T(8,128)(2,1)}, u32[]{:S(2)}, u32[]{:S(2)}) collective-permute-start(f16[1152,128]{1,0:T(8,128)(2,1)} %pad_maximum_fusion.8), channel_id=1, source_target_pairs={{0,4},{2,6},{4,8},{6,10},{8,12},{10,14},{1,5},{3,7},{5,9},{7,11},{... | collective-permute-start | bytes 884744 | tf_op jit(solution)/shard_map/ppermute | solution.py:14
  10.1 23.8 %collective-permute-start.13 = (f16[1152,128]{1,0:T(8,128)(2,1)}, f16[1152,128]{1,0:T(8,128)(2,1)}, u32[]{:S(2)}, u32[]{:S(2)}) collective-permute-start(f16[1152,128]{1,0:T(8,128)(2,1)} %pad_maximum_fusion.8), channel_id=1, source_target_pairs={{4,0},{6,2},{8,4},{10,6},{12,8},{14,10},{5,1},{7,3},{9,5},{11,7},{... | collective-permute-start | bytes 884744 | tf_op jit(solution)/shard_map/ppermute | solution.py:14
  13.0 13.2 %collective-permute-start.5 = (f16[1152,128]{1,0:T(8,128)(2,1)}, f16[1152,128]{1,0:T(8,128)(2,1)}, u32[]{:S(2)}, u32[]{:S(2)}) collective-permute-start(f16[1152,128]{1,0:T(8,128)(2,1)} %pad_maximum_fusion.7), channel_id=1, source_target_pairs={{0,2},{2,0},{4,6},{6,4},{8,10},{10,8},{12,14},{14,12},{1,3},{3,1},... | collective-permute-start | bytes 884744 | tf_op jit(solution)/shard_map/ppermute | solution.py:59
  13.1 1.7 %copy-start.5 = (s32[256]{0:T(256)S(1)}, s32[256]{0:T(256)}, u32[]{:S(2)}) copy-start(s32[256]{0:T(256)} %param.7) | copy-start | bytes 3076
  13.1 1.7 %copy-start.6 = (s32[64]{0:T(128)S(1)}, s32[64]{0:T(128)}, u32[]{:S(2)}) copy-start(s32[64]{0:T(128)} %param.8) | copy-start | bytes 772
  14.2 51.1 %collective-permute-start.3 = (bf16[256,2048]{1,0:T(8,128)(2,1)}, bf16[256,2048]{1,0:T(8,128)(2,1)}, u32[]{:S(2)}, u32[]{:S(2)}) collective-permute-start(bf16[256,2048]{1,0:T(8,128)(2,1)} %get-tuple-element.11), channel_id=1, source_target_pairs={{0,2},{2,0},{4,6},{6,4},{8,10},{10,8},{12,14},{14,12},{1,3},{3,1},... | collective-permute-start | bytes 3145736 | tf_op jit(solution)/shard_map/ppermute | solution.py:59
  14.8 7.7 %collective-permute-start.1 = (s32[256]{0:T(256)S(1)}, s32[256]{0:T(256)S(1)}, u32[]{:S(2)}, u32[]{:S(2)}) collective-permute-start(s32[256]{0:T(256)S(1)} %select_reduce_fusion), channel_id=1, source_target_pairs={{0,2},{2,0},{4,6},{6,4},{8,10},{10,8},{12,14},{14,12},{1,3},{3,1},... | collective-permute-start | bytes 3080 | tf_op jit(solution)/shard_map/ppermute | solution.py:59
  15.7 20.5 %copy-start.1 = (f16[1280,128]{1,0:T(8,128)(2,1)S(1)}, f16[1280,128]{1,0:T(8,128)(2,1)}, u32[]{:S(2)}) copy-start(f16[1280,128]{1,0:T(8,128)(2,1)} %get-tuple-element.7) | copy-start | bytes 983044
  22.6 3.7 %collective-permute-start.2 = (s32[512]{0:T(512)S(1)}, s32[512]{0:T(512)S(1)}, u32[]{:S(2)}, u32[]{:S(2)}) collective-permute-start(s32[512]{0:T(512)S(1)} %pad_add_fusion.1), channel_id=1, source_target_pairs={{0,16},{16,0},{1,17},{17,1},{2,18},{18,2},{3,19},{19,3},{4,20},{20... | collective-permute-start | bytes 6152 | tf_op jit(solution)/shard_map/ppermute | solution.py:62
  26.3 22.5 %collective-permute-start.6 = (f16[1152,128]{1,0:T(8,128)(2,1)}, f16[1152,128]{1,0:T(8,128)(2,1)S(1)}, u32[]{:S(2)}, u32[]{:S(2)}) collective-permute-start(f16[1152,128]{1,0:T(8,128)(2,1)} %collective-permute-done.5), channel_id=1, source_target_pairs={{0,4},{2,6},{4,8},{6,10},{8,12},{10,14},{1,5},{3,7},{5,9},{7,11},{... | collective-permute-start | bytes 884744 | tf_op jit(solution)/shard_map/ppermute | solution.py:14
  30.8 18.7 %collective-permute-start.8 = (f16[1152,128]{1,0:T(8,128)(2,1)}, f16[1152,128]{1,0:T(8,128)(2,1)S(1)}, u32[]{:S(2)}, u32[]{:S(2)}) collective-permute-start(f16[1152,128]{1,0:T(8,128)(2,1)} %collective-permute-done.5), channel_id=1, source_target_pairs={{4,0},{6,2},{8,4},{10,6},{12,8},{14,10},{5,1},{7,3},{9,5},{11,7},{... | collective-permute-start | bytes 884744 | tf_op jit(solution)/shard_map/ppermute | solution.py:14
  32.1 6.7 %collective-permute-start.12 = (f16[1152,128]{1,0:T(8,128)(2,1)}, f16[1152,128]{1,0:T(8,128)(2,1)S(1)}, u32[]{:S(2)}, u32[]{:S(2)}) collective-permute-start(f16[1152,128]{1,0:T(8,128)(2,1)} %collective-permute-done.11), channel_id=1, source_target_pairs={{4,8},{6,10},{8,12},{10,14},{5,9},{7,11},{9,13},{11,15},{20,24},{2... | collective-permute-start | bytes 884744 | tf_op jit(solution)/shard_map/ppermute | solution.py:14
  33.9 13.3 %collective-permute-start.14 = (f16[1152,128]{1,0:T(8,128)(2,1)}, f16[1152,128]{1,0:T(8,128)(2,1)S(1)}, u32[]{:S(2)}, u32[]{:S(2)}) collective-permute-start(f16[1152,128]{1,0:T(8,128)(2,1)} %collective-permute-done.13), channel_id=1, source_target_pairs={{4,0},{6,2},{8,4},{10,6},{5,1},{7,3},{9,5},{11,7},{20,16},{22,18},... | collective-permute-start | bytes 884744 | tf_op jit(solution)/shard_map/ppermute | solution.py:14
  47.3 17.1 %collective-permute-start.15 = (f16[1152,128]{1,0:T(8,128)(2,1)S(1)}, f16[1152,128]{1,0:T(8,128)(2,1)S(1)}, u32[]{:S(2)}, u32[]{:S(2)}) collective-permute-start(f16[1152,128]{1,0:T(8,128)(2,1)S(1)} %broadcast_select_fusion.4), channel_id=1, source_target_pairs={{8,12},{10,14},{4,0},{6,2},{9,13},{11,15},{5,1},{7,3},{24,28},{26,... | collective-permute-start | bytes 884744 | tf_op jit(solution)/shard_map/ppermute | solution.py:27
  48.7 2.2 %collective-permute-start.7 = (f16[1152,128]{1,0:T(8,128)(2,1)S(1)}, f16[1152,128]{1,0:T(8,128)(2,1)S(1)}, u32[]{:S(2)}, u32[]{:S(2)}) collective-permute-start(f16[1152,128]{1,0:T(8,128)(2,1)S(1)} %collective-permute-done.6), channel_id=1, source_target_pairs={{4,8},{6,10},{8,12},{10,14},{5,9},{7,11},{9,13},{11,15},{20,24},{2... | collective-permute-start | bytes 884744 | tf_op jit(solution)/shard_map/ppermute | solution.py:14
  49.5 13.3 %collective-permute-start.9 = (f16[1152,128]{1,0:T(8,128)(2,1)S(1)}, f16[1152,128]{1,0:T(8,128)(2,1)S(1)}, u32[]{:S(2)}, u32[]{:S(2)}) collective-permute-start(f16[1152,128]{1,0:T(8,128)(2,1)S(1)} %collective-permute-done.8), channel_id=1, source_target_pairs={{4,0},{6,2},{8,4},{10,6},{5,1},{7,3},{9,5},{11,7},{20,16},{22,18},... | collective-permute-start | bytes 884744 | tf_op jit(solution)/shard_map/ppermute | solution.py:14
  62.9 8.6 %collective-permute-start.10 = (f16[1152,128]{1,0:T(8,128)(2,1)S(1)}, f16[1152,128]{1,0:T(8,128)(2,1)S(1)}, u32[]{:S(2)}, u32[]{:S(2)}) collective-permute-start(f16[1152,128]{1,0:T(8,128)(2,1)S(1)} %broadcast_select_fusion.5), channel_id=1, source_target_pairs={{8,12},{10,14},{4,0},{6,2},{9,13},{11,15},{5,1},{7,3},{24,28},{26,... | collective-permute-start | bytes 884744 | tf_op jit(solution)/shard_map/ppermute | solution.py:27
  65.3 27.7 %copy-start.2 = (bf16[1024,128]{1,0:T(8,128)(2,1)S(1)}, bf16[1024,128]{1,0:T(8,128)(2,1)}, u32[]{:S(2)}) copy-start(bf16[1024,128]{1,0:T(8,128)(2,1)} %get-tuple-element.5) | copy-start | bytes 786436
  65.3 27.7 %copy-start.3 = (bf16[1024,128]{1,0:T(8,128)(2,1)S(1)}, bf16[1024,128]{1,0:T(8,128)(2,1)}, u32[]{:S(2)}) copy-start(bf16[1024,128]{1,0:T(8,128)(2,1)} %fusion.23) | copy-start | bytes 786436
  66.9 26.2 %collective-permute-start.4 = (bf16[512,1024]{1,0:T(8,128)(2,1)S(1)}, bf16[512,1024]{1,0:T(8,128)(2,1)S(1)}, u32[]{:S(2)}, u32[]{:S(2)}) collective-permute-start(bf16[512,1024]{1,0:T(8,128)(2,1)S(1)} %get-tuple-element.10), channel_id=1, source_target_pairs={{0,16},{16,0},{1,17},{17,1},{2,18},{18,2},{3,19},{19,3},{4,20},{20... | collective-permute-start | bytes 3145736 | tf_op jit(solution)/shard_map/ppermute | solution.py:62
  71.5 34.2 %collective-permute-start.19 = (f16[1280,128]{1,0:T(8,128)(2,1)S(1)}, f16[1280,128]{1,0:T(8,128)(2,1)S(1)}, u32[]{:S(2)}, u32[]{:S(2)}) collective-permute-start(f16[1280,128]{1,0:T(8,128)(2,1)S(1)} %constant_dynamic-update-slice_fusion.10), channel_id=1, source_target_pairs={{0,16},{16,0},{1,17},{17,1},{2,18},{18,2},{3,19},{19,3},{4,20},{20... | collective-permute-start | bytes 983048 | tf_op jit(solution)/shard_map/ppermute | solution.py:62
  100.7 2.5 %copy-start.4 = (f32[256,1024]{1,0:T(8,128)S(1)}, f32[256,1024]{1,0:T(8,128)}, u32[]{:S(2)}) copy-start(f32[256,1024]{1,0:T(8,128)} %fusion.90) | copy-start | bytes 3145732
  101.6 4.0 %collective-permute-start.16 = (f32[16,512]{1,0:T(8,128)S(1)}, f32[16,512]{1,0:T(8,128)S(1)}, u32[]{:S(2)}, u32[]{:S(2)}) collective-permute-start(f32[16,512]{1,0:T(8,128)S(1)} %slice.206), channel_id=1, source_target_pairs={{0,16},{16,0},{1,17},{17,1},{2,18},{18,2},{3,19},{19,3},{4,20},{20... | collective-permute-start | bytes 98312 | tf_op jit(solution)/shard_map/ppermute | solution.py:62
  103.3 11.7 %collective-permute-start = (f32[256,512]{1,0:T(8,128)S(1)}, f32[256,512]{1,0:T(8,128)S(1)}, u32[]{:S(2)}, u32[]{:S(2)}) collective-permute-start(f32[256,512]{1,0:T(8,128)S(1)} %constant_dynamic-slice_fusion.2), channel_id=1, source_target_pairs={{0,1},{1,0},{2,3},{3,2},{4,5},{5,4},{6,7},{7,6},{8,9},{9,8},{10,11... | collective-permute-start | bytes 1572872 | tf_op jit(solution)/shard_map/ppermute | solution.py:101
  105.6 1.2 %collective-permute-start.17 = (f32[16,256]{1,0:T(8,128)S(1)}, f32[16,256]{1,0:T(8,128)S(1)}, u32[]{:S(2)}, u32[]{:S(2)}) collective-permute-start(f32[16,256]{1,0:T(8,128)S(1)} %slice.208), channel_id=1, source_target_pairs={{0,2},{2,0},{4,6},{6,4},{8,10},{10,8},{12,14},{14,12},{1,3},{3,1},... | collective-permute-start | bytes 49160 | tf_op jit(solution)/shard_map/ppermute | solution.py:59
  106.9 6.0 %collective-permute-start.18 = (f32[16,256]{1,0:T(8,128)S(1)}, f32[16,256]{1,0:T(8,128)S(1)}, u32[]{:S(2)}, u32[]{:S(2)}) collective-permute-start(f32[16,256]{1,0:T(8,128)S(1)} %slice_add_fusion.11), channel_id=1, source_target_pairs={{0,1},{1,0},{2,3},{3,2},{4,5},{5,4},{6,7},{7,6},{8,9},{9,8},{10,11... | collective-permute-start | bytes 49160 | tf_op jit(solution)/shard_map/ppermute | solution.py:126
  108.6 4.8 %collective-permute-start.20 = (f16[1280,256]{1,0:T(8,128)(2,1)S(1)}, f16[1280,256]{1,0:T(8,128)(2,1)S(1)}, u32[]{:S(2)}, u32[]{:S(2)}) collective-permute-start(f16[1280,256]{1,0:T(8,128)(2,1)S(1)} %pad_maximum_fusion.2), channel_id=1, source_target_pairs={{0,2},{2,0},{4,6},{6,4},{8,10},{10,8},{12,14},{14,12},{1,3},{3,1},... | collective-permute-start | bytes 1966088 | tf_op jit(solution)/shard_map/ppermute | solution.py:59

commit v2 on v0

v2 whole, which is shorter than its diff:
```python
import jax
import jax.numpy as jnp
import numpy as np
from jax import lax
from jax.experimental import pallas as pl
from jax.experimental.pallas import tpu as pltpu
from jax.sharding import PartitionSpec as P

SCALING = 0.5
SHRINK_GAIN = 2.0**19
EXPAND_GAIN = 2.0**14
LANES = 128
VMEM_BYTES = 48 * 2**20


def sources(spots):
    table = []
    for half in range(spots):
        found = [half]
        if spots == 4:
            second = half - 2 if half >= 2 else half + 2
            third = half - 3 if half >= 3 else half + 3
            found += [1 if half == 0 else half - 1, second, half + 1 if half in (1, 2) else third]
        else:
            for step in range(1, spots):
                up, down = half - step, half + step
                if 2 * step > spots - 1:
                    found.append(up if half >= step else down)
                else:
                    found += [up, down]
        table.append([f if 0 <= f < spots else -(2**16) for f in found])
    return np.array(table, np.int32)


def line_steps(spots, half):
    def send(value, moves):
        return lax.ppermute(value, "adapter", [(2 * s + c, 2 * d + c) for s, d in moves for c in range(2)])

    def first(piece):
        up = send(piece, [(s, s + 1) for s in range(spots - 1)])
        down = send(piece, [(s, s - 1) for s in range(1, spots)])
        return up, down

    def rest(up, down):
        found = []
        merged = None
        if spots > 2:
            found += [up, down]
        else:
            found = [jnp.where(half >= 1, up, down)]
        for step in range(2, spots):
            goes_up = [(s, s + 1) for s in range(step - 1, spots - 1)]
            goes_down = [(s, s - 1) for s in range(1, spots - step + 1)]
            if 2 * step - 1 > spots:
                merged = send(merged, goes_up + goes_down)
            else:
                up, down = send(up, goes_up), send(down, goes_down)
                if 2 * step > spots - 1:
                    merged = jnp.where(half >= step, up, down)
                else:
                    found += [up, down]
                    continue
            found.append(merged)
        if spots == 4:
            up, down, second, third = found
            middle = (half == 1) | (half == 2)
            found = [jnp.where(half == 0, down, up), second, jnp.where(middle, down, third)]
        return found

    return first, rest


def two_terms(value):
    wide = value.astype(jnp.float32)
    high = lax.reduce_precision(wide, exponent_bits=8, mantissa_bits=7)
    return high.astype(jnp.bfloat16), (wide - high).astype(jnp.bfloat16)


def side_by_side(value):
    return jnp.concatenate(two_terms(value), axis=1)


def product_kernel(place_ref, tokens_ref, matrix_ref, out_ref):
    @pl.when(pl.program_id(0) == 0)
    def _():
        out_ref[...] = jnp.zeros_like(out_ref)

    out_ref[...] += jnp.dot(tokens_ref[...], matrix_ref[...], preferred_element_type=jnp.float32)


def base_product(tokens, matrix, place, span):
    rows, width = tokens.shape
    depth = min(width, 1024)
    return pl.pallas_call(
        product_kernel,
        grid_spec=pltpu.PrefetchScalarGridSpec(
            num_scalar_prefetch=1,
            grid=(width // depth,),
            in_specs=[
                pl.BlockSpec((rows, depth), lambda k, place: (0, k)),
                pl.BlockSpec((depth, span), lambda k, place: (k, place[0])),
            ],
            out_specs=pl.BlockSpec((rows, span), lambda k, place: (0, 0)),
        ),
        out_shape=jax.ShapeDtypeStruct((rows, span), jnp.float32),
        compiler_params=pltpu.CompilerParams(vmem_limit_bytes=VMEM_BYTES),
        cost_estimate=pl.CostEstimate(flops=0, bytes_accessed=0, transcendentals=0),
        name="base_product",
    )(jnp.reshape(place, (1,)), tokens, matrix)


PAD = 16


def pack_kernel(rows, place_ref, tokens_ref, slot_ref, *refs):
    out_ref = refs[-1]
    width = tokens_ref.shape[1]
    out_ref[:rows] = tokens_ref[...]
    tail = jnp.broadcast_to(slot_ref[...].astype(jnp.float32), (PAD, rows)).astype(out_ref.dtype)
    out_ref[rows : rows + PAD, :rows] = tail
    if width > rows:
        out_ref[rows : rows + PAD, rows:] = jnp.zeros((PAD, width - rows), out_ref.dtype)
    if len(refs) == 2:
        out_ref[rows + PAD :] = refs[0][...]


def pack_two(tokens, slot, place, quarter):
    rows = tokens.shape[0]
    return pl.pallas_call(
        lambda *refs: pack_kernel(rows, *refs),
        grid_spec=pltpu.PrefetchScalarGridSpec(
            num_scalar_prefetch=1,
            grid=(2,),
            in_specs=[
                pl.BlockSpec((rows, quarter), lambda i, place: (0, place[0] + i)),
                pl.BlockSpec((1, rows), lambda i, place: (0, 0)),
            ],
            out_specs=pl.BlockSpec((rows + PAD, quarter), lambda i, place: (0, i)),
        ),
        out_shape=jax.ShapeDtypeStruct((rows + PAD, 2 * quarter), tokens.dtype),
        cost_estimate=pl.CostEstimate(flops=0, bytes_accessed=0, transcendentals=0),
        name="pack_two",
    )(jnp.reshape(place, (1,)), tokens, slot)


def pack_core(tokens, slot, theirs, place, side, quarter):
    rows = tokens.shape[0]
    return pl.pallas_call(
        lambda *refs: pack_kernel(rows, *refs),
        grid_spec=pltpu.PrefetchScalarGridSpec(
            num_scalar_prefetch=1,
            grid=(1,),
            in_specs=[
                pl.BlockSpec((rows, quarter), lambda i, place: (0, place[0])),
                pl.BlockSpec((1, rows), lambda i, place: (0, 0)),
                pl.BlockSpec((rows + PAD, quarter), lambda i, place: (0, place[1])),
            ],
            out_specs=pl.BlockSpec((2 * (rows + PAD), quarter), lambda i, place: (0, 0)),
        ),
        out_shape=jax.ShapeDtypeStruct((2 * (rows + PAD), quarter), tokens.dtype),
        cost_estimate=pl.CostEstimate(flops=0, bytes_accessed=0, transcendentals=0),
        name="pack_core",
    )(jnp.stack([place, side]), tokens, slot, theirs)


def assemble_kernel(rows, place_ref, tokens_ref, slot_ref, theirs_ref, came_ref, every_ref, slots_ref):
    every_ref[:rows] = tokens_ref[...]
    every_ref[rows : 2 * rows] = theirs_ref[:rows]
    every_ref[2 * rows : 3 * rows] = came_ref[:rows]
    every_ref[3 * rows :] = came_ref[rows + PAD : 2 * rows + PAD]
    packed = [
        theirs_ref[rows : rows + PAD, :rows],
        came_ref[rows : rows + PAD, :rows],
        came_ref[2 * rows + PAD :, :rows],
    ]
    slots_ref[:, :rows] = slot_ref[...]
    for i, part in enumerate(packed):
        slots_ref[:, (i + 1) * rows : (i + 2) * rows] = part.astype(jnp.float32)[:1].astype(jnp.int32)


def assemble(tokens, slot, theirs, came, place, side, quarter):
    rows = tokens.shape[0]
    return pl.pallas_call(
        lambda *refs: assemble_kernel(rows, *refs),
        grid_spec=pltpu.PrefetchScalarGridSpec(
            num_scalar_prefetch=1,
            grid=(1,),
            in_specs=[
                pl.BlockSpec((rows, quarter), lambda i, place: (0, place[0])),
                pl.BlockSpec((1, rows), lambda i, place: (0, 0)),
                pl.BlockSpec((rows + PAD, quarter), lambda i, place: (0, place[1])),
                pl.BlockSpec((2 * (rows + PAD), quarter), lambda i, place: (0, 0)),
            ],
            out_specs=[
                pl.BlockSpec((4 * rows, quarter), lambda i, place: (0, 0)),
                pl.BlockSpec((1, 4 * rows), lambda i, place: (0, 0)),
            ],
        ),
        out_shape=[
            jax.ShapeDtypeStruct((4 * rows, quarter), tokens.dtype),
            jax.ShapeDtypeStruct((1, 4 * rows), jnp.int32),
        ],
        cost_estimate=pl.CostEstimate(flops=0, bytes_accessed=0, transcendentals=0),
        name="assemble",
    )(jnp.stack([place, side]), tokens, slot, theirs, came)


def shrink_kernel(rank, resident, which, first_ref, tokens_ref, slot_ref, *refs):
    weights, sums, out_ref = refs[: len(which)], refs[len(which) : -1], refs[-1]
    held = rank * resident
    count = tokens_ref.shape[0]
    tile = 256
    products = [
        jnp.dot(tokens_ref[...], w[...], preferred_element_type=jnp.float32) for w in weights
    ]
    for at in range(0, count, tile):
        slot = slot_ref[:, at : at + tile]
        total = sums[0][:, at : at + tile] if sums else jnp.zeros((rank, tile), jnp.float32)
        for product, side in zip(products, which):
            part = product[at : at + tile]
            part = jnp.transpose(part[:, :held] + part[:, held:])
            for j in range(resident):
                chosen = slot == first_ref[side] + j
                total += jnp.where(chosen, part[j * rank : (j + 1) * rank], 0.0)
        out_ref[:, at : at + tile] = total


def shrink_step(tokens, slot, weights, firsts, which, total, rank, resident):
    count, depth = tokens.shape
    sums = [] if total is None else [total]
    vmem = pl.BlockSpec(memory_space=pltpu.VMEM)
    return pl.pallas_call(
        lambda *refs: shrink_kernel(rank, resident, which, *refs),
        in_specs=[pl.BlockSpec(memory_space=pltpu.SMEM)] + [vmem] * (2 + len(weights) + len(sums)),
        out_specs=vmem,
        out_shape=jax.ShapeDtypeStruct((rank, count), jnp.float32),
        compiler_params=pltpu.CompilerParams(vmem_limit_bytes=24 * 2**20),
        cost_estimate=pl.CostEstimate(flops=0, bytes_accessed=0, transcendentals=0),
        name="shrink_step",
    )(firsts, tokens, slot, *weights, *sums)


def expand_kernel(rank, groups, scale, slots_ref, slot_ref, own_ref, came_ref, *refs):
    parts = refs[: 2 * len(groups)]
    bases, out_ref = refs[2 * len(groups) : -1], refs[-1]
    shrunk = own_ref[...] + came_ref[...]
    slot = slot_ref[...]
    update = 0.0
    at = 0
    for i, count in enumerate(groups):
        spread = jnp.concatenate(
            [jnp.where(slot == slots_ref[at + j], shrunk, 0.0) for j in range(count)], axis=0
        )
        at += count
        high = spread.astype(jnp.bfloat16)
        low = (spread - high.astype(jnp.float32)).astype(jnp.bfloat16)
        for left, right in ((high, parts[2 * i]), (low, parts[2 * i]), (high, parts[2 * i + 1])):
            update += lax.dot_general(
                left, right[...], (((0,), (0,)), ((), ())), preferred_element_type=jnp.float32
            )
    total = scale * update
    for base in bases:
        total += base[...]
    out_ref[...] = total.astype(jnp.bfloat16)


def expand_step(slots, slot, own, came, parts, bases, rank, scale):
    groups = [high.shape[0] // rank for high, _ in parts]
    flat = [term for pair in parts for term in pair]
    operands = [slot, own, came, *flat, *bases]
    rows, span = bases[0].shape
    depth = rank * sum(groups)
    return pl.pallas_call(
        lambda *refs: expand_kernel(rank, groups, scale, *refs),
        in_specs=[pl.BlockSpec(memory_space=pltpu.SMEM)]
        + [pl.BlockSpec(memory_space=pltpu.VMEM)] * len(operands),
        out_specs=pl.BlockSpec(memory_space=pltpu.VMEM),
        out_shape=jax.ShapeDtypeStruct((rows, span), jnp.bfloat16),
        compiler_params=pltpu.CompilerParams(vmem_limit_bytes=VMEM_BYTES),
        cost_estimate=pl.CostEstimate(flops=0, bytes_accessed=0, transcendentals=0),
        name="expand_step",
    )(slots, *operands)


def per_device(tokens, token_adapter_index, table, value_matrix, shrink_weight, expand_weight):
    rows, width = tokens.shape
    resident, rank, span = expand_weight.shape
    held = resident * rank
    owners = lax.axis_size("adapter")
    spots = owners // 2
    quarter = width // 4
    g, a = lax.axis_index("group"), lax.axis_index("adapter")
    c, half = a % 2, a // 2
    core_pairs = [(i, i ^ 1) for i in range(owners)]
    swap = [(0, 1), (1, 0)]
    first_step, other_steps = line_steps(spots, half)
    barrier = lax.optimization_barrier

    def over_core(value):
        return lax.ppermute(value, "adapter", core_pairs)

    def over_group(value):
        return lax.ppermute(value, "group", swap)

    def shrink_rows(side):
        return lax.dynamic_slice_in_dim(shrink_weight, (2 * g + side) * quarter, quarter, 0)

    give = (shrink_rows(1 - c) * SHRINK_GAIN).astype(jnp.float16)
    given = over_core(give)
    flat_expand = expand_weight.reshape(held, span)
    half_expand = lax.dynamic_slice_in_dim(flat_expand, g * (held // 2), held // 2, 0)
    half_expand = (half_expand * EXPAND_GAIN).astype(jnp.float16)
    blocks = [half_expand[:, i * LANES : (i + 1) * LANES] for i in range(span // LANES)]
    mine = jnp.concatenate([(shrink_rows(c) * SHRINK_GAIN).astype(jnp.float16), *blocks], axis=0)
    mine, _ = barrier((mine, give))
    mine_first = first_step(mine)

    matches = token_adapter_index[None, :] == lax.broadcasted_iota(
        jnp.int32, (table.shape[0], rows), 0
    )
    slot = jnp.sum(jnp.where(matches, table[:, None], 0), axis=0, keepdims=True)

    late_tokens, _ = barrier((tokens, mine))
    sent = pack_two(late_tokens, slot, 2 * (1 - g), quarter)
    theirs = over_group(sent)
    given_first = first_step(given)

    mine_up, mine_down, base_tokens, _ = barrier((*mine_first, tokens, sent))
    mine_first = (mine_up, mine_down)
    axes = ("tensor", "sub")
    if lax.axis_size("tensor") == 2 and lax.axis_size("sub") == 1:
        x = lax.axis_index("tensor")
        away = base_product(base_tokens, value_matrix, 1 - x, span)
        base_came = lax.ppermute(away, "tensor", swap)
        base_tokens, _ = barrier((tokens, away))
        bases = [base_product(base_tokens, value_matrix, x, span), base_came]
    else:
        partial = jnp.dot(base_tokens, value_matrix, preferred_element_type=jnp.float32)
        bases = [lax.psum_scatter(partial, axes, scatter_dimension=1, tiled=True)]

    own_mine, own_given, _ = barrier((mine, given, bases[0]))
    mine_pieces = [own_mine] + other_steps(*mine_first)
    given_pieces = [own_given] + other_steps(*given_first)
    source = jnp.asarray(sources(spots))[half]
    firsts = resident * (2 * source[:, None] + jnp.stack([c, 1 - c])[None, :]).reshape(-1)

    other_part = pack_core(tokens, slot, theirs, 2 * g + 1 - c, 1 - c, quarter)
    came = over_core(other_part)
    every, every_slot = assemble(tokens, slot, theirs, came, 2 * g + c, c, quarter)

    total = None
    for i, (mine_piece, given_piece) in enumerate(zip(mine_pieces, given_pieces)):
        weights = [side_by_side(mine_piece[:quarter]), side_by_side(given_piece)]
        if i < len(mine_pieces) - 1:
            total = shrink_step(
                every, every_slot, weights, firsts, (2 * i, 2 * i + 1), total, rank, resident
            )
        else:
            for side in range(2):
                total = shrink_step(
                    every, every_slot, weights[side : side + 1], firsts, (2 * i + side,), total, rank, resident
                )
    both_sum = total[:, : 2 * rows] + over_core(total[:, 2 * rows :])
    own_sum = both_sum[:, :rows] + over_group(both_sum[:, rows:])
    if len(bases) == 2:
        came_sum = lax.ppermute(own_sum, "tensor", swap)
    else:
        came_sum = lax.psum(own_sum, axes) - own_sum

    def expand_of(piece):
        cut = piece[quarter:].reshape(span // LANES, held // 2, LANES)
        return jnp.concatenate([cut[i] for i in range(span // LANES)], axis=1)

    here = jnp.concatenate([expand_of(piece) for piece in mine_pieces], axis=0)
    across = over_group(here)
    beside = over_core(jnp.concatenate([here, across], axis=0))
    parts = [two_terms(here), two_terms(across), two_terms(beside)]
    steps = jnp.arange(resident // 2, dtype=jnp.int32)
    sides = jnp.stack([c, 1 - c])[:, None, None, None]
    halves = jnp.stack([g, 1 - g])[None, :, None, None] * (resident // 2)
    slots = (2 * source[:, None] + sides) * resident + halves + steps
    slots = slots.astype(jnp.int32).reshape(-1)
    scale = SCALING / (SHRINK_GAIN * EXPAND_GAIN)
    return expand_step(slots, slot, own_sum, came_sum, parts, bases, rank, scale)


def solution(mesh):
    placed = (
        P(("group", "adapter"), ("tensor", "sub")),
        P(("group", "adapter")),
        P("group"),
        P(("tensor", "sub"), None),
        P(("tensor", "sub"), "adapter"),
        P("adapter", None, ("tensor", "sub")),
    )
    return jax.shard_map(
        per_device,
        mesh=mesh,
        in_specs=placed,
        out_specs=P(("group", "adapter"), ("tensor", "sub")),
        check_vma=False,
    )
```

time: 385 us -> 106 us (0.28)
  waiting for transfers between devices: 285 us -> 23 us
  Pallas kernels: 0 us -> 28.8 us
  matrix products: 23.5 us -> 0 us
  local copies, waits for them, and re-layouts: 26.7 us -> 3.63 us
  between operations: 13.5 us -> 0.45 us
  other arithmetic: 10.6 us -> 23.2 us
  starting transfers between devices: 16.2 us -> 25.7 us
  blocking collectives: 9.37 us -> 0 us
    all_to_all x3 -> x0, waiting for transfers between devices: 265 us -> none  [the longest x1 172 us: per_device(): lax.all_to_all(packed, 'adapter', split_axis=0, concat_axis=0, tiled=True)]
    pallas_call x0 -> x11, Pallas kernels: none -> 28.8 us  [the longest x2 8.87 us: base_product(): pl.pallas_call(product_kernel, grid_spec=pltpu.PrefetchScalarGridSpec(num...]
    ppermute x0 -> x19, starting transfers between devices: none -> 25.7 us  [the longest x10 18.8 us: send(): lax.ppermute(value, 'adapter', [(2 * s + c, 2 * d + c) for s, d in moves...]
    dot_general x3 -> x0, matrix products: 23.5 us -> none  [the longest x1 11.4 us: shrink_masked(): jnp.dot(flattened, shrink_weight, precision=lax.Precision.HIGHEST, prefer...]
    ppermute x0 -> x19, waiting for transfers between devices: none -> 23 us  [the longest x10 18.7 us: send(): lax.ppermute(value, 'adapter', [(2 * s + c, 2 * d + c) for s, d in moves...]
    gather x4 -> x0, local copies, waits for them, and re-layouts: 19.7 us -> none  [the longest x1 7.82 us: per_device(): tokens[source]]
    reduce_scatter x1 -> x0, waiting for transfers between devices: 19.4 us -> none  [per_device(): lax.psum_scatter(matrix_product + jnp.transpose(adapter_update), ('tensor...]
    all_to_all x3 -> x0, starting transfers between devices: 16 us -> none  [the longest x1 6.33 us: per_device(): lax.all_to_all(labels, 'adapter', split_axis=0, concat_axis=0, tiled=True)]
  transfers between devices with their start and end apart: 4 -> 19, of which waited for: 3 -> 4; matrix products, arithmetic and copies ran while one was open for 5% -> 22% of each run, Pallas kernels for 0% -> 25%
where the time goes in v2:
time: 106 us; the launch traced here: 105 us
  Pallas kernels  28.8 us (27%)
  starting transfers between devices  25.7 us (24%)
  other arithmetic  23.2 us (22%)
  waiting for transfers between devices  23 us (22%)
  local copies, waits for them, and re-layouts  3.63 us (3%)
    ppermute x10, starting transfers between devices, send(): lax.ppermute(value, 'adapter', [(2 * s + c, 2 * d + c) for s, d in moves...  18.8 us
    ppermute x10, waiting for transfers between devices, send(): lax.ppermute(value, 'adapter', [(2 * s + c, 2 * d + c) for s, d in moves...  18.7 us
    pallas_call x2, Pallas kernels, base_product(): pl.pallas_call(product_kernel, grid_spec=pltpu.PrefetchScalarGridSpec(num...  8.87 us
    pallas_call x5, Pallas kernels, shrink_step(): pl.pallas_call(lambda *refs: shrink_kernel(rank, resident, which, *refs),...  8.33 us
    convert_element_type x10, other arithmetic, two_terms(): return (high.astype(jnp.bfloat16), (wide - high).astype(jnp.bfloat16))  8.17 us
    concatenate x7, other arithmetic, side_by_side(): return jnp.concatenate(two_terms(value), axis=1)  4.31 us
    unnamed x5, other arithmetic  3.83 us
    pallas_call x1, Pallas kernels, assemble(): pl.pallas_call(lambda *refs: assemble_kernel(rows, *refs), grid_spec=pltp...  3.74 us
  transfers between devices with their start and end apart: 19, of which 4 were waited for; matrix products, arithmetic and copies ran while one was open for 22% of the time, Pallas kernels for 25%

profile of v2, /device:TPU:0, one launch (start us, length us, event | category | flops | bytes accessed | tf_op | source)
XLA Modules:
  0.0 104.8 jit_solution(17211959865546627128)
XLA Ops:
  1.6 1.2 %fusion.11 = f16[1280,128]{1,0:T(8,128)(2,1)S(1)} fusion(f32[4096,128]{1,0:T(8,128)} %param.11, s32[]{:T(128)S(6)} %select_n.71), kind=kLoop, calls=%fused_computation.46 | loop fusion | flops 262143 | bytes 786436
  3.9 4.5 %collective-permute-start.8 = (f16[1280,128]{1,0:T(8,128)(2,1)S(1)}, f16[1280,128]{1,0:T(8,128)(2,1)S(1)}, u32[]{:S(2)}, u32[]{:S(2)}) collective-permute-start(f16[1280,128]{1,0:T(8,128)(2,1)S(1)} %constant_dynamic-update-slice_fusion), channel_id=1, source_target_pairs={{0,4},{2,6},{4,8},{6,10},{8,12},{10,14},{1,5},{3,7},{5,9},{7,11},{... | collective-permute-start | bytes 983048 | tf_op jit(solution)/shard_map/ppermute | solution.py:37
  8.4 1.3 %collective-permute-start.9 = (f16[1280,128]{1,0:T(8,128)(2,1)S(1)}, f16[1280,128]{1,0:T(8,128)(2,1)}, u32[]{:S(2)}, u32[]{:S(2)}) collective-permute-start(f16[1280,128]{1,0:T(8,128)(2,1)S(1)} %constant_dynamic-update-slice_fusion), channel_id=1, source_target_pairs={{4,0},{6,2},{8,4},{10,6},{12,8},{14,10},{5,1},{7,3},{9,5},{11,7},{... | collective-permute-start | bytes 983048 | tf_op jit(solution)/shard_map/ppermute | solution.py:37
  9.7 1.3 %select_reduce_fusion = s32[256]{0:T(256)} fusion(s32[64]{0:T(128)} %param.9, s32[256]{0:T(256)} %param.8), kind=kLoop, calls=%fused_computation.56 | loop fusion | flops 48896 | bytes 2304 | tf_op jit(solution)/shard_map/reduce_sum | solution.py:321
  11.0 2.1 %pack_two.1 = bf16[272,2048]{1,0:T(8,128)(2,1)} custom-call(s32[1]{0:T(128)} %bitcast.7.refs_0_, bf16[256,4096]{1,0:T(8,128)(2,1)} %tokens_ref.1, s32[1,256]{1,0:T(1,128)} %bitcast.13), custom_call_target="tpu_custom_call" | custom-call | tf_op jit(solution)/shard_map/pack_two/pallas_call | solution.py:129
  13.1 1.5 %collective-permute-start = (bf16[272,2048]{1,0:T(8,128)(2,1)}, bf16[272,2048]{1,0:T(8,128)(2,1)}, u32[]{:S(2)}, u32[]{:S(2)}) collective-permute-start(bf16[272,2048]{1,0:T(8,128)(2,1)} %pack_two.1), channel_id=1, source_target_pairs={{0,16},{16,0},{1,17},{17,1},{2,18},{18,2},{3,19},{19,3},{4,20},{20... | collective-permute-start | bytes 3342344 | tf_op jit(solution)/shard_map/ppermute | solution.py:303
  17.1 1.3 %collective-permute-start.3 = (f16[1024,128]{1,0:T(8,128)(2,1)S(1)}, f16[1024,128]{1,0:T(8,128)(2,1)S(1)}, u32[]{:S(2)}, u32[]{:S(2)}) collective-permute-start(f16[1024,128]{1,0:T(8,128)(2,1)S(1)} %collective-permute-done.2), channel_id=1, source_target_pairs={{4,0},{6,2},{8,4},{10,6},{12,8},{14,10},{5,1},{7,3},{9,5},{11,7},{... | collective-permute-start | bytes 786440 | tf_op jit(solution)/shard_map/ppermute | solution.py:37
  18.4 5.2 %collective-permute-start.4 = (f16[1024,128]{1,0:T(8,128)(2,1)S(1)}, f16[1024,128]{1,0:T(8,128)(2,1)S(1)}, u32[]{:S(2)}, u32[]{:S(2)}) collective-permute-start(f16[1024,128]{1,0:T(8,128)(2,1)S(1)} %collective-permute-done.2), channel_id=1, source_target_pairs={{0,4},{2,6},{4,8},{6,10},{8,12},{10,14},{1,5},{3,7},{5,9},{7,11},{... | collective-permute-start | bytes 786440 | tf_op jit(solution)/shard_map/ppermute | solution.py:37
  24.3 1.3 %collective-permute-start.11 = (f16[1280,128]{1,0:T(8,128)(2,1)}, f16[1280,128]{1,0:T(8,128)(2,1)S(1)}, u32[]{:S(2)}, u32[]{:S(2)}) collective-permute-start(f16[1280,128]{1,0:T(8,128)(2,1)} %collective-permute-done.9), channel_id=1, source_target_pairs={{4,0},{6,2},{8,4},{10,6},{5,1},{7,3},{9,5},{11,7},{20,16},{22,18},... | collective-permute-start | bytes 983048 | tf_op jit(solution)/shard_map/ppermute | solution.py:37
  25.7 4.8 %base_product.2 = f32[256,512]{1,0:T(8,128)} custom-call(s32[1]{0:T(128)} %bitcast.11.place_ref, bf16[256,4096]{1,0:T(8,128)(2,1)S(1)} %copy-done, bf16[4096,1024]{1,0:T(8,128)(2,1)} %matrix_ref.3), custom_call_target="tpu_custom_call" | custom-call | tf_op jit(solution)/shard_map/base_product/pallas_call | solution.py:94
  30.5 4.0 %base_product.3.refs_10_ = f32[256,512]{1,0:T(8,128)S(1)} custom-call(s32[1]{0:T(128)} %bitcast.10.place_ref, bf16[256,4096]{1,0:T(8,128)(2,1)S(1)} %copy-done, bf16[4096,1024]{1,0:T(8,128)(2,1)} %matrix_ref.3), custom_call_target="tpu_custom_call" | custom-call | tf_op jit(solution)/shard_map/base_product/pallas_call | solution.py:94
  35.5 1.6 %collective-permute-start.18 = (f32[256,512]{1,0:T(8,128)}, f32[256,512]{1,0:T(8,128)}, u32[]{:S(2)}, u32[]{:S(2)}) collective-permute-start(f32[256,512]{1,0:T(8,128)} %base_product.2), channel_id=1, source_target_pairs={{0,1},{1,0},{2,3},{3,2},{4,5},{5,4},{6,7},{7,6},{8,9},{9,8},{10,11... | collective-permute-start | bytes 1572872 | tf_op jit(solution)/shard_map/ppermute | solution.py:334
  37.8 1.3 %collective-permute-start.6 = (f16[1024,128]{1,0:T(8,128)(2,1)S(1)}, f16[1024,128]{1,0:T(8,128)(2,1)S(1)}, u32[]{:S(2)}, u32[]{:S(2)}) collective-permute-start(f16[1024,128]{1,0:T(8,128)(2,1)S(1)} %collective-permute-done.3), channel_id=1, source_target_pairs={{4,0},{6,2},{8,4},{10,6},{5,1},{7,3},{9,5},{11,7},{20,16},{22,18},... | collective-permute-start | bytes 786440 | tf_op jit(solution)/shard_map/ppermute | solution.py:37
  39.2 1.3 %collective-permute-start.12 = (f16[1280,128]{1,0:T(8,128)(2,1)S(1)}, f16[1280,128]{1,0:T(8,128)(2,1)S(1)}, u32[]{:S(2)}, u32[]{:S(2)}) collective-permute-start(f16[1280,128]{1,0:T(8,128)(2,1)S(1)} %broadcast_select_fusion.1), channel_id=1, source_target_pairs={{8,12},{10,14},{4,0},{6,2},{9,13},{11,15},{5,1},{7,3},{24,28},{26,... | collective-permute-start | bytes 983048 | tf_op jit(solution)/shard_map/ppermute | solution.py:37
  40.7 14.9 %collective-permute-done.6 = f16[1024,128]{1,0:T(8,128)(2,1)S(1)} collective-permute-done((f16[1024,128]{1,0:T(8,128)(2,1)S(1)}, f16[1024,128]{1,0:T(8,128)(2,1)S(1)}, u32[]{:S(2)}, u32[]{:S(2)}) %collective-permute-start.6) | collective-permute-done | bytes 262176 | tf_op jit(solution)/shard_map/ppermute | solution.py:37
  56.5 1.3 %collective-permute-start.7 = (f16[1024,128]{1,0:T(8,128)(2,1)}, f16[1024,128]{1,0:T(8,128)(2,1)}, u32[]{:S(2)}, u32[]{:S(2)}) collective-permute-start(f16[1024,128]{1,0:T(8,128)(2,1)} %get-tuple-element.28), channel_id=1, source_target_pairs={{8,12},{10,14},{4,0},{6,2},{9,13},{11,15},{5,1},{7,3},{24,28},{26,... | collective-permute-start | bytes 786440 | tf_op jit(solution)/shard_map/ppermute | solution.py:37
  58.9 3.8 %collective-permute-done.12 = f16[1280,128]{1,0:T(8,128)(2,1)S(1)} collective-permute-done((f16[1280,128]{1,0:T(8,128)(2,1)S(1)}, f16[1280,128]{1,0:T(8,128)(2,1)S(1)}, u32[]{:S(2)}, u32[]{:S(2)}) %collective-permute-start.12) | collective-permute-done | bytes 327712 | tf_op jit(solution)/shard_map/ppermute | solution.py:37
  67.0 3.0 %pack_core.1 = bf16[544,1024]{1,0:T(8,128)(2,1)} custom-call(s32[2]{0:T(128)} %get-tuple-element.68.refs_0_, bf16[256,4096]{1,0:T(8,128)(2,1)} %tokens_ref.1, s32[1,256]{1,0:T(1,128)} %bitcast.14, bf16[272,2048]{1,0:T(8,128)(2,1)} %collective-permute-done.refs_3_), custom_call_target="tpu_custom_call" | custom-call | tf_op jit(solution)/shard_map/pack_core/pallas_call | solution.py:148
  71.7 1.9 %pad_maximum_fusion.4.refs_3_ = bf16[1024,256]{1,0:T(8,128)(2,1)} fusion(bf16[1024,128]{1,0:T(8,128)(2,1)} %get-tuple-element.54, bf16[1024,128]{1,0:T(8,128)(2,1)} %get-tuple-element.53), kind=kLoop, calls=%fused_computation.37 | loop fusion | flops 1048576 | bytes 1048576 | tf_op jit(solution)/shard_map/concatenate | solution.py:80
  74.3 1.7 %reduce-precision_convert_fusion.2.refs_4_ = bf16[256,512]{1,0:T(8,128)(2,1)} fusion(f16[256,512]{1,0:T(8,128)(2,1)} %get-tuple-element.26), kind=kLoop, calls=%fused_computation.6 | loop fusion | flops 393216 | bytes 524288 | tf_op jit(solution)/shard_map/convert_element_type | solution.py:76
  76.0 1.2 %reduce-precision_convert_fusion.5 = (bf16[1024,128]{1,0:T(8,128)(2,1)S(1)}, bf16[1024,128]{1,0:T(8,128)(2,1)S(1)}, bf16[1024,128]{1,0:T(8,128)(2,1)S(1)}, bf16[1024,128]{1,0:T(8,128)(2,1)S(1)}) fusion(f16[1024,128]{1,0:T(8,128)(2,1)S(1)} %copy-done.9, f16[1024,128]{1,0:T(8,128)(2,1)S(1)} %copy-done.11, pred[]{:T(512)S(6)} %eq.26, ...), kind=kLoop, calls=%fused_computation.12 | loop fusion | flops 1572864 | bytes 1835010 | tf_op jit(solution)/shard_map/convert_element_type | solution.py:76
  78.3 3.7 %assemble.1 = (bf16[1024,1024]{1,0:T(8,128)(2,1)}, s32[1,1024]{1,0:T(1,128)}) custom-call(s32[2]{0:T(128)} %pad_add_fusion.1.refs_0_, bf16[256,4096]{1,0:T(8,128)(2,1)} %tokens_ref.1, s32[1,256]{1,0:T(1,128)} %bitcast.15, bf16[272,2048]{1,0:T(8,128)(2,1)} %collective-permute-done.refs_3_, bf16[544,1024]{1,0:T(8,128)(2,1)} %collective-permute-done.1.refs_4_), custom_call_target="tpu_custom_call" | custom-call | tf_op jit(solution)/shard_map/assemble/pallas_call | solution.py:183
  82.0 1.6 %copy-done.1 = bf16[1024,1024]{1,0:T(8,128)(2,1)S(1)} copy-done((bf16[1024,1024]{1,0:T(8,128)(2,1)S(1)}, bf16[1024,1024]{1,0:T(8,128)(2,1)}, u32[]{:S(2)}) %copy-start.1) | copy-done | bytes 2097176
  84.3 1.9 %shrink_step.5.refs_5_ = f32[16,1024]{1,0:T(8,128)S(1)} custom-call(s32[8]{0:T(128)S(1)} %mul.72.refs_0_, bf16[1024,1024]{1,0:T(8,128)(2,1)S(1)} %copy-done.1, s32[1,1024]{1,0:T(1,128)S(1)} %copy-done.6, bf16[1024,256]{1,0:T(8,128)(2,1)S(1)} %pad_maximum_fusion.6.refs_3_, bf16[1024,256]{1,0:T(8,128)(2,1)S(1)} %pad_maximum_fusion.7.refs_4_), custom_call_target="tpu_custom_call" | custom-call | tf_op jit(solution)/shard_map/shrink_step/pallas_call | solution.py:232
  86.2 1.9 %shrink_step.6.refs_5_ = f32[16,1024]{1,0:T(8,128)S(1)} custom-call(s32[8]{0:T(128)S(1)} %mul.72.refs_0_, bf16[1024,1024]{1,0:T(8,128)(2,1)S(1)} %copy-done.1, s32[1,1024]{1,0:T(1,128)S(1)} %copy-done.6, bf16[1024,256]{1,0:T(8,128)(2,1)S(1)} %copy-done.2, bf16[1024,256]{1,0:T(8,128)(2,1)S(1)} %copy-done.4, f32[16,1024]{1,0:T(8,128)S(1)} %shrink_step.5.refs_5_), custom_call_target="tpu_custom_call" | custom-call | tf_op jit(solution)/shard_map/shrink_step/pallas_call | solution.py:232
  88.1 1.9 %shrink_step.7.refs_4_ = f32[16,1024]{1,0:T(8,128)S(1)} custom-call(s32[8]{0:T(128)S(1)} %mul.72.refs_0_, bf16[1024,1024]{1,0:T(8,128)(2,1)S(1)} %copy-done.1, s32[1,1024]{1,0:T(1,128)S(1)} %copy-done.6, bf16[1024,256]{1,0:T(8,128)(2,1)S(1)} %pad_maximum_fusion.2.refs_3_, bf16[1024,256]{1,0:T(8,128)(2,1)S(1)} %pad_maximum_fusion.3.refs_4_, ...), custom_call_target="tpu_custom_call" | custom-call | tf_op jit(solution)/shard_map/shrink_step/pallas_call | solution.py:232
  90.0 1.3 %shrink_step.8.refs_4_ = f32[16,1024]{1,0:T(8,128)S(1)} custom-call(s32[8]{0:T(128)S(1)} %mul.72.refs_0_, bf16[1024,1024]{1,0:T(8,128)(2,1)S(1)} %copy-done.1, s32[1,1024]{1,0:T(1,128)S(1)} %copy-done.6, bf16[1024,256]{1,0:T(8,128)(2,1)S(1)} %pad_maximum_fusion.1.refs_3_, f32[16,1024]{1,0:T(8,128)S(1)} %shrink_step.7.refs_4_), custom_call_target="tpu_custom_call" | custom-call | tf_op jit(solution)/shard_map/shrink_step/pallas_call | solution.py:232
  91.4 1.3 %shrink_step.9 = f32[16,1024]{1,0:T(8,128)S(1)} custom-call(s32[8]{0:T(128)S(1)} %mul.72.refs_0_, bf16[1024,1024]{1,0:T(8,128)(2,1)S(1)} %copy-done.1, s32[1,1024]{1,0:T(1,128)S(1)} %copy-done.6, bf16[1024,256]{1,0:T(8,128)(2,1)S(1)} %copy-done.3, f32[16,1024]{1,0:T(8,128)S(1)} %shrink_step.8.refs_4_), custom_call_target="tpu_custom_call" | custom-call | tf_op jit(solution)/shard_map/shrink_step/pallas_call | solution.py:232
  94.4 1.6 %collective-permute-start.14 = (f32[16,256]{1,0:T(8,128)S(1)}, f32[16,256]{1,0:T(8,128)S(1)}, u32[]{:S(2)}, u32[]{:S(2)}) collective-permute-start(f32[16,256]{1,0:T(8,128)S(1)} %slice.158), channel_id=1, source_target_pairs={{0,16},{16,0},{1,17},{17,1},{2,18},{18,2},{3,19},{19,3},{4,20},{20... | collective-permute-start | bytes 49160 | tf_op jit(solution)/shard_map/ppermute | solution.py:303
  97.0 1.2 %collective-permute-done.14 = f32[16,256]{1,0:T(8,128)S(1)} collective-permute-done((f32[16,256]{1,0:T(8,128)S(1)}, f32[16,256]{1,0:T(8,128)S(1)}, u32[]{:S(2)}, u32[]{:S(2)}) %collective-permute-start.14) | collective-permute-done | bytes 16416 | tf_op jit(solution)/shard_map/ppermute | solution.py:303
  98.9 3.0 %collective-permute-done.15.refs_3_ = f32[16,256]{1,0:T(8,128)S(1)} collective-permute-done((f32[16,256]{1,0:T(8,128)S(1)}, f32[16,256]{1,0:T(8,128)S(1)}, u32[]{:S(2)}, u32[]{:S(2)}) %collective-permute-start.15) | collective-permute-done | bytes 16416 | tf_op jit(solution)/shard_map/ppermute | solution.py:366
  102.0 2.8 %expand_step.1 = bf16[256,512]{1,0:T(8,128)(2,1)} custom-call(s32[64]{0:T(128)S(1)} %add.112.refs_0_, s32[1,256]{1,0:T(1,128)S(1)} %bitcast.16, f32[16,256]{1,0:T(8,128)S(1)} %slice_add_fusion.1.refs_2_, f32[16,256]{1,0:T(8,128)S(1)} %collective-permute-done.15.refs_3_, bf16[256,512]{1,0:T(8,128)(2,1)S(1)} %copy-done.5, ...), custom_call_target="tpu_custom_call" | custom-call | tf_op jit(solution)/shard_map/expand_step/pallas_call | solution.py:273
  (92 shorter events, 21.5 us)
Async XLA Ops:
  1.1 16.0 %collective-permute-start.2 = (f16[1024,128]{1,0:T(8,128)(2,1)S(1)}, f16[1024,128]{1,0:T(8,128)(2,1)S(1)}, u32[]{:S(2)}, u32[]{:S(2)}) collective-permute-start(f16[1024,128]{1,0:T(8,128)(2,1)S(1)} %multiply_convert_fusion), channel_id=1, source_target_pairs={{0,2},{2,0},{4,6},{6,4},{8,10},{10,8},{12,14},{14,12},{1,3},{3,1},... | collective-permute-start | bytes 786440 | tf_op jit(solution)/shard_map/ppermute | solution.py:300
  1.6 24.0 %copy-start = (bf16[256,4096]{1,0:T(8,128)(2,1)S(1)}, bf16[256,4096]{1,0:T(8,128)(2,1)}, u32[]{:S(2)}) copy-start(bf16[256,4096]{1,0:T(8,128)(2,1)} %tokens_ref.1) | copy-start | bytes 6291460
  3.9 19.8 %collective-permute-start.8 = (f16[1280,128]{1,0:T(8,128)(2,1)S(1)}, f16[1280,128]{1,0:T(8,128)(2,1)S(1)}, u32[]{:S(2)}, u32[]{:S(2)}) collective-permute-start(f16[1280,128]{1,0:T(8,128)(2,1)S(1)} %constant_dynamic-update-slice_fusion), channel_id=1, source_target_pairs={{0,4},{2,6},{4,8},{6,10},{8,12},{10,14},{1,5},{3,7},{5,9},{7,11},{... | collective-permute-start | bytes 983048 | tf_op jit(solution)/shard_map/ppermute | solution.py:37
  8.4 15.2 %collective-permute-start.9 = (f16[1280,128]{1,0:T(8,128)(2,1)S(1)}, f16[1280,128]{1,0:T(8,128)(2,1)}, u32[]{:S(2)}, u32[]{:S(2)}) collective-permute-start(f16[1280,128]{1,0:T(8,128)(2,1)S(1)} %constant_dynamic-update-slice_fusion), channel_id=1, source_target_pairs={{4,0},{6,2},{8,4},{10,6},{12,8},{14,10},{5,1},{7,3},{9,5},{11,7},{... | collective-permute-start | bytes 983048 | tf_op jit(solution)/shard_map/ppermute | solution.py:37
  13.1 53.9 %collective-permute-start = (bf16[272,2048]{1,0:T(8,128)(2,1)}, bf16[272,2048]{1,0:T(8,128)(2,1)}, u32[]{:S(2)}, u32[]{:S(2)}) collective-permute-start(bf16[272,2048]{1,0:T(8,128)(2,1)} %pack_two.1), channel_id=1, source_target_pairs={{0,16},{16,0},{1,17},{17,1},{2,18},{18,2},{3,19},{19,3},{4,20},{20... | collective-permute-start | bytes 3342344 | tf_op jit(solution)/shard_map/ppermute | solution.py:303
  17.1 18.4 %collective-permute-start.3 = (f16[1024,128]{1,0:T(8,128)(2,1)S(1)}, f16[1024,128]{1,0:T(8,128)(2,1)S(1)}, u32[]{:S(2)}, u32[]{:S(2)}) collective-permute-start(f16[1024,128]{1,0:T(8,128)(2,1)S(1)} %collective-permute-done.2), channel_id=1, source_target_pairs={{4,0},{6,2},{8,4},{10,6},{12,8},{14,10},{5,1},{7,3},{9,5},{11,7},{... | collective-permute-start | bytes 786440 | tf_op jit(solution)/shard_map/ppermute | solution.py:37
  18.4 18.7 %collective-permute-start.4 = (f16[1024,128]{1,0:T(8,128)(2,1)S(1)}, f16[1024,128]{1,0:T(8,128)(2,1)S(1)}, u32[]{:S(2)}, u32[]{:S(2)}) collective-permute-start(f16[1024,128]{1,0:T(8,128)(2,1)S(1)} %collective-permute-done.2), channel_id=1, source_target_pairs={{0,4},{2,6},{4,8},{6,10},{8,12},{10,14},{1,5},{3,7},{5,9},{7,11},{... | collective-permute-start | bytes 786440 | tf_op jit(solution)/shard_map/ppermute | solution.py:37
  23.7 14.1 %collective-permute-start.10 = (f16[1280,128]{1,0:T(8,128)(2,1)S(1)}, f16[1280,128]{1,0:T(8,128)(2,1)S(1)}, u32[]{:S(2)}, u32[]{:S(2)}) collective-permute-start(f16[1280,128]{1,0:T(8,128)(2,1)S(1)} %collective-permute-done.8), channel_id=1, source_target_pairs={{4,8},{6,10},{8,12},{10,14},{5,9},{7,11},{9,13},{11,15},{20,24},{2... | collective-permute-start | bytes 983048 | tf_op jit(solution)/shard_map/ppermute | solution.py:37
  24.3 14.8 %collective-permute-start.11 = (f16[1280,128]{1,0:T(8,128)(2,1)}, f16[1280,128]{1,0:T(8,128)(2,1)S(1)}, u32[]{:S(2)}, u32[]{:S(2)}) collective-permute-start(f16[1280,128]{1,0:T(8,128)(2,1)} %collective-permute-done.9), channel_id=1, source_target_pairs={{4,0},{6,2},{8,4},{10,6},{5,1},{7,3},{9,5},{11,7},{20,16},{22,18},... | collective-permute-start | bytes 983048 | tf_op jit(solution)/shard_map/ppermute | solution.py:37
  35.5 23.2 %copy-start.8 = (f16[1024,128]{1,0:T(8,128)(2,1)}, f16[1024,128]{1,0:T(8,128)(2,1)S(1)}, u32[]{:S(2)}) copy-start(f16[1024,128]{1,0:T(8,128)(2,1)S(1)} %collective-permute-done.3) | copy-start | bytes 786436
  35.5 63.4 %collective-permute-start.18 = (f32[256,512]{1,0:T(8,128)}, f32[256,512]{1,0:T(8,128)}, u32[]{:S(2)}, u32[]{:S(2)}) collective-permute-start(f32[256,512]{1,0:T(8,128)} %base_product.2), channel_id=1, source_target_pairs={{0,1},{1,0},{2,3},{3,2},{4,5},{5,4},{6,7},{7,6},{8,9},{9,8},{10,11... | collective-permute-start | bytes 1572872 | tf_op jit(solution)/shard_map/ppermute | solution.py:334
  37.1 21.7 %copy-start.10 = (f16[1024,128]{1,0:T(8,128)(2,1)}, f16[1024,128]{1,0:T(8,128)(2,1)S(1)}, u32[]{:S(2)}) copy-start(f16[1024,128]{1,0:T(8,128)(2,1)S(1)} %collective-permute-done.4) | copy-start | bytes 786436
  37.1 3.6 %collective-permute-start.5 = (f16[1024,128]{1,0:T(8,128)(2,1)S(1)}, f16[1024,128]{1,0:T(8,128)(2,1)S(1)}, u32[]{:S(2)}, u32[]{:S(2)}) collective-permute-start(f16[1024,128]{1,0:T(8,128)(2,1)S(1)} %collective-permute-done.4), channel_id=1, source_target_pairs={{4,8},{6,10},{8,12},{10,14},{5,9},{7,11},{9,13},{11,15},{20,24},{2... | collective-permute-start | bytes 786440 | tf_op jit(solution)/shard_map/ppermute | solution.py:37
  37.8 17.8 %collective-permute-start.6 = (f16[1024,128]{1,0:T(8,128)(2,1)S(1)}, f16[1024,128]{1,0:T(8,128)(2,1)S(1)}, u32[]{:S(2)}, u32[]{:S(2)}) collective-permute-start(f16[1024,128]{1,0:T(8,128)(2,1)S(1)} %collective-permute-done.3), channel_id=1, source_target_pairs={{4,0},{6,2},{8,4},{10,6},{5,1},{7,3},{9,5},{11,7},{20,16},{22,18},... | collective-permute-start | bytes 786440 | tf_op jit(solution)/shard_map/ppermute | solution.py:37
  39.2 23.4 %collective-permute-start.12 = (f16[1280,128]{1,0:T(8,128)(2,1)S(1)}, f16[1280,128]{1,0:T(8,128)(2,1)S(1)}, u32[]{:S(2)}, u32[]{:S(2)}) collective-permute-start(f16[1280,128]{1,0:T(8,128)(2,1)S(1)} %broadcast_select_fusion.1), channel_id=1, source_target_pairs={{8,12},{10,14},{4,0},{6,2},{9,13},{11,15},{5,1},{7,3},{24,28},{26,... | collective-permute-start | bytes 983048 | tf_op jit(solution)/shard_map/ppermute | solution.py:37
  56.5 19.5 %collective-permute-start.7 = (f16[1024,128]{1,0:T(8,128)(2,1)}, f16[1024,128]{1,0:T(8,128)(2,1)}, u32[]{:S(2)}, u32[]{:S(2)}) collective-permute-start(f16[1024,128]{1,0:T(8,128)(2,1)} %get-tuple-element.28), channel_id=1, source_target_pairs={{8,12},{10,14},{4,0},{6,2},{9,13},{11,15},{5,1},{7,3},{24,28},{26,... | collective-permute-start | bytes 786440 | tf_op jit(solution)/shard_map/ppermute | solution.py:37
  64.8 28.5 %collective-permute-start.16 = (f16[256,512]{1,0:T(8,128)(2,1)}, f16[256,512]{1,0:T(8,128)(2,1)}, u32[]{:S(2)}, u32[]{:S(2)}) collective-permute-start(f16[256,512]{1,0:T(8,128)(2,1)} %get-tuple-element.26), channel_id=1, source_target_pairs={{0,16},{16,0},{1,17},{17,1},{2,18},{18,2},{3,19},{19,3},{4,20},{20... | collective-permute-start | bytes 786440 | tf_op jit(solution)/shard_map/ppermute | solution.py:303
  70.0 6.0 %copy-start.9 = (f16[1024,128]{1,0:T(8,128)(2,1)S(1)}, f16[1024,128]{1,0:T(8,128)(2,1)}, u32[]{:S(2)}) copy-start(f16[1024,128]{1,0:T(8,128)(2,1)} %copy-done.8) | copy-start | bytes 786436
  70.0 6.0 %copy-start.11 = (f16[1024,128]{1,0:T(8,128)(2,1)S(1)}, f16[1024,128]{1,0:T(8,128)(2,1)}, u32[]{:S(2)}) copy-start(f16[1024,128]{1,0:T(8,128)(2,1)} %copy-done.10) | copy-start | bytes 786436
  70.0 8.3 %collective-permute-start.1 = (bf16[544,1024]{1,0:T(8,128)(2,1)}, bf16[544,1024]{1,0:T(8,128)(2,1)}, u32[]{:S(2)}, u32[]{:S(2)}) collective-permute-start(bf16[544,1024]{1,0:T(8,128)(2,1)} %pack_core.1), channel_id=1, source_target_pairs={{0,2},{2,0},{4,6},{6,4},{8,10},{10,8},{12,14},{14,12},{1,3},{3,1},... | collective-permute-start | bytes 3342344 | tf_op jit(solution)/shard_map/ppermute | solution.py:300
  82.0 1.6 %copy-start.1 = (bf16[1024,1024]{1,0:T(8,128)(2,1)S(1)}, bf16[1024,1024]{1,0:T(8,128)(2,1)}, u32[]{:S(2)}) copy-start(bf16[1024,1024]{1,0:T(8,128)(2,1)} %get-tuple-element.17.refs_1_) | copy-start | bytes 6291460
  83.6 0.7 copy-start.6
  84.3 1.9 %copy-start.2 = (bf16[1024,256]{1,0:T(8,128)(2,1)S(1)}, bf16[1024,256]{1,0:T(8,128)(2,1)}, u32[]{:S(2)}) copy-start(bf16[1024,256]{1,0:T(8,128)(2,1)} %pad_maximum_fusion.4.refs_3_) | copy-start | bytes 1572868
  84.3 1.9 %copy-start.4 = (bf16[1024,256]{1,0:T(8,128)(2,1)S(1)}, bf16[1024,256]{1,0:T(8,128)(2,1)}, u32[]{:S(2)}) copy-start(bf16[1024,256]{1,0:T(8,128)(2,1)} %get-tuple-element.72.refs_4_) | copy-start | bytes 1572868
  90.0 1.4 %copy-start.3 = (bf16[1024,256]{1,0:T(8,128)(2,1)S(1)}, bf16[1024,256]{1,0:T(8,128)(2,1)}, u32[]{:S(2)}) copy-start(bf16[1024,256]{1,0:T(8,128)(2,1)} %get-tuple-element.71.refs_3_) | copy-start | bytes 1572868
  91.4 2.0 %copy-start.12 = (f16[512,512]{1,0:T(8,128)(2,1)S(1)}, f16[512,512]{1,0:T(8,128)(2,1)}, u32[]{:S(2)}) copy-start(f16[512,512]{1,0:T(8,128)(2,1)} %maximum_dynamic-update-slice_fusion) | copy-start | bytes 1572868
  92.7 9.3 %copy-start.5 = (bf16[256,512]{1,0:T(8,128)(2,1)S(1)}, bf16[256,512]{1,0:T(8,128)(2,1)}, u32[]{:S(2)}) copy-start(bf16[256,512]{1,0:T(8,128)(2,1)} %reduce-precision_convert_fusion.2.refs_4_) | copy-start | bytes 786436
  92.7 9.3 %copy-start.7 = (s32[256]{0:T(256)S(1)}, s32[256]{0:T(256)}, u32[]{:S(2)}) copy-start(s32[256]{0:T(256)} %select_reduce_fusion) | copy-start | bytes 3076
  92.7 1.7 %collective-permute-start.13 = (f32[16,512]{1,0:T(8,128)S(1)}, f32[16,512]{1,0:T(8,128)S(1)}, u32[]{:S(2)}, u32[]{:S(2)}) collective-permute-start(f32[16,512]{1,0:T(8,128)S(1)} %slice.156), channel_id=1, source_target_pairs={{0,2},{2,0},{4,6},{6,4},{8,10},{10,8},{12,14},{14,12},{1,3},{3,1},... | collective-permute-start | bytes 98312 | tf_op jit(solution)/shard_map/ppermute | solution.py:300
  94.3 4.5 %collective-permute-start.17 = (f16[512,512]{1,0:T(8,128)(2,1)S(1)}, f16[512,512]{1,0:T(8,128)(2,1)S(1)}, u32[]{:S(2)}, u32[]{:S(2)}) collective-permute-start(f16[512,512]{1,0:T(8,128)(2,1)S(1)} %constant_dynamic-update-slice_fusion.4), channel_id=1, source_target_pairs={{0,2},{2,0},{4,6},{6,4},{8,10},{10,8},{12,14},{14,12},{1,3},{3,1},... | collective-permute-start | bytes 1572872 | tf_op jit(solution)/shard_map/ppermute | solution.py:300
  94.4 3.8 %collective-permute-start.14 = (f32[16,256]{1,0:T(8,128)S(1)}, f32[16,256]{1,0:T(8,128)S(1)}, u32[]{:S(2)}, u32[]{:S(2)}) collective-permute-start(f32[16,256]{1,0:T(8,128)S(1)} %slice.158), channel_id=1, source_target_pairs={{0,16},{16,0},{1,17},{17,1},{2,18},{18,2},{3,19},{19,3},{4,20},{20... | collective-permute-start | bytes 49160 | tf_op jit(solution)/shard_map/ppermute | solution.py:303
  98.2 3.7 %collective-permute-start.15 = (f32[16,256]{1,0:T(8,128)S(1)}, f32[16,256]{1,0:T(8,128)S(1)}, u32[]{:S(2)}, u32[]{:S(2)}) collective-permute-start(f32[16,256]{1,0:T(8,128)S(1)} %slice_add_fusion.1.refs_2_), channel_id=1, source_target_pairs={{0,1},{1,0},{2,3},{3,2},{4,5},{5,4},{6,7},{7,6},{8,9},{9,8},{10,11... | collective-permute-start | bytes 49160 | tf_op jit(solution)/shard_map/ppermute | solution.py:366

commit v3 on v0

v3 whole, which is shorter than its diff:
```python
import jax
import jax.numpy as jnp
import numpy as np
from jax import lax
from jax.experimental import pallas as pl
from jax.experimental.pallas import tpu as pltpu
from jax.sharding import PartitionSpec as P

SCALING = 0.5
SHRINK_GAIN = 2.0**19
EXPAND_GAIN = 2.0**14
LANES = 128


def sources(spots):
    table = []
    for half in range(spots):
        found = [half]
        if spots == 4:
            second = half - 2 if half >= 2 else half + 2
            third = half - 3 if half >= 3 else half + 3
            found += [1 if half == 0 else half - 1, second, half + 1 if half in (1, 2) else third]
        else:
            for step in range(1, spots):
                up, down = half - step, half + step
                if 2 * step > spots - 1:
                    found.append(up if half >= step else down)
                else:
                    found += [up, down]
        table.append([f if 0 <= f < spots else -(2**16) for f in found])
    return np.array(table, np.int32)


class Line:
    def __init__(self, piece, spots, half):
        self.spots, self.half = spots, half
        self.up = self.down = piece
        self.found, self.step = [piece], 1

    def send(self, value, moves):
        return lax.ppermute(value, "adapter", [(2 * s + c, 2 * d + c) for s, d in moves for c in range(2)])

    def advance(self):
        spots, step, half = self.spots, self.step, self.half
        goes_up = [(s, s + 1) for s in range(step - 1, spots - 1)]
        goes_down = [(s, s - 1) for s in range(1, spots - step + 1)]
        self.step += 1
        if 2 * step - 1 > spots:
            self.up = self.down = self.send(self.up, goes_up + goes_down)
            self.found.append(self.up)
            return
        self.up, self.down = self.send(self.up, goes_up), self.send(self.down, goes_down)
        if 2 * step > spots - 1:
            self.up = self.down = jnp.where(half >= step, self.up, self.down)
            self.found.append(self.up)
        else:
            self.found += [self.up, self.down]

    def pieces(self):
        if self.spots != 4:
            return self.found
        own, up, down, second, third = self.found
        half = self.half
        middle = (half == 1) | (half == 2)
        return [own, jnp.where(half == 0, down, up), second, jnp.where(middle, down, third)]


def two_terms(value):
    wide = value.astype(jnp.float32)
    high = lax.reduce_precision(wide, exponent_bits=8, mantissa_bits=7)
    return high.astype(jnp.bfloat16), (wide - high).astype(jnp.bfloat16)


def side_by_side(value):
    return jnp.concatenate(two_terms(value), axis=1)


def product_kernel(span, place_ref, tokens_ref, matrix_ref, out_ref):
    columns = pl.ds(pl.multiple_of(place_ref[0] * span, LANES), span)
    out_ref[...] = jnp.dot(
        tokens_ref[...], matrix_ref[:, columns], preferred_element_type=jnp.float32
    )


def base_product(tokens, matrix, place, span):
    vmem = pl.BlockSpec(memory_space=pltpu.VMEM)
    return pl.pallas_call(
        lambda *refs: product_kernel(span, *refs),
        in_specs=[pl.BlockSpec(memory_space=pltpu.SMEM), vmem, vmem],
        out_specs=vmem,
        out_shape=jax.ShapeDtypeStruct((tokens.shape[0], span), jnp.float32),
        compiler_params=pltpu.CompilerParams(vmem_limit_bytes=16 * 2**20),
        cost_estimate=pl.CostEstimate(flops=0, bytes_accessed=0, transcendentals=0),
        name="base_product",
    )(jnp.reshape(place, (1,)), tokens, matrix)


PAD = 16


def pack_kernel(rows, place_ref, table_ref, index_ref, away_ref, *refs):
    own_ref, core_ref, slot_ref, sent_ref, kept_ref = refs
    index = index_ref[...]
    slot = jnp.zeros_like(index)
    for j in range(table_ref.shape[0]):
        slot += jnp.where(index == j, table_ref[j], 0)
    slot_ref[...] = slot
    tail = jnp.broadcast_to(slot.astype(jnp.float32), (PAD, rows)).astype(sent_ref.dtype)
    width = core_ref.shape[1]
    step = rows + PAD
    for source, out_ref, start in ((away_ref, sent_ref, 0), (own_ref, sent_ref, step), (core_ref, kept_ref, 0)):
        out_ref[start : start + rows] = source[...]
        out_ref[start + rows : start + step, :rows] = tail
        if width > rows:
            out_ref[start + rows : start + step, rows:] = jnp.zeros((PAD, width - rows), out_ref.dtype)


def pack(tokens, table, index, places, quarter):
    rows = tokens.shape[0]

    def column(i):
        return pl.BlockSpec((rows, quarter), lambda _, place: (0, place[i]))

    def whole(*shape):
        return pl.BlockSpec(shape, lambda _, place: (0, 0))

    shapes = [(1, rows), (2 * (rows + PAD), quarter), (rows + PAD, quarter)]
    return pl.pallas_call(
        lambda *refs: pack_kernel(rows, *refs),
        grid_spec=pltpu.PrefetchScalarGridSpec(
            num_scalar_prefetch=1,
            grid=(1,),
            in_specs=[pl.BlockSpec(memory_space=pltpu.SMEM), whole(1, rows), *map(column, range(3))],
            out_specs=[whole(*shape) for shape in shapes],
        ),
        out_shape=[
            jax.ShapeDtypeStruct(shapes[0], jnp.int32),
            jax.ShapeDtypeStruct(shapes[1], tokens.dtype),
            jax.ShapeDtypeStruct(shapes[2], tokens.dtype),
        ],
        cost_estimate=pl.CostEstimate(flops=0, bytes_accessed=0, transcendentals=0),
        name="pack",
    )(jnp.stack(places), table, index, tokens, tokens, tokens)


def shrink_kernel(rank, resident, rows, which, places, sums, first_ref, column_ref, *refs):
    weights = refs[-1 - sums - len(which) : len(refs) - 1 - sums]
    out_ref = refs[-1]
    held = rank * resident
    quarter = weights[0].shape[0]
    for part, (operand, row, slots) in enumerate(places):
        columns = slice(part * rows, (part + 1) * rows)
        if slots is None:
            tokens = refs[operand][row : row + rows]
            slot = refs[operand][row + rows : row + rows + PAD, :rows]
            slot = slot.astype(jnp.float32)[:1].astype(jnp.int32)
        else:
            tokens = refs[operand][:, pl.ds(pl.multiple_of(column_ref[0], quarter), quarter)]
            slot = refs[slots][...]
        total = refs[-2][:, columns] if sums else jnp.zeros((rank, rows), jnp.float32)
        for w, side in zip(weights, which):
            product = jnp.dot(tokens, w[...], preferred_element_type=jnp.float32)
            product = jnp.transpose(product[:, :held] + product[:, held:])
            for j in range(resident):
                chosen = slot == first_ref[side] + j
                total += jnp.where(chosen, product[j * rank : (j + 1) * rank], 0.0)
        out_ref[:, columns] = total


def shrink_step(operands, places, weights, firsts, column, which, sums, rows, rank, resident):
    vmem = pl.BlockSpec(memory_space=pltpu.VMEM)
    smem = pl.BlockSpec(memory_space=pltpu.SMEM)
    operands = [*operands, *weights, *sums]
    return pl.pallas_call(
        lambda *refs: shrink_kernel(rank, resident, rows, which, places, len(sums), *refs),
        in_specs=[smem, smem] + [vmem] * len(operands),
        out_specs=vmem,
        out_shape=jax.ShapeDtypeStruct((rank, len(places) * rows), jnp.float32),
        compiler_params=pltpu.CompilerParams(vmem_limit_bytes=16 * 2**20),
        cost_estimate=pl.CostEstimate(flops=0, bytes_accessed=0, transcendentals=0),
        name="shrink_step",
    )(firsts, jnp.reshape(column, (1,)), *operands)


def expand_kernel(rank, groups, scale, count, slots_ref, slot_ref, *refs):
    parts = refs[: 2 * len(groups)]
    bases, sums, out_ref = refs[2 * len(groups) : -1 - count], refs[-1 - count : -1], refs[-1]
    shrunk = sum(ref[...] for ref in sums[1:]) + sums[0][...] if count > 1 else sums[0][...]
    slot = slot_ref[...]
    update = 0.0
    at = 0
    for i, count in enumerate(groups):
        spread = jnp.concatenate(
            [jnp.where(slot == slots_ref[at + j], shrunk, 0.0) for j in range(count)], axis=0
        )
        at += count
        high = spread.astype(jnp.bfloat16)
        low = (spread - high.astype(jnp.float32)).astype(jnp.bfloat16)
        for left, right in ((high, parts[2 * i]), (low, parts[2 * i]), (high, parts[2 * i + 1])):
            update += lax.dot_general(
                left, right[...], (((0,), (0,)), ((), ())), preferred_element_type=jnp.float32
            )
    total = scale * update
    for base in bases:
        total += base[...]
    out_ref[...] = total.astype(jnp.bfloat16)


def expand_step(slots, slot, shrunk, parts, bases, rank, scale):
    groups = [high.shape[0] // rank for high, _ in parts]
    flat = [term for pair in parts for term in pair]
    operands = [slot, *flat, *bases, *shrunk]
    rows, span = bases[0].shape
    depth = rank * sum(groups)
    return pl.pallas_call(
        lambda *refs: expand_kernel(rank, groups, scale, len(shrunk), *refs),
        in_specs=[pl.BlockSpec(memory_space=pltpu.SMEM)]
        + [pl.BlockSpec(memory_space=pltpu.VMEM)] * len(operands),
        out_specs=pl.BlockSpec(memory_space=pltpu.VMEM),
        out_shape=jax.ShapeDtypeStruct((rows, span), jnp.bfloat16),
        compiler_params=pltpu.CompilerParams(vmem_limit_bytes=16 * 2**20),
        cost_estimate=pl.CostEstimate(flops=0, bytes_accessed=0, transcendentals=0),
        name="expand_step",
    )(slots, *operands)


def per_device(tokens, token_adapter_index, table, value_matrix, shrink_weight, expand_weight):
    rows, width = tokens.shape
    resident, rank, span = expand_weight.shape
    held = resident * rank
    owners = lax.axis_size("adapter")
    spots = owners // 2
    quarter = width // 4
    g, a = lax.axis_index("group"), lax.axis_index("adapter")
    c, half = a % 2, a // 2
    core_pairs = [(i, i ^ 1) for i in range(owners)]
    swap = [(0, 1), (1, 0)]
    barrier = lax.optimization_barrier

    def over_core(value):
        return lax.ppermute(value, "adapter", core_pairs)

    def over_group(value):
        return lax.ppermute(value, "group", swap)

    def shrink_rows(weight, side):
        rows_there = lax.dynamic_slice_in_dim(weight, (2 * g + side) * quarter, quarter, 0)
        return (rows_there * SHRINK_GAIN).astype(jnp.float16)

    give = shrink_rows(shrink_weight, 1 - c)
    given = over_core(give)
    shrink_later, expand_later, _ = barrier((shrink_weight, expand_weight, give))
    half_expand = lax.dynamic_slice_in_dim(
        expand_later.reshape(held, span), g * (held // 2), held // 2, 0
    )
    half_expand = (half_expand * EXPAND_GAIN).astype(jnp.float16)
    blocks = [half_expand[:, i * LANES : (i + 1) * LANES] for i in range(span // LANES)]
    mine = jnp.concatenate([shrink_rows(shrink_later, c), *blocks], axis=0)
    mine_line = Line(mine, spots, half)
    mine_line.advance()

    later, _ = barrier((tokens, mine))
    places = [2 * (1 - g) + 1 - c, 2 * (1 - g) + c, 2 * g + 1 - c]
    slot, sent, kept = pack(later, table, token_adapter_index[None, :], places, quarter)
    theirs = over_group(sent)
    given_line = Line(given, spots, half)
    given_line.advance()
    came_own = over_core(kept)
    came_theirs = over_core(theirs[: rows + PAD])

    source = jnp.asarray(sources(spots))[half]
    firsts = resident * (2 * source[:, None] + jnp.stack([c, 1 - c])[None, :]).reshape(-1)
    if spots > 2:
        mine_line.advance()
        given_line.advance()

    base_tokens, came_own, mine_line.up, mine_line.down = barrier(
        (tokens, came_own, mine_line.up, mine_line.down)
    )
    axes = ("tensor", "sub")
    if lax.axis_size("tensor") == 2 and lax.axis_size("sub") == 1:
        x = lax.axis_index("tensor")
        away = base_product(base_tokens, value_matrix, 1 - x, span)
        base_came = lax.ppermute(away, "tensor", swap)
        base_tokens, _ = barrier((tokens, away))
        bases = [base_product(base_tokens, value_matrix, x, span), base_came]
    else:
        partial = jnp.dot(base_tokens, value_matrix, preferred_element_type=jnp.float32)
        bases = [lax.psum_scatter(partial, axes, scatter_dimension=1, tiled=True)]

    for _ in range(spots - 3):
        mine_line.advance()
        given_line.advance()
    mine_pieces, given_pieces = mine_line.pieces(), given_line.pieces()

    column = (2 * g + c) * quarter

    def weights_of(start, stop):
        weights = []
        for i in range(start, stop):
            weights += [side_by_side(mine_pieces[i][:quarter]), side_by_side(given_pieces[i])]
        return weights

    def products(operands, places, weights, start, sums):
        which = list(range(2 * start, 2 * start + len(weights)))
        return shrink_step(
            operands, places, weights, firsts, column, which, sums, rows, rank, resident
        )

    here_parts = ((tokens, slot, came_own), ((0, 0, 1), (2, 0, None)))
    there_parts = ((theirs, came_theirs), ((0, rows + PAD, None), (1, 0, None)))
    all_parts = (
        (tokens, slot, came_own, theirs, came_theirs),
        ((0, 0, 1), (3, rows + PAD, None), (2, 0, None), (4, 0, None)),
    )

    last = len(mine_pieces) - 1
    here_sum = there_sum = None
    for start in range(0, last, 3):
        weights = weights_of(start, min(start + 3, last))
        here_sum = products(*here_parts, weights, start, [] if start == 0 else [here_sum])
        there_sum = products(*there_parts, weights, start, [] if start == 0 else [there_sum])
    expand_pieces = mine_pieces
    if spots == 4:
        mine_line.found[-1], given_line.found[-1], here_sum, there_sum = barrier(
            (mine_line.found[-1], given_line.found[-1], here_sum, there_sum)
        )
        mine_pieces, given_pieces = mine_line.pieces(), given_line.pieces()
    before = jnp.concatenate(
        [here_sum[:, :rows], there_sum[:, :rows], here_sum[:, rows:], there_sum[:, rows:]], axis=1
    )
    total = products(*all_parts, weights_of(last, last + 1), last, [before])
    both_sum = total[:, : 2 * rows] + over_core(total[:, 2 * rows :])
    own_sum, other_sum = both_sum[:, :rows], both_sum[:, rows:]
    if len(bases) == 2:
        across = [(i, 3 - i) for i in range(4)]
        shrunk = [
            own_sum,
            lax.ppermute(other_sum, ("group", "tensor"), across),
            over_group(other_sum),
            lax.ppermute(own_sum, "tensor", swap),
        ]
    else:
        shrunk = [lax.psum(own_sum + over_group(other_sum), axes)]

    def expand_of(piece):
        cut = piece[quarter:].reshape(span // LANES, held // 2, LANES)
        return jnp.concatenate([cut[i] for i in range(span // LANES)], axis=1)

    here = jnp.concatenate([expand_of(piece) for piece in expand_pieces], axis=0)
    across = over_group(here)
    beside = over_core(jnp.concatenate([here, across], axis=0))
    terms = [two_terms(here), two_terms(across), two_terms(beside)]
    steps = jnp.arange(resident // 2, dtype=jnp.int32)
    sides = jnp.stack([c, 1 - c])[:, None, None, None]
    halves = jnp.stack([g, 1 - g])[None, :, None, None] * (resident // 2)
    slots = (2 * source[:, None] + sides) * resident + halves + steps
    slots = slots.astype(jnp.int32).reshape(-1)
    scale = SCALING / (SHRINK_GAIN * EXPAND_GAIN)
    return expand_step(slots, slot, shrunk, terms, bases, rank, scale)


def solution(mesh):
    placed = (
        P(("group", "adapter"), ("tensor", "sub")),
        P(("group", "adapter")),
        P("group"),
        P(("tensor", "sub"), None),
        P(("tensor", "sub"), "adapter"),
        P("adapter", None, ("tensor", "sub")),
    )
    return jax.shard_map(
        per_device,
        mesh=mesh,
        in_specs=placed,
        out_specs=P(("group", "adapter"), ("tensor", "sub")),
        check_vma=False,
    )
```

time: 385 us -> 73.4 us (0.19)
  waiting for transfers between devices: 285 us -> 14.9 us
  matrix products: 23.5 us -> 0 us
  local copies, waits for them, and re-layouts: 26.7 us -> 7.22 us
  Pallas kernels: 0 us -> 15 us
  between operations: 13.5 us -> 0.61 us
  starting transfers between devices: 16.2 us -> 28.2 us
  blocking collectives: 9.37 us -> 0 us
  other arithmetic: 10.6 us -> 6.16 us
    all_to_all x3 -> x0, waiting for transfers between devices: 265 us -> none  [the longest x1 172 us: per_device(): lax.all_to_all(packed, 'adapter', split_axis=0, concat_axis=0, tiled=True)]
    ppermute x0 -> x21, starting transfers between devices: none -> 28.2 us  [the longest x10 18.7 us: send(): lax.ppermute(value, 'adapter', [(2 * s + c, 2 * d + c) for s, d in moves...]
    dot_general x3 -> x0, matrix products: 23.5 us -> none  [the longest x1 11.4 us: shrink_masked(): jnp.dot(flattened, shrink_weight, precision=lax.Precision.HIGHEST, prefer...]
    gather x4 -> x0, local copies, waits for them, and re-layouts: 19.7 us -> none  [the longest x1 7.82 us: per_device(): tokens[source]]
    reduce_scatter x1 -> x0, waiting for transfers between devices: 19.4 us -> none  [per_device(): lax.psum_scatter(matrix_product + jnp.transpose(adapter_update), ('tensor...]
    all_to_all x3 -> x0, starting transfers between devices: 16 us -> none  [the longest x1 6.33 us: per_device(): lax.all_to_all(labels, 'adapter', split_axis=0, concat_axis=0, tiled=True)]
    pallas_call x0 -> x7, Pallas kernels: none -> 15 us  [the longest x3 6.86 us: shrink_step(): pl.pallas_call(lambda *refs: shrink_kernel(rank, resident, rows, which, p...]
    ppermute x0 -> x21, waiting for transfers between devices: none -> 14.9 us  [the longest x10 10.1 us: send(): lax.ppermute(value, 'adapter', [(2 * s + c, 2 * d + c) for s, d in moves...]
  transfers between devices with their start and end apart: 4 -> 21, of which waited for: 3 -> 8; matrix products, arithmetic and copies ran while one was open for 5% -> 6% of each run, Pallas kernels for 0% -> 18%
where the time goes in v3:
time: 73.4 us; the launch traced here: 72.2 us
  starting transfers between devices  28.2 us (38%)
  Pallas kernels  15 us (20%)
  waiting for transfers between devices  14.9 us (20%)
  local copies, waits for them, and re-layouts  7.22 us (10%)
  other arithmetic  6.16 us (8%)
    ppermute x10, starting transfers between devices, send(): lax.ppermute(value, 'adapter', [(2 * s + c, 2 * d + c) for s, d in moves...  18.7 us
    ppermute x10, waiting for transfers between devices, send(): lax.ppermute(value, 'adapter', [(2 * s + c, 2 * d + c) for s, d in moves...  10.1 us
    unnamed x16, local copies, waits for them, and re-layouts  6.87 us
    pallas_call x3, Pallas kernels, shrink_step(): pl.pallas_call(lambda *refs: shrink_kernel(rank, resident, rows, which, p...  6.86 us
    ppermute x3, starting transfers between devices, over_group(): return lax.ppermute(value, 'group', swap)  3.63 us
    pallas_call x1, Pallas kernels, pack(): pl.pallas_call(lambda *refs: pack_kernel(rows, *refs), grid_spec=pltpu.Pr...  3.35 us
    ppermute x3, waiting for transfers between devices, over_group(): return lax.ppermute(value, 'group', swap)  2.57 us
    pallas_call x2, Pallas kernels, base_product(): pl.pallas_call(lambda *refs: product_kernel(span, *refs), in_specs=[pl.Bl...  2.53 us
  transfers between devices with their start and end apart: 21, of which 8 were waited for; matrix products, arithmetic and copies ran while one was open for 6% of the time, Pallas kernels for 18%

profile of v3, /device:TPU:0, one launch (start us, length us, event | category | flops | bytes accessed | tf_op | source)
XLA Modules:
  0.0 72.2 jit_solution(17859313926206826948)
XLA Ops:
  0.0 1.1 %multiply_convert_fusion.1 = f16[1024,128]{1,0:T(8,128)(2,1)S(1)} fusion(f32[4096,128]{1,0:T(8,128)} %param.11, s32[]{:T(128)S(6)} %select_n.70), kind=kLoop, calls=%fused_computation.42 | loop fusion | flops 262144 | bytes 786436 | tf_op jit(solution)/shard_map/convert_element_type | solution.py:248
  1.1 1.1 %reduce-precision_convert_fusion.8 = (bf16[1024,128]{1,0:T(8,128)(2,1)S(1)}, f16[1024,128]{1,0:T(8,128)(2,1)S(1)}) fusion(f32[4096,128]{1,0:T(8,128)} %param.11, s32[]{:T(128)S(6)} %select_n.71), kind=kLoop, calls=%fused_computation.18 | loop fusion | flops 655360 | bytes 1048580 | tf_op jit(solution)/shard_map/convert_element_type | solution.py:71
  2.5 4.9 %collective-permute-start.1 = (f16[1280,128]{1,0:T(8,128)(2,1)S(1)}, f16[1280,128]{1,0:T(8,128)(2,1)S(1)}, u32[]{:S(2)}, u32[]{:S(2)}) collective-permute-start(f16[1280,128]{1,0:T(8,128)(2,1)S(1)} %constant_dynamic-update-slice_fusion), channel_id=1, source_target_pairs={{0,4},{2,6},{4,8},{6,10},{8,12},{10,14},{1,5},{3,7},{5,9},{7,11},{... | collective-permute-start | bytes 983048 | tf_op jit(solution)/shard_map/ppermute | solution.py:41
  7.4 1.3 %collective-permute-start = (f16[1280,128]{1,0:T(8,128)(2,1)S(1)}, f16[1280,128]{1,0:T(8,128)(2,1)S(1)}, u32[]{:S(2)}, u32[]{:S(2)}) collective-permute-start(f16[1280,128]{1,0:T(8,128)(2,1)S(1)} %constant_dynamic-update-slice_fusion), channel_id=1, source_target_pairs={{4,0},{6,2},{8,4},{10,6},{12,8},{14,10},{5,1},{7,3},{9,5},{11,7},{... | collective-permute-start | bytes 983048 | tf_op jit(solution)/shard_map/ppermute | solution.py:41
  9.4 3.4 %pack.1 = (s32[1,256]{1,0:T(1,128)}, bf16[544,1024]{1,0:T(8,128)(2,1)}, bf16[272,1024]{1,0:T(8,128)(2,1)}) custom-call(s32[3]{0:T(128)} %pad_add_fusion.1.refs_0_, s32[64]{0:T(128)} %refs_1_.1, s32[1,256]{1,0:T(1,128)} %bitcast.15, bf16[256,4096]{1,0:T(8,128)(2,1)} %refs_2_.7, bf16[256,4096]{1,0:T(8,128)(2,1)} %refs_2_.7, bf16[256,4096]{1,0:T(8,128)(2,1)} %refs_2_.7), custom_call_target="tpu_custom_call" | custom-call | tf_op jit(solution)/shard_map/pack/pallas_call | solution.py:128
  13.4 0.7 fusion.12
  14.6 4.7 %collective-permute-start.12 = (f16[1024,128]{1,0:T(8,128)(2,1)S(1)}, f16[1024,128]{1,0:T(8,128)(2,1)S(1)}, u32[]{:S(2)}, u32[]{:S(2)}) collective-permute-start(f16[1024,128]{1,0:T(8,128)(2,1)S(1)} %collective-permute-done.11), channel_id=1, source_target_pairs={{0,4},{2,6},{4,8},{6,10},{8,12},{10,14},{1,5},{3,7},{5,9},{7,11},{... | collective-permute-start | bytes 786440 | tf_op jit(solution)/shard_map/ppermute | solution.py:41
  19.3 1.3 %collective-permute-start.14 = (f16[1024,128]{1,0:T(8,128)(2,1)S(1)}, f16[1024,128]{1,0:T(8,128)(2,1)S(1)}, u32[]{:S(2)}, u32[]{:S(2)}) collective-permute-start(f16[1024,128]{1,0:T(8,128)(2,1)S(1)} %collective-permute-done.11), channel_id=1, source_target_pairs={{4,0},{6,2},{8,4},{10,6},{12,8},{14,10},{5,1},{7,3},{9,5},{11,7},{... | collective-permute-start | bytes 786440 | tf_op jit(solution)/shard_map/ppermute | solution.py:41
  20.7 0.7 collective-permute-start.2
  21.4 1.3 %collective-permute-start.3 = (f16[1280,128]{1,0:T(8,128)(2,1)S(1)}, f16[1280,128]{1,0:T(8,128)(2,1)S(1)}, u32[]{:S(2)}, u32[]{:S(2)}) collective-permute-start(f16[1280,128]{1,0:T(8,128)(2,1)S(1)} %collective-permute-done), channel_id=1, source_target_pairs={{4,0},{6,2},{8,4},{10,6},{5,1},{7,3},{9,5},{11,7},{20,16},{22,18},... | collective-permute-start | bytes 983048 | tf_op jit(solution)/shard_map/ppermute | solution.py:41
  22.9 2.2 %collective-permute-done.12 = f16[1024,128]{1,0:T(8,128)(2,1)S(1)} collective-permute-done((f16[1024,128]{1,0:T(8,128)(2,1)S(1)}, f16[1024,128]{1,0:T(8,128)(2,1)S(1)}, u32[]{:S(2)}, u32[]{:S(2)}) %collective-permute-start.12) | collective-permute-done | bytes 262176 | tf_op jit(solution)/shard_map/ppermute | solution.py:41
  25.1 1.5 %collective-permute-start.9 = (bf16[544,1024]{1,0:T(8,128)(2,1)S(1)}, bf16[544,1024]{1,0:T(8,128)(2,1)S(1)}, u32[]{:S(2)}, u32[]{:S(2)}) collective-permute-start(bf16[544,1024]{1,0:T(8,128)(2,1)S(1)} %copy-done.5), channel_id=1, source_target_pairs={{0,16},{16,0},{1,17},{17,1},{2,18},{18,2},{3,19},{19,3},{4,20},{20... | collective-permute-start | bytes 3342344 | tf_op jit(solution)/shard_map/ppermute | solution.py:244
  26.6 2.9 %collective-permute-done.14 = f16[1024,128]{1,0:T(8,128)(2,1)S(1)} collective-permute-done((f16[1024,128]{1,0:T(8,128)(2,1)S(1)}, f16[1024,128]{1,0:T(8,128)(2,1)S(1)}, u32[]{:S(2)}, u32[]{:S(2)}) %collective-permute-start.14) | collective-permute-done | bytes 262176 | tf_op jit(solution)/shard_map/ppermute | solution.py:41
  30.3 1.3 %collective-permute-start.15 = (f16[1024,128]{1,0:T(8,128)(2,1)S(1)}, f16[1024,128]{1,0:T(8,128)(2,1)S(1)}, u32[]{:S(2)}, u32[]{:S(2)}) collective-permute-start(f16[1024,128]{1,0:T(8,128)(2,1)S(1)} %collective-permute-done.14), channel_id=1, source_target_pairs={{4,0},{6,2},{8,4},{10,6},{5,1},{7,3},{9,5},{11,7},{20,16},{22,18},... | collective-permute-start | bytes 786440 | tf_op jit(solution)/shard_map/ppermute | solution.py:41
  31.6 5.0 %collective-permute-done.3 = f16[1280,128]{1,0:T(8,128)(2,1)S(1)} collective-permute-done((f16[1280,128]{1,0:T(8,128)(2,1)S(1)}, f16[1280,128]{1,0:T(8,128)(2,1)S(1)}, u32[]{:S(2)}, u32[]{:S(2)}) %collective-permute-start.3) | collective-permute-done | bytes 327712 | tf_op jit(solution)/shard_map/ppermute | solution.py:41
  36.8 1.3 %collective-permute-start.5 = (f16[1280,128]{1,0:T(8,128)(2,1)S(1)}, f16[1280,128]{1,0:T(8,128)(2,1)S(1)}, u32[]{:S(2)}, u32[]{:S(2)}) collective-permute-start(f16[1280,128]{1,0:T(8,128)(2,1)S(1)} %broadcast_select_fusion.1), channel_id=1, source_target_pairs={{8,12},{10,14},{4,0},{6,2},{9,13},{11,15},{5,1},{7,3},{24,28},{26,... | collective-permute-start | bytes 983048 | tf_op jit(solution)/shard_map/ppermute | solution.py:41
  38.2 3.4 %copy-done.1 = bf16[4096,1024]{1,0:T(8,128)(2,1)S(1)} copy-done((bf16[4096,1024]{1,0:T(8,128)(2,1)S(1)}, bf16[4096,1024]{1,0:T(8,128)(2,1)}, u32[]{:S(2)}) %copy-start.1) | copy-done | bytes 8388632
  41.5 1.3 %base_product.2 = f32[256,512]{1,0:T(8,128)S(1)} custom-call(s32[1]{0:T(128)} %bitcast.11.refs_0_, bf16[256,4096]{1,0:T(8,128)(2,1)S(1)} %copy-done, bf16[4096,1024]{1,0:T(8,128)(2,1)S(1)} %copy-done.1), custom_call_target="tpu_custom_call" | custom-call | tf_op jit(solution)/shard_map/base_product/pallas_call | solution.py:87
  42.8 1.6 %collective-permute-start.8 = (f32[256,512]{1,0:T(8,128)S(1)}, f32[256,512]{1,0:T(8,128)S(1)}, u32[]{:S(2)}, u32[]{:S(2)}) collective-permute-start(f32[256,512]{1,0:T(8,128)S(1)} %base_product.2), channel_id=1, source_target_pairs={{0,1},{1,0},{2,3},{3,2},{4,5},{5,4},{6,7},{7,6},{8,9},{9,8},{10,11... | collective-permute-start | bytes 1572872 | tf_op jit(solution)/shard_map/ppermute | solution.py:284
  44.5 3.4 %copy-done.2 = bf16[4096,1024]{1,0:T(8,128)(2,1)S(1)} copy-done((bf16[4096,1024]{1,0:T(8,128)(2,1)S(1)}, bf16[4096,1024]{1,0:T(8,128)(2,1)}, u32[]{:S(2)}) %copy-start.2) | copy-done | bytes 8388632
  47.9 1.3 %base_product.3.refs_8_ = f32[256,512]{1,0:T(8,128)S(1)} custom-call(s32[1]{0:T(128)} %bitcast.10.refs_0_, bf16[256,4096]{1,0:T(8,128)(2,1)S(1)} %copy-done, bf16[4096,1024]{1,0:T(8,128)(2,1)S(1)} %copy-done.2), custom_call_target="tpu_custom_call" | custom-call | tf_op jit(solution)/shard_map/base_product/pallas_call | solution.py:87
  49.3 1.3 %collective-permute-start.16 = (f16[1024,128]{1,0:T(8,128)(2,1)S(1)}, f16[1024,128]{1,0:T(8,128)(2,1)S(1)}, u32[]{:S(2)}, u32[]{:S(2)}) collective-permute-start(f16[1024,128]{1,0:T(8,128)(2,1)S(1)} %get-tuple-element.34), channel_id=1, source_target_pairs={{8,12},{10,14},{4,0},{6,2},{9,13},{11,15},{5,1},{7,3},{24,28},{26,... | collective-permute-start | bytes 786440 | tf_op jit(solution)/shard_map/ppermute | solution.py:41
  51.2 1.6 %collective-permute-start.6 = (f16[256,512]{1,0:T(8,128)(2,1)S(1)}, f16[256,512]{1,0:T(8,128)(2,1)S(1)}, u32[]{:S(2)}, u32[]{:S(2)}) collective-permute-start(f16[256,512]{1,0:T(8,128)(2,1)S(1)} %get-tuple-element.40), channel_id=1, source_target_pairs={{0,16},{16,0},{1,17},{17,1},{2,18},{18,2},{3,19},{19,3},{4,20},{20... | collective-permute-start | bytes 786440 | tf_op jit(solution)/shard_map/ppermute | solution.py:244
  53.2 2.5 %shrink_step.3 = f32[16,512]{1,0:T(8,128)S(1)} custom-call(s32[8]{0:T(128)S(1)} %mul.83.refs_0_, s32[1]{0:T(128)} %bitcast.12.refs_1_, bf16[256,4096]{1,0:T(8,128)(2,1)S(1)} %copy-done, s32[1,256]{1,0:T(1,128)S(1)} %copy-done.3, bf16[272,1024]{1,0:T(8,128)(2,1)S(1)} %collective-permute-done.4.refs_4_, ...), custom_call_target="tpu_custom_call" | custom-call | tf_op jit(solution)/shard_map/shrink_step/pallas_call | solution.py:174
  55.7 2.0 %collective-permute-done.6 = f16[256,512]{1,0:T(8,128)(2,1)S(1)} collective-permute-done((f16[256,512]{1,0:T(8,128)(2,1)S(1)}, f16[256,512]{1,0:T(8,128)(2,1)S(1)}, u32[]{:S(2)}, u32[]{:S(2)}) %collective-permute-start.6) | collective-permute-done | bytes 262176 | tf_op jit(solution)/shard_map/ppermute | solution.py:244
  57.8 2.5 %shrink_step.4 = f32[16,512]{1,0:T(8,128)S(1)} custom-call(s32[8]{0:T(128)S(1)} %mul.83.refs_0_, s32[1]{0:T(128)} %bitcast.12.refs_1_, bf16[544,1024]{1,0:T(8,128)(2,1)S(1)} %collective-permute-done.9.refs_2_.refs_5_, bf16[272,1024]{1,0:T(8,128)(2,1)S(1)} %collective-permute-done.10.refs_3_.refs_6_, bf16[1024,256]{1,0:T(8,128)(2,1)S(1)} %get-tuple-element.83.refs_5_.refs_4_, ...), custom_call_target="tpu_custom_call" | custom-call | tf_op jit(solution)/shard_map/shrink_step/pallas_call | solution.py:174
  60.7 1.9 %shrink_step.5 = f32[16,1024]{1,0:T(8,128)S(1)} custom-call(s32[8]{0:T(128)S(1)} %mul.83.refs_0_, s32[1]{0:T(128)} %bitcast.12.refs_1_, bf16[256,4096]{1,0:T(8,128)(2,1)S(1)} %copy-done, s32[1,256]{1,0:T(1,128)S(1)} %copy-done.3, bf16[272,1024]{1,0:T(8,128)(2,1)S(1)} %collective-permute-done.4.refs_4_, ...), custom_call_target="tpu_custom_call" | custom-call | tf_op jit(solution)/shard_map/shrink_step/pallas_call | solution.py:174
  63.3 0.8 %collective-permute-done.17 = f32[16,512]{1,0:T(8,128)S(1)} collective-permute-done((f32[16,512]{1,0:T(8,128)S(1)}, f32[16,512]{1,0:T(8,128)S(1)}, u32[]{:S(2)}, u32[]{:S(2)}) %collective-permute-start.17) | collective-permute-done | bytes 32800 | tf_op jit(solution)/shard_map/ppermute | solution.py:241
  64.1 1.5 %collective-permute-start.18 = (f32[16,256]{1,0:T(8,128)S(1)}, f32[16,256]{1,0:T(8,128)S(1)}, u32[]{:S(2)}, u32[]{:S(2)}) collective-permute-start(f32[16,256]{1,0:T(8,128)S(1)} %get-tuple-element.71), channel_id=1, source_target_pairs={{0,17},{1,16},{16,1},{17,0},{2,19},{3,18},{18,3},{19,2},{4,21},{5,... | collective-permute-start | bytes 49160 | tf_op jit(solution)/shard_map/ppermute | solution.py:339
  66.2 1.5 %collective-permute-start.20 = (f32[16,256]{1,0:T(8,128)S(1)}, f32[16,256]{1,0:T(8,128)S(1)}, u32[]{:S(2)}, u32[]{:S(2)}) collective-permute-start(f32[16,256]{1,0:T(8,128)S(1)} %get-tuple-element.72.refs_10_), channel_id=1, source_target_pairs={{0,1},{1,0},{2,3},{3,2},{4,5},{5,4},{6,7},{7,6},{8,9},{9,8},{10,11... | collective-permute-start | bytes 49160 | tf_op jit(solution)/shard_map/ppermute | solution.py:341
  67.8 1.0 %collective-permute-done.18.refs_11_ = f32[16,256]{1,0:T(8,128)S(1)} collective-permute-done((f32[16,256]{1,0:T(8,128)S(1)}, f32[16,256]{1,0:T(8,128)S(1)}, u32[]{:S(2)}, u32[]{:S(2)}) %collective-permute-start.18) | collective-permute-done | bytes 16416 | tf_op jit(solution)/shard_map/ppermute | solution.py:339
  69.9 2.3 %expand_step.1 = bf16[256,512]{1,0:T(8,128)(2,1)} custom-call(s32[64]{0:T(128)S(1)} %add.115.refs_0_, s32[1,256]{1,0:T(1,128)S(1)} %copy-done.3, bf16[256,512]{1,0:T(8,128)(2,1)S(1)} %reduce-precision_convert_fusion.10.refs_2_, bf16[256,512]{1,0:T(8,128)(2,1)S(1)} %get-tuple-element.39.refs_3_, bf16[256,512]{1,0:T(8,128)(2,1)S(1)} %get-tuple-element.70.refs_4_, ...), custom_call_target="tpu_custom_call" | custom-call | tf_op jit(solution)/shard_map/expand_step/pallas_call | solution.py:215
  (80 shorter events, 7.2 us)
Async XLA Ops:
  0.0 2.3 %copy-start.4 = (f32[8,16,512]{2,1,0:T(8,128)S(1)}, f32[8,16,512]{2,1,0:T(8,128)}, u32[]{:S(2)}) copy-start(f32[8,16,512]{2,1,0:T(8,128)} %param.12) | copy-start | bytes 786436
  2.5 18.3 %collective-permute-start.1 = (f16[1280,128]{1,0:T(8,128)(2,1)S(1)}, f16[1280,128]{1,0:T(8,128)(2,1)S(1)}, u32[]{:S(2)}, u32[]{:S(2)}) collective-permute-start(f16[1280,128]{1,0:T(8,128)(2,1)S(1)} %constant_dynamic-update-slice_fusion), channel_id=1, source_target_pairs={{0,4},{2,6},{4,8},{6,10},{8,12},{10,14},{1,5},{3,7},{5,9},{7,11},{... | collective-permute-start | bytes 983048 | tf_op jit(solution)/shard_map/ppermute | solution.py:41
  7.4 14.0 %collective-permute-start = (f16[1280,128]{1,0:T(8,128)(2,1)S(1)}, f16[1280,128]{1,0:T(8,128)(2,1)S(1)}, u32[]{:S(2)}, u32[]{:S(2)}) collective-permute-start(f16[1280,128]{1,0:T(8,128)(2,1)S(1)} %constant_dynamic-update-slice_fusion), channel_id=1, source_target_pairs={{4,0},{6,2},{8,4},{10,6},{12,8},{14,10},{5,1},{7,3},{9,5},{11,7},{... | collective-permute-start | bytes 983048 | tf_op jit(solution)/shard_map/ppermute | solution.py:41
  8.7 5.9 %collective-permute-start.11 = (f16[1024,128]{1,0:T(8,128)(2,1)S(1)}, f16[1024,128]{1,0:T(8,128)(2,1)S(1)}, u32[]{:S(2)}, u32[]{:S(2)}) collective-permute-start(f16[1024,128]{1,0:T(8,128)(2,1)S(1)} %multiply_convert_fusion.1), channel_id=1, source_target_pairs={{0,2},{2,0},{4,6},{6,4},{8,10},{10,8},{12,14},{14,12},{1,3},{3,1},... | collective-permute-start | bytes 786440 | tf_op jit(solution)/shard_map/ppermute | solution.py:241
  12.8 24.0 %collective-permute-start.4 = (bf16[272,1024]{1,0:T(8,128)(2,1)}, bf16[272,1024]{1,0:T(8,128)(2,1)S(1)}, u32[]{:S(2)}, u32[]{:S(2)}) collective-permute-start(bf16[272,1024]{1,0:T(8,128)(2,1)} %get-tuple-element.23), channel_id=1, source_target_pairs={{0,2},{2,0},{4,6},{6,4},{8,10},{10,8},{12,14},{14,12},{1,3},{3,1},... | collective-permute-start | bytes 1671176 | tf_op jit(solution)/shard_map/ppermute | solution.py:241
  14.6 10.4 %copy-start.5 = (bf16[544,1024]{1,0:T(8,128)(2,1)S(1)}, bf16[544,1024]{1,0:T(8,128)(2,1)}, u32[]{:S(2)}) copy-start(bf16[544,1024]{1,0:T(8,128)(2,1)} %get-tuple-element.28) | copy-start | bytes 3342340
  14.6 10.4 %collective-permute-start.12 = (f16[1024,128]{1,0:T(8,128)(2,1)S(1)}, f16[1024,128]{1,0:T(8,128)(2,1)S(1)}, u32[]{:S(2)}, u32[]{:S(2)}) collective-permute-start(f16[1024,128]{1,0:T(8,128)(2,1)S(1)} %collective-permute-done.11), channel_id=1, source_target_pairs={{0,4},{2,6},{4,8},{6,10},{8,12},{10,14},{1,5},{3,7},{5,9},{7,11},{... | collective-permute-start | bytes 786440 | tf_op jit(solution)/shard_map/ppermute | solution.py:41
  19.3 10.2 %collective-permute-start.14 = (f16[1024,128]{1,0:T(8,128)(2,1)S(1)}, f16[1024,128]{1,0:T(8,128)(2,1)S(1)}, u32[]{:S(2)}, u32[]{:S(2)}) collective-permute-start(f16[1024,128]{1,0:T(8,128)(2,1)S(1)} %collective-permute-done.11), channel_id=1, source_target_pairs={{4,0},{6,2},{8,4},{10,6},{12,8},{14,10},{5,1},{7,3},{9,5},{11,7},{... | collective-permute-start | bytes 786440 | tf_op jit(solution)/shard_map/ppermute | solution.py:41
  20.7 9.6 %collective-permute-start.2 = (f16[1280,128]{1,0:T(8,128)(2,1)S(1)}, f16[1280,128]{1,0:T(8,128)(2,1)S(1)}, u32[]{:S(2)}, u32[]{:S(2)}) collective-permute-start(f16[1280,128]{1,0:T(8,128)(2,1)S(1)} %collective-permute-done.1), channel_id=1, source_target_pairs={{4,8},{6,10},{8,12},{10,14},{5,9},{7,11},{9,13},{11,15},{20,24},{2... | collective-permute-start | bytes 983048 | tf_op jit(solution)/shard_map/ppermute | solution.py:41
  21.4 15.2 %collective-permute-start.3 = (f16[1280,128]{1,0:T(8,128)(2,1)S(1)}, f16[1280,128]{1,0:T(8,128)(2,1)S(1)}, u32[]{:S(2)}, u32[]{:S(2)}) collective-permute-start(f16[1280,128]{1,0:T(8,128)(2,1)S(1)} %collective-permute-done), channel_id=1, source_target_pairs={{4,0},{6,2},{8,4},{10,6},{5,1},{7,3},{9,5},{11,7},{20,16},{22,18},... | collective-permute-start | bytes 983048 | tf_op jit(solution)/shard_map/ppermute | solution.py:41
  22.7 15.4 %copy-start = (bf16[256,4096]{1,0:T(8,128)(2,1)S(1)}, bf16[256,4096]{1,0:T(8,128)(2,1)}, u32[]{:S(2)}) copy-start(bf16[256,4096]{1,0:T(8,128)(2,1)} %refs_2_.7) | copy-start | bytes 6291460
  25.1 27.9 %collective-permute-start.9 = (bf16[544,1024]{1,0:T(8,128)(2,1)S(1)}, bf16[544,1024]{1,0:T(8,128)(2,1)S(1)}, u32[]{:S(2)}, u32[]{:S(2)}) collective-permute-start(bf16[544,1024]{1,0:T(8,128)(2,1)S(1)} %copy-done.5), channel_id=1, source_target_pairs={{0,16},{16,0},{1,17},{17,1},{2,18},{18,2},{3,19},{19,3},{4,20},{20... | collective-permute-start | bytes 3342344 | tf_op jit(solution)/shard_map/ppermute | solution.py:244
  29.5 19.7 %collective-permute-start.13 = (f16[1024,128]{1,0:T(8,128)(2,1)S(1)}, f16[1024,128]{1,0:T(8,128)(2,1)S(1)}, u32[]{:S(2)}, u32[]{:S(2)}) collective-permute-start(f16[1024,128]{1,0:T(8,128)(2,1)S(1)} %collective-permute-done.12), channel_id=1, source_target_pairs={{4,8},{6,10},{8,12},{10,14},{5,9},{7,11},{9,13},{11,15},{20,24},{2... | collective-permute-start | bytes 786440 | tf_op jit(solution)/shard_map/ppermute | solution.py:41
  30.3 18.9 %collective-permute-start.15 = (f16[1024,128]{1,0:T(8,128)(2,1)S(1)}, f16[1024,128]{1,0:T(8,128)(2,1)S(1)}, u32[]{:S(2)}, u32[]{:S(2)}) collective-permute-start(f16[1024,128]{1,0:T(8,128)(2,1)S(1)} %collective-permute-done.14), channel_id=1, source_target_pairs={{4,0},{6,2},{8,4},{10,6},{5,1},{7,3},{9,5},{11,7},{20,16},{22,18},... | collective-permute-start | bytes 786440 | tf_op jit(solution)/shard_map/ppermute | solution.py:41
  36.8 13.9 %collective-permute-start.5 = (f16[1280,128]{1,0:T(8,128)(2,1)S(1)}, f16[1280,128]{1,0:T(8,128)(2,1)S(1)}, u32[]{:S(2)}, u32[]{:S(2)}) collective-permute-start(f16[1280,128]{1,0:T(8,128)(2,1)S(1)} %broadcast_select_fusion.1), channel_id=1, source_target_pairs={{8,12},{10,14},{4,0},{6,2},{9,13},{11,15},{5,1},{7,3},{24,28},{26,... | collective-permute-start | bytes 983048 | tf_op jit(solution)/shard_map/ppermute | solution.py:41
  38.1 3.4 %copy-start.1 = (bf16[4096,1024]{1,0:T(8,128)(2,1)S(1)}, bf16[4096,1024]{1,0:T(8,128)(2,1)}, u32[]{:S(2)}) copy-start(bf16[4096,1024]{1,0:T(8,128)(2,1)} %refs_2_.5) | copy-start | bytes 25165828
  42.8 25.0 %collective-permute-start.8 = (f32[256,512]{1,0:T(8,128)S(1)}, f32[256,512]{1,0:T(8,128)S(1)}, u32[]{:S(2)}, u32[]{:S(2)}) collective-permute-start(f32[256,512]{1,0:T(8,128)S(1)} %base_product.2), channel_id=1, source_target_pairs={{0,1},{1,0},{2,3},{3,2},{4,5},{5,4},{6,7},{7,6},{8,9},{9,8},{10,11... | collective-permute-start | bytes 1572872 | tf_op jit(solution)/shard_map/ppermute | solution.py:284
  44.5 3.4 %copy-start.2 = (bf16[4096,1024]{1,0:T(8,128)(2,1)S(1)}, bf16[4096,1024]{1,0:T(8,128)(2,1)}, u32[]{:S(2)}) copy-start(bf16[4096,1024]{1,0:T(8,128)(2,1)} %refs_2_.5) | copy-start | bytes 25165828
  49.3 11.0 %collective-permute-start.16 = (f16[1024,128]{1,0:T(8,128)(2,1)S(1)}, f16[1024,128]{1,0:T(8,128)(2,1)S(1)}, u32[]{:S(2)}, u32[]{:S(2)}) collective-permute-start(f16[1024,128]{1,0:T(8,128)(2,1)S(1)} %get-tuple-element.34), channel_id=1, source_target_pairs={{8,12},{10,14},{4,0},{6,2},{9,13},{11,15},{5,1},{7,3},{24,28},{26,... | collective-permute-start | bytes 786440 | tf_op jit(solution)/shard_map/ppermute | solution.py:41
  51.0 2.2 %copy-start.3 = (s32[1,256]{1,0:T(1,128)S(1)}, s32[1,256]{1,0:T(1,128)}, u32[]{:S(2)}) copy-start(s32[1,256]{1,0:T(1,128)} %get-tuple-element.22.refs_3_.refs_1_) | copy-start | bytes 3076
  51.2 6.5 %collective-permute-start.6 = (f16[256,512]{1,0:T(8,128)(2,1)S(1)}, f16[256,512]{1,0:T(8,128)(2,1)S(1)}, u32[]{:S(2)}, u32[]{:S(2)}) collective-permute-start(f16[256,512]{1,0:T(8,128)(2,1)S(1)} %get-tuple-element.40), channel_id=1, source_target_pairs={{0,16},{16,0},{1,17},{17,1},{2,18},{18,2},{3,19},{19,3},{4,20},{20... | collective-permute-start | bytes 786440 | tf_op jit(solution)/shard_map/ppermute | solution.py:244
  53.0 4.8 %collective-permute-start.10 = (bf16[272,1024]{1,0:T(8,128)(2,1)S(1)}, bf16[272,1024]{1,0:T(8,128)(2,1)S(1)}, u32[]{:S(2)}, u32[]{:S(2)}) collective-permute-start(bf16[272,1024]{1,0:T(8,128)(2,1)S(1)} %slice.166), channel_id=1, source_target_pairs={{0,2},{2,0},{4,6},{6,4},{8,10},{10,8},{12,14},{14,12},{1,3},{3,1},... | collective-permute-start | bytes 1671176 | tf_op jit(solution)/shard_map/ppermute | solution.py:241
  57.7 9.9 %collective-permute-start.7 = (f16[512,512]{1,0:T(8,128)(2,1)S(1)}, f16[512,512]{1,0:T(8,128)(2,1)S(1)}, u32[]{:S(2)}, u32[]{:S(2)}) collective-permute-start(f16[512,512]{1,0:T(8,128)(2,1)S(1)} %constant_dynamic-update-slice_fusion.5), channel_id=1, source_target_pairs={{0,2},{2,0},{4,6},{6,4},{8,10},{10,8},{12,14},{14,12},{1,3},{3,1},... | collective-permute-start | bytes 1572872 | tf_op jit(solution)/shard_map/ppermute | solution.py:241
  62.7 1.4 %collective-permute-start.17 = (f32[16,512]{1,0:T(8,128)S(1)}, f32[16,512]{1,0:T(8,128)S(1)}, u32[]{:S(2)}, u32[]{:S(2)}) collective-permute-start(f32[16,512]{1,0:T(8,128)S(1)} %slice.172), channel_id=1, source_target_pairs={{0,2},{2,0},{4,6},{6,4},{8,10},{10,8},{12,14},{14,12},{1,3},{3,1},... | collective-permute-start | bytes 98312 | tf_op jit(solution)/shard_map/ppermute | solution.py:241
  64.1 4.7 %collective-permute-start.18 = (f32[16,256]{1,0:T(8,128)S(1)}, f32[16,256]{1,0:T(8,128)S(1)}, u32[]{:S(2)}, u32[]{:S(2)}) collective-permute-start(f32[16,256]{1,0:T(8,128)S(1)} %get-tuple-element.71), channel_id=1, source_target_pairs={{0,17},{1,16},{16,1},{17,0},{2,19},{3,18},{18,3},{19,2},{4,21},{5,... | collective-permute-start | bytes 49160 | tf_op jit(solution)/shard_map/ppermute | solution.py:339
  65.7 3.7 %collective-permute-start.19 = (f32[16,256]{1,0:T(8,128)S(1)}, f32[16,256]{1,0:T(8,128)S(1)}, u32[]{:S(2)}, u32[]{:S(2)}) collective-permute-start(f32[16,256]{1,0:T(8,128)S(1)} %get-tuple-element.71), channel_id=1, source_target_pairs={{0,16},{16,0},{1,17},{17,1},{2,18},{18,2},{3,19},{19,3},{4,20},{20... | collective-permute-start | bytes 49160 | tf_op jit(solution)/shard_map/ppermute | solution.py:244
  66.2 3.7 %collective-permute-start.20 = (f32[16,256]{1,0:T(8,128)S(1)}, f32[16,256]{1,0:T(8,128)S(1)}, u32[]{:S(2)}, u32[]{:S(2)}) collective-permute-start(f32[16,256]{1,0:T(8,128)S(1)} %get-tuple-element.72.refs_10_), channel_id=1, source_target_pairs={{0,1},{1,0},{2,3},{3,2},{4,5},{5,4},{6,7},{7,6},{8,9},{9,8},{10,11... | collective-permute-start | bytes 49160 | tf_op jit(solution)/shard_map/ppermute | solution.py:341

commit v4 on v3

--- a/solution.py
+++ b/solution.py
@@ -13,22 +13,47 @@
 
 
 def sources(spots):
+    if spots == 4:
+        return np.array([[0, 1, 2, 3], [1, 0, 2, 3], [2, 3, 1, 0], [3, 2, 1, 0]], np.int32)
     table = []
     for half in range(spots):
         found = [half]
-        if spots == 4:
-            second = half - 2 if half >= 2 else half + 2
-            third = half - 3 if half >= 3 else half + 3
-            found += [1 if half == 0 else half - 1, second, half + 1 if half in (1, 2) else third]
-        else:
-            for step in range(1, spots):
-                up, down = half - step, half + step
-                if 2 * step > spots - 1:
-                    found.append(up if half >= step else down)
-                else:
-                    found += [up, down]
+        for step in range(1, spots):
+            up, down = half - step, half + step
+            if 2 * step > spots - 1:
+                found.append(up if half >= step else down)
+            else:
+                found += [up, down]
         table.append([f if 0 <= f < spots else -(2**16) for f in found])
     return np.array(table, np.int32)
+
+
+class FourLine:
+    def __init__(self, piece, half):
+        self.own, self.half = piece, half
+
+    def send(self, value, moves):
+        return lax.ppermute(value, "adapter", [(2 * s + c, 2 * d + c) for s, d in moves for c in range(2)])
+
+    def first(self):
+        self.end = self.send(self.own, [(0, 1), (1, 0), (2, 3), (3, 2)])
+        self.middle = self.send(self.own, [(1, 2), (2, 1)])
+
+    def second(self):
+        self.far_middle = self.send(self.end, [(1, 2), (2, 1)])
+        self.far_end = self.send(self.middle, [(1, 0), (2, 3)])
+
+    def third(self):
+        self.last = self.send(self.far_middle, [(1, 0), (2, 3)])
+
+    def pieces(self):
+        inner = (self.half == 1) | (self.half == 2)
+        return [
+            self.own,
+            self.end,
+            jnp.where(inner, self.middle, self.far_end),
+            jnp.where(inner, self.far_middle, self.last),
+        ]
 
 
 class Line:
@@ -57,12 +82,7 @@
             self.found += [self.up, self.down]
 
     def pieces(self):
-        if self.spots != 4:
-            return self.found
-        own, up, down, second, third = self.found
-        half = self.half
-        middle = (half == 1) | (half == 2)
-        return [own, jnp.where(half == 0, down, up), second, jnp.where(middle, down, third)]
+        return self.found
 
 
 def two_terms(value):
@@ -75,24 +95,59 @@
     return jnp.concatenate(two_terms(value), axis=1)
 
 
-def product_kernel(span, place_ref, tokens_ref, matrix_ref, out_ref):
-    columns = pl.ds(pl.multiple_of(place_ref[0] * span, LANES), span)
-    out_ref[...] = jnp.dot(
-        tokens_ref[...], matrix_ref[:, columns], preferred_element_type=jnp.float32
-    )
-
-
-def base_product(tokens, matrix, place, span):
-    vmem = pl.BlockSpec(memory_space=pltpu.VMEM)
+def product_kernel(span, pieces, place_ref, tokens_ref, matrix_ref, *refs):
+    out_refs, (tokens_here, matrix_here, token_sems, matrix_sems) = refs[:2], refs[2:]
+    depth = tokens_ref.shape[1] // pieces
+    parts = [pl.ds(k * depth, depth) for k in range(pieces)]
+    copies = [[], []]
+    for i in range(2):
+        columns = pl.ds(pl.multiple_of(place_ref[i] * span, LANES), span)
+        for k, part in enumerate(parts):
+            arriving = []
+            if i == 0:
+                arriving.append(
+                    pltpu.make_async_copy(
+                        tokens_ref.at[:, part], tokens_here.at[:, part], token_sems.at[k]
+                    )
+                )
+            arriving.append(
+                pltpu.make_async_copy(
+                    matrix_ref.at[part, columns], matrix_here.at[i, part], matrix_sems.at[i, k]
+                )
+            )
+            for copy in arriving:
+                copy.start()
+            copies[i].append(arriving)
+    for i, out_ref in enumerate(out_refs):
+        total = 0.0
+        for k, part in enumerate(parts):
+            for copy in copies[i][k]:
+                copy.wait()
+            total += jnp.dot(
+                tokens_here[:, part], matrix_here[i, part], preferred_element_type=jnp.float32
+            )
+        out_ref[...] = total
+
+
+def base_product(tokens, matrix, places, span):
+    rows, width = tokens.shape
+    pieces = 4
+    vmem, hbm = pl.BlockSpec(memory_space=pltpu.VMEM), pl.BlockSpec(memory_space=pltpu.HBM)
     return pl.pallas_call(
-        lambda *refs: product_kernel(span, *refs),
-        in_specs=[pl.BlockSpec(memory_space=pltpu.SMEM), vmem, vmem],
-        out_specs=vmem,
-        out_shape=jax.ShapeDtypeStruct((tokens.shape[0], span), jnp.float32),
-        compiler_params=pltpu.CompilerParams(vmem_limit_bytes=16 * 2**20),
+        lambda *refs: product_kernel(span, pieces, *refs),
+        in_specs=[pl.BlockSpec(memory_space=pltpu.SMEM), hbm, hbm],
+        out_specs=[vmem] * 2,
+        out_shape=[jax.ShapeDtypeStruct((rows, span), jnp.float32)] * 2,
+        scratch_shapes=[
+            pltpu.VMEM((rows, width), tokens.dtype),
+            pltpu.VMEM((2, width, span), matrix.dtype),
+            pltpu.SemaphoreType.DMA((pieces,)),
+            pltpu.SemaphoreType.DMA((2, pieces)),
+        ],
+        compiler_params=pltpu.CompilerParams(vmem_limit_bytes=52 * 2**20),
         cost_estimate=pl.CostEstimate(flops=0, bytes_accessed=0, transcendentals=0),
         name="base_product",
-    )(jnp.reshape(place, (1,)), tokens, matrix)
+    )(jnp.stack(places), tokens, matrix)
 
 
 PAD = 16
@@ -256,41 +311,51 @@
     half_expand = (half_expand * EXPAND_GAIN).astype(jnp.float16)
     blocks = [half_expand[:, i * LANES : (i + 1) * LANES] for i in range(span // LANES)]
     mine = jnp.concatenate([shrink_rows(shrink_later, c), *blocks], axis=0)
-    mine_line = Line(mine, spots, half)
-    mine_line.advance()
+    four = spots == 4
+    if four:
+        mine_line = FourLine(mine, half)
+        mine_line.first()
+    else:
+        mine_line = Line(mine, spots, half)
+        mine_line.advance()
 
     later, _ = barrier((tokens, mine))
     places = [2 * (1 - g) + 1 - c, 2 * (1 - g) + c, 2 * g + 1 - c]
     slot, sent, kept = pack(later, table, token_adapter_index[None, :], places, quarter)
     theirs = over_group(sent)
-    given_line = Line(given, spots, half)
-    given_line.advance()
-    came_own = over_core(kept)
+    if four:
+        given_line = FourLine(given, half)
+        given_line.first()
+    else:
+        given_line = Line(given, spots, half)
+        given_line.advance()
     came_theirs = over_core(theirs[: rows + PAD])
 
     source = jnp.asarray(sources(spots))[half]
     firsts = resident * (2 * source[:, None] + jnp.stack([c, 1 - c])[None, :]).reshape(-1)
-    if spots > 2:
-        mine_line.advance()
-        given_line.advance()
-
-    base_tokens, came_own, mine_line.up, mine_line.down = barrier(
-        (tokens, came_own, mine_line.up, mine_line.down)
-    )
+    base_tokens = tokens
+    if four:
+        mine_line.second()
+        given_line.second()
+        given_line.far_middle, base_tokens, kept = barrier((given_line.far_middle, tokens, kept))
+    came_own = over_core(kept)
+
     axes = ("tensor", "sub")
     if lax.axis_size("tensor") == 2 and lax.axis_size("sub") == 1:
         x = lax.axis_index("tensor")
-        away = base_product(base_tokens, value_matrix, 1 - x, span)
-        base_came = lax.ppermute(away, "tensor", swap)
-        base_tokens, _ = barrier((tokens, away))
-        bases = [base_product(base_tokens, value_matrix, x, span), base_came]
+        away, own_base = base_product(base_tokens, value_matrix, [1 - x, x], span)
+        bases = [own_base, lax.ppermute(away, "tensor", swap)]
     else:
         partial = jnp.dot(base_tokens, value_matrix, preferred_element_type=jnp.float32)
         bases = [lax.psum_scatter(partial, axes, scatter_dimension=1, tiled=True)]
 
-    for _ in range(spots - 3):
-        mine_line.advance()
-        given_line.advance()
+    if four:
+        mine_line.third()
+        given_line.third()
+    else:
+        for _ in range(spots - 2):
+            mine_line.advance()
+            given_line.advance()
     mine_pieces, given_pieces = mine_line.pieces(), given_line.pieces()
 
     column = (2 * g + c) * quarter
@@ -302,7 +367,7 @@
         return weights
 
     def products(operands, places, weights, start, sums):
-        which = list(range(2 * start, 2 * start + len(weights)))
+        which = list(range(start, start + len(weights)))
         return shrink_step(
             operands, places, weights, firsts, column, which, sums, rows, rank, resident
         )
@@ -318,18 +383,23 @@
     here_sum = there_sum = None
     for start in range(0, last, 3):
         weights = weights_of(start, min(start + 3, last))
-        here_sum = products(*here_parts, weights, start, [] if start == 0 else [here_sum])
-        there_sum = products(*there_parts, weights, start, [] if start == 0 else [there_sum])
-    expand_pieces = mine_pieces
-    if spots == 4:
-        mine_line.found[-1], given_line.found[-1], here_sum, there_sum = barrier(
-            (mine_line.found[-1], given_line.found[-1], here_sum, there_sum)
+        here_sum = products(*here_parts, weights, 2 * start, [] if start == 0 else [here_sum])
+        there_sum = products(*there_parts, weights, 2 * start, [] if start == 0 else [there_sum])
+    late_mine, late_given = mine_pieces, given_pieces
+    if four:
+        mine_line.last, given_line.last, here_sum, there_sum = barrier(
+            (mine_line.last, given_line.last, here_sum, there_sum)
         )
-        mine_pieces, given_pieces = mine_line.pieces(), given_line.pieces()
-    before = jnp.concatenate(
+        late_mine, late_given = mine_line.pieces(), given_line.pieces()
+    total = jnp.concatenate(
         [here_sum[:, :rows], there_sum[:, :rows], here_sum[:, rows:], there_sum[:, rows:]], axis=1
     )
-    total = products(*all_parts, weights_of(last, last + 1), last, [before])
+    total = products(*all_parts, [side_by_side(late_mine[last][:quarter])], 2 * last, [total])
+    if four:
+        given_line.last, total = barrier((given_line.last, total))
+        late_given = given_line.pieces()
+    almost = total
+    total = products(*all_parts, [side_by_side(late_given[last])], 2 * last + 1, [total])
     both_sum = total[:, : 2 * rows] + over_core(total[:, 2 * rows :])
     own_sum, other_sum = both_sum[:, :rows], both_sum[:, rows:]
     if len(bases) == 2:
@@ -347,8 +417,8 @@
         cut = piece[quarter:].reshape(span // LANES, held // 2, LANES)
         return jnp.concatenate([cut[i] for i in range(span // LANES)], axis=1)
 
-    here = jnp.concatenate([expand_of(piece) for piece in expand_pieces], axis=0)
-    across = over_group(here)
+    here = jnp.concatenate([expand_of(piece) for piece in mine_pieces], axis=0)
+    across, _ = barrier((over_group(here), almost))
     beside = over_core(jnp.concatenate([here, across], axis=0))
     terms = [two_terms(here), two_terms(across), two_terms(beside)]
     steps = jnp.arange(resident // 2, dtype=jnp.int32)

time: 73.4 us -> 67.6 us (0.921); the launches traced: 72.2 us -> 67.2 us
  local copies, waits for them, and re-layouts: 7.22 us -> 0.46 us
  starting transfers between devices: 28.2 us -> 21.9 us
  Pallas kernels: 15 us -> 19.5 us
  waiting for transfers between devices: 14.9 us -> 16.8 us
  other arithmetic: 6.16 us -> 7.93 us
    unnamed x16 -> x12, local copies, waits for them, and re-layouts: 6.87 us -> 0.11 us
    ppermute x10, starting transfers between devices: 18.7 us -> 13.4 us  [send(): lax.ppermute(value, 'adapter', [(2 * s + c, 2 * d + c) for s, d in moves...]
    pallas_call x2 -> x1, Pallas kernels: 2.53 us -> 6.23 us  [base_product(): pl.pallas_call(lambda *refs: product_kernel(span, pieces, *refs), in_spec...]
    ppermute x10, waiting for transfers between devices: 10.1 us -> 13.3 us  [send(): lax.ppermute(value, 'adapter', [(2 * s + c, 2 * d + c) for s, d in moves...]
    unnamed x4, other arithmetic: 0.1 us -> 1.96 us
    ppermute x3, starting transfers between devices: 3.63 us -> 2.6 us  [over_group(): return lax.ppermute(value, 'group', swap)]
    ppermute x3, waiting for transfers between devices: 2.57 us -> 1.55 us  [over_group(): return lax.ppermute(value, 'group', swap)]
    ppermute x1, starting transfers between devices: 1.5 us -> 0.54 us  [per_device(): lax.ppermute(own_sum, 'tensor', swap)]
  transfers between devices with their start and end apart: 21 -> 21, of which waited for: 8 -> 8; matrix products, arithmetic and copies ran while one was open for 6% -> 11% of each run, Pallas kernels for 18% -> 26%
where the time goes in v4:
time: 67.6 us; the launch traced here: 67.2 us
  starting transfers between devices  21.9 us (32%)
  Pallas kernels  19.5 us (29%)
  waiting for transfers between devices  16.8 us (25%)
  other arithmetic  7.93 us (12%)
    ppermute x10, starting transfers between devices, send(): lax.ppermute(value, 'adapter', [(2 * s + c, 2 * d + c) for s, d in moves...  13.4 us
    ppermute x10, waiting for transfers between devices, send(): lax.ppermute(value, 'adapter', [(2 * s + c, 2 * d + c) for s, d in moves...  13.3 us
    pallas_call x4, Pallas kernels, shrink_step(): pl.pallas_call(lambda *refs: shrink_kernel(rank, resident, rows, which, p...  7.64 us
    pallas_call x1, Pallas kernels, base_product(): pl.pallas_call(lambda *refs: product_kernel(span, pieces, *refs), in_spec...  6.23 us
    pallas_call x1, Pallas kernels, pack(): pl.pallas_call(lambda *refs: pack_kernel(rows, *refs), grid_spec=pltpu.Pr...  3.36 us
    ppermute x3, starting transfers between devices, over_group(): return lax.ppermute(value, 'group', swap)  2.6 us
    ppermute x1, starting transfers between devices, per_device(): lax.ppermute(other_sum, ('group', 'tensor'), across)  2.51 us
    convert_element_type x13, other arithmetic, two_terms(): return (high.astype(jnp.bfloat16), (wide - high).astype(jnp.bfloat16))  2.33 us
  transfers between devices with their start and end apart: 21, of which 8 were waited for; matrix products, arithmetic and copies ran while one was open for 11% of the time, Pallas kernels for 26%

profile of v4, /device:TPU:0, one launch (start us, length us, event | category | flops | bytes accessed | tf_op | source)
XLA Modules:
  0.0 67.2 jit_solution(3096959540662170612)
XLA Ops:
  0.0 1.1 %multiply_convert_fusion.1 = f16[1024,128]{1,0:T(8,128)(2,1)S(1)} fusion(f32[4096,128]{1,0:T(8,128)} %param.11, s32[]{:T(128)S(6)} %select_n.54), kind=kLoop, calls=%fused_computation.42 | loop fusion | flops 262144 | bytes 786436 | tf_op jit(solution)/shard_map/convert_element_type | solution.py:303
  1.7 1.1 %reduce-precision_convert_fusion.9 = (bf16[1024,128]{1,0:T(8,128)(2,1)S(1)}, f16[1024,128]{1,0:T(8,128)(2,1)S(1)}) fusion(f32[4096,128]{1,0:T(8,128)} %param.11, s32[]{:T(128)S(6)} %select_n.55), kind=kLoop, calls=%fused_computation.20 | loop fusion | flops 655360 | bytes 1048580 | tf_op jit(solution)/shard_map/convert_element_type | solution.py:91
  2.9 0.6 constant_dynamic-update-slice_fusion.6
  3.6 0.7 %collective-permute-start.1 = (f16[1280,128]{1,0:T(8,128)(2,1)S(1)}, f16[1280,128]{1,0:T(8,128)(2,1)S(1)}, u32[]{:S(2)}, u32[]{:S(2)}) collective-permute-start(f16[1280,128]{1,0:T(8,128)(2,1)S(1)} %constant_dynamic-update-slice_fusion), channel_id=1, source_target_pairs={{4,8},{6,10},{8,4},{10,6},{5,9},{7,11},{9,5},{11,7},{20,24},{22,26... | collective-permute-start | bytes 983048 | tf_op jit(solution)/shard_map/ppermute | solution.py:36
  4.3 5.5 %collective-permute-start = (f16[1280,128]{1,0:T(8,128)(2,1)S(1)}, f16[1280,128]{1,0:T(8,128)(2,1)S(1)}, u32[]{:S(2)}, u32[]{:S(2)}) collective-permute-start(f16[1280,128]{1,0:T(8,128)(2,1)S(1)} %constant_dynamic-update-slice_fusion), channel_id=1, source_target_pairs={{0,4},{2,6},{4,0},{6,2},{8,12},{10,14},{12,8},{14,10},{1,5},{3,7},... | collective-permute-start | bytes 983048 | tf_op jit(solution)/shard_map/ppermute | solution.py:36
  9.7 0.7 pad_add_fusion.1.refs_0_
  10.4 3.4 %pack.1 = (s32[1,256]{1,0:T(1,128)}, bf16[544,1024]{1,0:T(8,128)(2,1)}, bf16[272,1024]{1,0:T(8,128)(2,1)}) custom-call(s32[3]{0:T(128)} %pad_add_fusion.1.refs_0_, s32[64]{0:T(128)} %refs_1_.1, s32[1,256]{1,0:T(1,128)} %bitcast.15, bf16[256,4096]{1,0:T(8,128)(2,1)} %refs_2_.7, bf16[256,4096]{1,0:T(8,128)(2,1)} %refs_2_.7, bf16[256,4096]{1,0:T(8,128)(2,1)} %refs_2_.7), custom_call_target="tpu_custom_call" | custom-call | tf_op jit(solution)/shard_map/pack/pallas_call | solution.py:183
  13.7 1.5 %collective-permute-start.13 = (bf16[544,1024]{1,0:T(8,128)(2,1)}, bf16[544,1024]{1,0:T(8,128)(2,1)S(1)}, u32[]{:S(2)}, u32[]{:S(2)}) collective-permute-start(bf16[544,1024]{1,0:T(8,128)(2,1)} %get-tuple-element.30), channel_id=1, source_target_pairs={{0,16},{16,0},{1,17},{17,1},{2,18},{18,2},{3,19},{19,3},{4,20},{20... | collective-permute-start | bytes 3342344 | tf_op jit(solution)/shard_map/ppermute | solution.py:299
  15.3 0.7 %fusion.12 = s32[4]{0:T(128)S(1)} fusion(s32[4,4]{1,0:T(4,128)} %constant.59.clone, s32[]{:T(128)S(6)} %select_n.52), kind=kLoop, calls=%fused_computation.68 | loop fusion | flops 4 | bytes 36 | tf_op jit(solution)/shard_map/mul | solution.py:427
  16.8 0.7 collective-permute-start.11
  17.9 0.7 %collective-permute-start.3 = (f16[1280,128]{1,0:T(8,128)(2,1)S(1)}, f16[1280,128]{1,0:T(8,128)(2,1)S(1)}, u32[]{:S(2)}, u32[]{:S(2)}) collective-permute-start(f16[1280,128]{1,0:T(8,128)(2,1)S(1)} %collective-permute-done), channel_id=1, source_target_pairs={{4,8},{6,10},{8,4},{10,6},{5,9},{7,11},{9,5},{11,7},{20,24},{22,26... | collective-permute-start | bytes 983048 | tf_op jit(solution)/shard_map/ppermute | solution.py:36
  18.6 1.3 %collective-permute-start.2 = (f16[1280,128]{1,0:T(8,128)(2,1)S(1)}, f16[1280,128]{1,0:T(8,128)(2,1)S(1)}, u32[]{:S(2)}, u32[]{:S(2)}) collective-permute-start(f16[1280,128]{1,0:T(8,128)(2,1)S(1)} %collective-permute-done.1), channel_id=1, source_target_pairs={{4,0},{6,2},{8,12},{10,14},{5,1},{7,3},{9,13},{11,15},{20,16},{22,... | collective-permute-start | bytes 983048 | tf_op jit(solution)/shard_map/ppermute | solution.py:36
  20.0 0.7 maximum_dynamic-update-slice_fusion.2
  20.6 1.3 %collective-permute-start.12 = (f16[1024,128]{1,0:T(8,128)(2,1)S(1)}, f16[1024,128]{1,0:T(8,128)(2,1)S(1)}, u32[]{:S(2)}, u32[]{:S(2)}) collective-permute-start(f16[1024,128]{1,0:T(8,128)(2,1)S(1)} %collective-permute-done.11), channel_id=1, source_target_pairs={{4,0},{6,2},{8,12},{10,14},{5,1},{7,3},{9,13},{11,15},{20,16},{22,... | collective-permute-start | bytes 786440 | tf_op jit(solution)/shard_map/ppermute | solution.py:36
  21.9 2.7 %collective-permute-done.7 = f16[1024,128]{1,0:T(8,128)(2,1)S(1)} collective-permute-done((f16[1024,128]{1,0:T(8,128)(2,1)S(1)}, f16[1024,128]{1,0:T(8,128)(2,1)S(1)}, u32[]{:S(2)}, u32[]{:S(2)}) %collective-permute-start.7) | collective-permute-done | bytes 262176 | tf_op jit(solution)/shard_map/ppermute | solution.py:36
  24.6 0.7 collective-permute-start.8
  25.4 9.5 %collective-permute-done.2 = f16[1280,128]{1,0:T(8,128)(2,1)S(1)} collective-permute-done((f16[1280,128]{1,0:T(8,128)(2,1)S(1)}, f16[1280,128]{1,0:T(8,128)(2,1)S(1)}, u32[]{:S(2)}, u32[]{:S(2)}) %collective-permute-start.2) | collective-permute-done | bytes 327712 | tf_op jit(solution)/shard_map/ppermute | solution.py:36
  35.1 1.3 %collective-permute-start.4 = (f16[1280,128]{1,0:T(8,128)(2,1)S(1)}, f16[1280,128]{1,0:T(8,128)(2,1)S(1)}, u32[]{:S(2)}, u32[]{:S(2)}) collective-permute-start(f16[1280,128]{1,0:T(8,128)(2,1)S(1)} %collective-permute-done.3), channel_id=1, source_target_pairs={{4,0},{6,2},{8,12},{10,14},{5,1},{7,3},{9,13},{11,15},{20,16},{22,... | collective-permute-start | bytes 983048 | tf_op jit(solution)/shard_map/ppermute | solution.py:36
  36.4 0.6 maximum_dynamic-update-slice_fusion.1
  37.3 1.3 %collective-permute-start.9 = (f16[1024,128]{1,0:T(8,128)(2,1)S(1)}, f16[1024,128]{1,0:T(8,128)(2,1)S(1)}, u32[]{:S(2)}, u32[]{:S(2)}) collective-permute-start(f16[1024,128]{1,0:T(8,128)(2,1)S(1)} %collective-permute-done.8), channel_id=1, source_target_pairs={{4,0},{6,2},{8,12},{10,14},{5,1},{7,3},{9,13},{11,15},{20,16},{22,... | collective-permute-start | bytes 786440 | tf_op jit(solution)/shard_map/ppermute | solution.py:36
  38.6 6.2 %base_product.1 = (f32[256,512]{1,0:T(8,128)S(1)}, f32[256,512]{1,0:T(8,128)S(1)}) custom-call(s32[2]{0:T(128)S(1)} %pad_add_fusion.2.refs_0_, bf16[256,4096]{1,0:T(8,128)(2,1)} %refs_2_.7, bf16[4096,1024]{1,0:T(8,128)(2,1)} %refs_2_.6), custom_call_target="tpu_custom_call" | custom-call | tf_op jit(solution)/shard_map/base_product/pallas_call | solution.py:136
  44.8 1.6 %collective-permute-start.16 = (f32[256,512]{1,0:T(8,128)S(1)}, f32[256,512]{1,0:T(8,128)S(1)}, u32[]{:S(2)}, u32[]{:S(2)}) collective-permute-start(f32[256,512]{1,0:T(8,128)S(1)} %get-tuple-element.39), channel_id=1, source_target_pairs={{0,1},{1,0},{2,3},{3,2},{4,5},{5,4},{6,7},{7,6},{8,9},{9,8},{10,11... | collective-permute-start | bytes 1572872 | tf_op jit(solution)/shard_map/ppermute | solution.py:347
  46.6 1.0 %collective-permute-done.4 = f16[1280,128]{1,0:T(8,128)(2,1)S(1)} collective-permute-done((f16[1280,128]{1,0:T(8,128)(2,1)S(1)}, f16[1280,128]{1,0:T(8,128)(2,1)S(1)}, u32[]{:S(2)}, u32[]{:S(2)}) %collective-permute-start.4) | collective-permute-done | bytes 327712 | tf_op jit(solution)/shard_map/ppermute | solution.py:36
  48.1 0.6 collective-permute-start.5
  48.7 2.5 %shrink_step.4 = f32[16,512]{1,0:T(8,128)S(1)} custom-call(s32[8]{0:T(128)S(1)} %mul.83.refs_0_, s32[1]{0:T(128)} %bitcast.10.refs_1_, bf16[256,4096]{1,0:T(8,128)(2,1)S(1)} %copy-done, s32[1,256]{1,0:T(1,128)S(1)} %copy-done.1, bf16[272,1024]{1,0:T(8,128)(2,1)S(1)} %collective-permute-done.10.refs_4_, ...), custom_call_target="tpu_custom_call" | custom-call | tf_op jit(solution)/shard_map/shrink_step/pallas_call | solution.py:229
  51.2 2.5 %shrink_step.5 = f32[16,512]{1,0:T(8,128)S(1)} custom-call(s32[8]{0:T(128)S(1)} %mul.83.refs_0_, s32[1]{0:T(128)} %bitcast.10.refs_1_, bf16[544,1024]{1,0:T(8,128)(2,1)S(1)} %collective-permute-done.13.refs_2_.refs_5_, bf16[272,1024]{1,0:T(8,128)(2,1)S(1)} %collective-permute-done.14.refs_3_.refs_6_, ...), custom_call_target="tpu_custom_call" | custom-call | tf_op jit(solution)/shard_map/shrink_step/pallas_call | solution.py:229
  53.9 1.4 %shrink_step.6.refs_8_ = f32[16,1024]{1,0:T(8,128)S(1)} custom-call(s32[8]{0:T(128)S(1)} %mul.83.refs_0_, s32[1]{0:T(128)} %bitcast.10.refs_1_, bf16[256,4096]{1,0:T(8,128)(2,1)S(1)} %copy-done, s32[1,256]{1,0:T(1,128)S(1)} %copy-done.1, bf16[272,1024]{1,0:T(8,128)(2,1)S(1)} %collective-permute-done.10.refs_4_, ...), custom_call_target="tpu_custom_call" | custom-call | tf_op jit(solution)/shard_map/shrink_step/pallas_call | solution.py:229
  55.5 1.4 %shrink_step.7 = f32[16,1024]{1,0:T(8,128)S(1)} custom-call(s32[8]{0:T(128)S(1)} %mul.83.refs_0_, s32[1]{0:T(128)} %bitcast.10.refs_1_, bf16[256,4096]{1,0:T(8,128)(2,1)S(1)} %copy-done, s32[1,256]{1,0:T(1,128)S(1)} %copy-done.1, bf16[272,1024]{1,0:T(8,128)(2,1)S(1)} %collective-permute-done.10.refs_4_, ...), custom_call_target="tpu_custom_call" | custom-call | tf_op jit(solution)/shard_map/shrink_step/pallas_call | solution.py:229
  58.1 2.5 %collective-permute-start.18 = (f32[16,256]{1,0:T(8,128)S(1)}, f32[16,256]{1,0:T(8,128)S(1)}, u32[]{:S(2)}, u32[]{:S(2)}) collective-permute-start(f32[16,256]{1,0:T(8,128)S(1)} %get-tuple-element.77), channel_id=1, source_target_pairs={{0,17},{1,16},{16,1},{17,0},{2,19},{3,18},{18,3},{19,2},{4,21},{5,... | collective-permute-start | bytes 49160 | tf_op jit(solution)/shard_map/ppermute | solution.py:409
  61.9 1.0 %collective-permute-done.18.refs_11_ = f32[16,256]{1,0:T(8,128)S(1)} collective-permute-done((f32[16,256]{1,0:T(8,128)S(1)}, f32[16,256]{1,0:T(8,128)S(1)}, u32[]{:S(2)}, u32[]{:S(2)}) %collective-permute-start.18) | collective-permute-done | bytes 16416 | tf_op jit(solution)/shard_map/ppermute | solution.py:409
  62.8 1.5 %collective-permute-done.19.refs_12_ = f32[16,256]{1,0:T(8,128)S(1)} collective-permute-done((f32[16,256]{1,0:T(8,128)S(1)}, f32[16,256]{1,0:T(8,128)S(1)}, u32[]{:S(2)}, u32[]{:S(2)}) %collective-permute-start.19) | collective-permute-done | bytes 16416 | tf_op jit(solution)/shard_map/ppermute | solution.py:299
  64.9 2.3 %expand_step.1 = bf16[256,512]{1,0:T(8,128)(2,1)} custom-call(s32[64]{0:T(128)S(1)} %add.115.refs_0_, s32[1,256]{1,0:T(1,128)S(1)} %copy-done.1, bf16[256,512]{1,0:T(8,128)(2,1)S(1)} %reduce-precision_convert_fusion.10.refs_2_, bf16[256,512]{1,0:T(8,128)(2,1)S(1)} %get-tuple-element.45.refs_3_, bf16[256,512]{1,0:T(8,128)(2,1)S(1)} %get-tuple-element.72.refs_4_, ...), custom_call_target="tpu_custom_call" | custom-call | tf_op jit(solution)/shard_map/expand_step/pallas_call | solution.py:270
  (77 shorter events, 6.5 us)
Async XLA Ops:
  0.0 2.8 %copy-start.2 = (f32[8,16,512]{2,1,0:T(8,128)S(1)}, f32[8,16,512]{2,1,0:T(8,128)}, u32[]{:S(2)}) copy-start(f32[8,16,512]{2,1,0:T(8,128)} %param.12) | copy-start | bytes 786436
  1.1 15.5 %collective-permute-start.6 = (f16[1024,128]{1,0:T(8,128)(2,1)S(1)}, f16[1024,128]{1,0:T(8,128)(2,1)S(1)}, u32[]{:S(2)}, u32[]{:S(2)}) collective-permute-start(f16[1024,128]{1,0:T(8,128)(2,1)S(1)} %multiply_convert_fusion.1), channel_id=1, source_target_pairs={{0,2},{2,0},{4,6},{6,4},{8,10},{10,8},{12,14},{14,12},{1,3},{3,1},... | collective-permute-start | bytes 786440 | tf_op jit(solution)/shard_map/ppermute | solution.py:296
  3.6 15.0 %collective-permute-start.1 = (f16[1280,128]{1,0:T(8,128)(2,1)S(1)}, f16[1280,128]{1,0:T(8,128)(2,1)S(1)}, u32[]{:S(2)}, u32[]{:S(2)}) collective-permute-start(f16[1280,128]{1,0:T(8,128)(2,1)S(1)} %constant_dynamic-update-slice_fusion), channel_id=1, source_target_pairs={{4,8},{6,10},{8,4},{10,6},{5,9},{7,11},{9,5},{11,7},{20,24},{22,26... | collective-permute-start | bytes 983048 | tf_op jit(solution)/shard_map/ppermute | solution.py:36
  4.3 13.5 %collective-permute-start = (f16[1280,128]{1,0:T(8,128)(2,1)S(1)}, f16[1280,128]{1,0:T(8,128)(2,1)S(1)}, u32[]{:S(2)}, u32[]{:S(2)}) collective-permute-start(f16[1280,128]{1,0:T(8,128)(2,1)S(1)} %constant_dynamic-update-slice_fusion), channel_id=1, source_target_pairs={{0,4},{2,6},{4,0},{6,2},{8,12},{10,14},{12,8},{14,10},{1,5},{3,7},... | collective-permute-start | bytes 983048 | tf_op jit(solution)/shard_map/ppermute | solution.py:36
  13.7 34.0 %collective-permute-start.13 = (bf16[544,1024]{1,0:T(8,128)(2,1)}, bf16[544,1024]{1,0:T(8,128)(2,1)S(1)}, u32[]{:S(2)}, u32[]{:S(2)}) collective-permute-start(bf16[544,1024]{1,0:T(8,128)(2,1)} %get-tuple-element.30), channel_id=1, source_target_pairs={{0,16},{16,0},{1,17},{17,1},{2,18},{18,2},{3,19},{19,3},{4,20},{20... | collective-permute-start | bytes 3342344 | tf_op jit(solution)/shard_map/ppermute | solution.py:299
  16.7 7.9 %collective-permute-start.7 = (f16[1024,128]{1,0:T(8,128)(2,1)S(1)}, f16[1024,128]{1,0:T(8,128)(2,1)S(1)}, u32[]{:S(2)}, u32[]{:S(2)}) collective-permute-start(f16[1024,128]{1,0:T(8,128)(2,1)S(1)} %collective-permute-done.6), channel_id=1, source_target_pairs={{0,4},{2,6},{4,0},{6,2},{8,12},{10,14},{12,8},{14,10},{1,5},{3,7},... | collective-permute-start | bytes 786440 | tf_op jit(solution)/shard_map/ppermute | solution.py:36
  16.8 3.9 %collective-permute-start.11 = (f16[1024,128]{1,0:T(8,128)(2,1)S(1)}, f16[1024,128]{1,0:T(8,128)(2,1)S(1)}, u32[]{:S(2)}, u32[]{:S(2)}) collective-permute-start(f16[1024,128]{1,0:T(8,128)(2,1)S(1)} %collective-permute-done.6), channel_id=1, source_target_pairs={{4,8},{6,10},{8,4},{10,6},{5,9},{7,11},{9,5},{11,7},{20,24},{22,26... | collective-permute-start | bytes 786440 | tf_op jit(solution)/shard_map/ppermute | solution.py:36
  17.9 17.2 %collective-permute-start.3 = (f16[1280,128]{1,0:T(8,128)(2,1)S(1)}, f16[1280,128]{1,0:T(8,128)(2,1)S(1)}, u32[]{:S(2)}, u32[]{:S(2)}) collective-permute-start(f16[1280,128]{1,0:T(8,128)(2,1)S(1)} %collective-permute-done), channel_id=1, source_target_pairs={{4,8},{6,10},{8,4},{10,6},{5,9},{7,11},{9,5},{11,7},{20,24},{22,26... | collective-permute-start | bytes 983048 | tf_op jit(solution)/shard_map/ppermute | solution.py:36
  18.6 16.3 %collective-permute-start.2 = (f16[1280,128]{1,0:T(8,128)(2,1)S(1)}, f16[1280,128]{1,0:T(8,128)(2,1)S(1)}, u32[]{:S(2)}, u32[]{:S(2)}) collective-permute-start(f16[1280,128]{1,0:T(8,128)(2,1)S(1)} %collective-permute-done.1), channel_id=1, source_target_pairs={{4,0},{6,2},{8,12},{10,14},{5,1},{7,3},{9,13},{11,15},{20,16},{22,... | collective-permute-start | bytes 983048 | tf_op jit(solution)/shard_map/ppermute | solution.py:36
  20.6 24.2 %collective-permute-start.12 = (f16[1024,128]{1,0:T(8,128)(2,1)S(1)}, f16[1024,128]{1,0:T(8,128)(2,1)S(1)}, u32[]{:S(2)}, u32[]{:S(2)}) collective-permute-start(f16[1024,128]{1,0:T(8,128)(2,1)S(1)} %collective-permute-done.11), channel_id=1, source_target_pairs={{4,0},{6,2},{8,12},{10,14},{5,1},{7,3},{9,13},{11,15},{20,16},{22,... | collective-permute-start | bytes 786440 | tf_op jit(solution)/shard_map/ppermute | solution.py:36
  24.6 12.6 %collective-permute-start.8 = (f16[1024,128]{1,0:T(8,128)(2,1)S(1)}, f16[1024,128]{1,0:T(8,128)(2,1)S(1)}, u32[]{:S(2)}, u32[]{:S(2)}) collective-permute-start(f16[1024,128]{1,0:T(8,128)(2,1)S(1)} %collective-permute-done.7), channel_id=1, source_target_pairs={{4,8},{6,10},{8,4},{10,6},{5,9},{7,11},{9,5},{11,7},{20,24},{22,26... | collective-permute-start | bytes 786440 | tf_op jit(solution)/shard_map/ppermute | solution.py:36
  35.1 12.5 %collective-permute-start.4 = (f16[1280,128]{1,0:T(8,128)(2,1)S(1)}, f16[1280,128]{1,0:T(8,128)(2,1)S(1)}, u32[]{:S(2)}, u32[]{:S(2)}) collective-permute-start(f16[1280,128]{1,0:T(8,128)(2,1)S(1)} %collective-permute-done.3), channel_id=1, source_target_pairs={{4,0},{6,2},{8,12},{10,14},{5,1},{7,3},{9,13},{11,15},{20,16},{22,... | collective-permute-start | bytes 983048 | tf_op jit(solution)/shard_map/ppermute | solution.py:36
  37.2 11.5 %collective-permute-start.10 = (bf16[272,1024]{1,0:T(8,128)(2,1)}, bf16[272,1024]{1,0:T(8,128)(2,1)S(1)}, u32[]{:S(2)}, u32[]{:S(2)}) collective-permute-start(bf16[272,1024]{1,0:T(8,128)(2,1)} %get-tuple-element.29), channel_id=1, source_target_pairs={{0,2},{2,0},{4,6},{6,4},{8,10},{10,8},{12,14},{14,12},{1,3},{3,1},... | collective-permute-start | bytes 1671176 | tf_op jit(solution)/shard_map/ppermute | solution.py:296
  37.3 16.4 %collective-permute-start.9 = (f16[1024,128]{1,0:T(8,128)(2,1)S(1)}, f16[1024,128]{1,0:T(8,128)(2,1)S(1)}, u32[]{:S(2)}, u32[]{:S(2)}) collective-permute-start(f16[1024,128]{1,0:T(8,128)(2,1)S(1)} %collective-permute-done.8), channel_id=1, source_target_pairs={{4,0},{6,2},{8,12},{10,14},{5,1},{7,3},{9,13},{11,15},{20,16},{22,... | collective-permute-start | bytes 786440 | tf_op jit(solution)/shard_map/ppermute | solution.py:36
  44.8 17.0 %collective-permute-start.16 = (f32[256,512]{1,0:T(8,128)S(1)}, f32[256,512]{1,0:T(8,128)S(1)}, u32[]{:S(2)}, u32[]{:S(2)}) collective-permute-start(f32[256,512]{1,0:T(8,128)S(1)} %get-tuple-element.39), channel_id=1, source_target_pairs={{0,1},{1,0},{2,3},{3,2},{4,5},{5,4},{6,7},{7,6},{8,9},{9,8},{10,11... | collective-permute-start | bytes 1572872 | tf_op jit(solution)/shard_map/ppermute | solution.py:347
  46.5 1.5 %copy-start.3 = (f16[512,512]{1,0:T(8,128)(2,1)S(1)}, f16[512,512]{1,0:T(8,128)(2,1)}, u32[]{:S(2)}) copy-start(f16[512,512]{1,0:T(8,128)(2,1)} %maximum_dynamic-update-slice_fusion.1) | copy-start | bytes 1572868
  46.6 2.1 %copy-start = (bf16[256,4096]{1,0:T(8,128)(2,1)S(1)}, bf16[256,4096]{1,0:T(8,128)(2,1)}, u32[]{:S(2)}) copy-start(bf16[256,4096]{1,0:T(8,128)(2,1)} %refs_2_.7) | copy-start | bytes 6291460
  46.6 2.1 %copy-start.1 = (s32[1,256]{1,0:T(1,128)S(1)}, s32[1,256]{1,0:T(1,128)}, u32[]{:S(2)}) copy-start(s32[1,256]{1,0:T(1,128)} %get-tuple-element.26.refs_3_.refs_1_) | copy-start | bytes 3076
  47.8 3.4 %collective-permute-start.14 = (bf16[272,1024]{1,0:T(8,128)(2,1)S(1)}, bf16[272,1024]{1,0:T(8,128)(2,1)S(1)}, u32[]{:S(2)}, u32[]{:S(2)}) collective-permute-start(bf16[272,1024]{1,0:T(8,128)(2,1)S(1)} %slice.168), channel_id=1, source_target_pairs={{0,2},{2,0},{4,6},{6,4},{8,10},{10,8},{12,14},{14,12},{1,3},{3,1},... | collective-permute-start | bytes 1671176 | tf_op jit(solution)/shard_map/ppermute | solution.py:296
  48.1 9.0 %collective-permute-start.5 = (f16[256,512]{1,0:T(8,128)(2,1)S(1)}, f16[256,512]{1,0:T(8,128)(2,1)S(1)}, u32[]{:S(2)}, u32[]{:S(2)}) collective-permute-start(f16[256,512]{1,0:T(8,128)(2,1)S(1)} %get-tuple-element.46), channel_id=1, source_target_pairs={{0,16},{16,0},{1,17},{17,1},{2,18},{18,2},{3,19},{19,3},{4,20},{20... | collective-permute-start | bytes 786440 | tf_op jit(solution)/shard_map/ppermute | solution.py:299
  56.8 1.3 %collective-permute-start.17 = (f32[16,512]{1,0:T(8,128)S(1)}, f32[16,512]{1,0:T(8,128)S(1)}, u32[]{:S(2)}, u32[]{:S(2)}) collective-permute-start(f32[16,512]{1,0:T(8,128)S(1)} %slice.172), channel_id=1, source_target_pairs={{0,2},{2,0},{4,6},{6,4},{8,10},{10,8},{12,14},{14,12},{1,3},{3,1},... | collective-permute-start | bytes 98312 | tf_op jit(solution)/shard_map/ppermute | solution.py:296
  57.2 4.5 %collective-permute-start.15 = (f16[512,512]{1,0:T(8,128)(2,1)S(1)}, f16[512,512]{1,0:T(8,128)(2,1)S(1)}, u32[]{:S(2)}, u32[]{:S(2)}) collective-permute-start(f16[512,512]{1,0:T(8,128)(2,1)S(1)} %constant_dynamic-update-slice_fusion.5), channel_id=1, source_target_pairs={{0,2},{2,0},{4,6},{6,4},{8,10},{10,8},{12,14},{14,12},{1,3},{3,1},... | collective-permute-start | bytes 1572872 | tf_op jit(solution)/shard_map/ppermute | solution.py:296
  58.1 4.7 %collective-permute-start.18 = (f32[16,256]{1,0:T(8,128)S(1)}, f32[16,256]{1,0:T(8,128)S(1)}, u32[]{:S(2)}, u32[]{:S(2)}) collective-permute-start(f32[16,256]{1,0:T(8,128)S(1)} %get-tuple-element.77), channel_id=1, source_target_pairs={{0,17},{1,16},{16,1},{17,0},{2,19},{3,18},{18,3},{19,2},{4,21},{5,... | collective-permute-start | bytes 49160 | tf_op jit(solution)/shard_map/ppermute | solution.py:409
  60.6 3.7 %collective-permute-start.19 = (f32[16,256]{1,0:T(8,128)S(1)}, f32[16,256]{1,0:T(8,128)S(1)}, u32[]{:S(2)}, u32[]{:S(2)}) collective-permute-start(f32[16,256]{1,0:T(8,128)S(1)} %get-tuple-element.77), channel_id=1, source_target_pairs={{0,16},{16,0},{1,17},{17,1},{2,18},{18,2},{3,19},{19,3},{4,20},{20... | collective-permute-start | bytes 49160 | tf_op jit(solution)/shard_map/ppermute | solution.py:299
  61.1 3.7 %collective-permute-start.20 = (f32[16,256]{1,0:T(8,128)S(1)}, f32[16,256]{1,0:T(8,128)S(1)}, u32[]{:S(2)}, u32[]{:S(2)}) collective-permute-start(f32[16,256]{1,0:T(8,128)S(1)} %get-tuple-element.78.refs_10_), channel_id=1, source_target_pairs={{0,1},{1,0},{2,3},{3,2},{4,5},{5,4},{6,7},{7,6},{8,9},{9,8},{10,11... | collective-permute-start | bytes 49160 | tf_op jit(solution)/shard_map/ppermute | solution.py:411

commit v5 on v4

--- a/solution.py
+++ b/solution.py
@@ -96,11 +96,11 @@
 
 
 def product_kernel(span, pieces, place_ref, tokens_ref, matrix_ref, *refs):
-    out_refs, (tokens_here, matrix_here, token_sems, matrix_sems) = refs[:2], refs[2:]
+    out_refs, (tokens_here, matrix_here, token_sems, matrix_sems) = refs[:-4], refs[-4:]
     depth = tokens_ref.shape[1] // pieces
     parts = [pl.ds(k * depth, depth) for k in range(pieces)]
-    copies = [[], []]
-    for i in range(2):
+    copies = [[] for _ in out_refs]
+    for i in range(len(out_refs)):
         columns = pl.ds(pl.multiple_of(place_ref[i] * span, LANES), span)
         for k, part in enumerate(parts):
             arriving = []
@@ -136,13 +136,13 @@
     return pl.pallas_call(
         lambda *refs: product_kernel(span, pieces, *refs),
         in_specs=[pl.BlockSpec(memory_space=pltpu.SMEM), hbm, hbm],
-        out_specs=[vmem] * 2,
-        out_shape=[jax.ShapeDtypeStruct((rows, span), jnp.float32)] * 2,
+        out_specs=[vmem] * len(places),
+        out_shape=[jax.ShapeDtypeStruct((rows, span), jnp.float32)] * len(places),
         scratch_shapes=[
             pltpu.VMEM((rows, width), tokens.dtype),
-            pltpu.VMEM((2, width, span), matrix.dtype),
+            pltpu.VMEM((len(places), width, span), matrix.dtype),
             pltpu.SemaphoreType.DMA((pieces,)),
-            pltpu.SemaphoreType.DMA((2, pieces)),
+            pltpu.SemaphoreType.DMA((len(places), pieces)),
         ],
         compiler_params=pltpu.CompilerParams(vmem_limit_bytes=52 * 2**20),
         cost_estimate=pl.CostEstimate(flops=0, bytes_accessed=0, transcendentals=0),
@@ -198,39 +198,68 @@
     )(jnp.stack(places), table, index, tokens, tokens, tokens)
 
 
-def shrink_kernel(rank, resident, rows, which, places, sums, first_ref, column_ref, *refs):
-    weights = refs[-1 - sums - len(which) : len(refs) - 1 - sums]
-    out_ref = refs[-1]
+def shrink_kernel(rank, resident, rows, which, places, mode, first_ref, column_ref, *refs):
     held = rank * resident
+    count = 1 + max(max(p[0], p[2] or 0) for p in places)
+    operands, refs = refs[:count], refs[count:]
+    weights, refs = refs[: len(which)], refs[len(which) :]
     quarter = weights[0].shape[0]
+    group = lax.broadcasted_iota(jnp.int32, (1, held), 1) // rank
+
+    def rows_of(arrays, part):
+        per = arrays[0].shape[0] // rows
+        return arrays[part // per][part % per * rows : (part % per + 1) * rows]
+
+    if mode:
+        outs = refs[-mode:]
+        inputs = refs[:-mode]
+        slot_rows = inputs[-(len(places) // 2) :]
+        sums = inputs[: -(len(places) // 2)]
     for part, (operand, row, slots) in enumerate(places):
-        columns = slice(part * rows, (part + 1) * rows)
         if slots is None:
-            tokens = refs[operand][row : row + rows]
-            slot = refs[operand][row + rows : row + rows + PAD, :rows]
-            slot = slot.astype(jnp.float32)[:1].astype(jnp.int32)
+            tokens = operands[operand][row : row + rows]
         else:
-            tokens = refs[operand][:, pl.ds(pl.multiple_of(column_ref[0], quarter), quarter)]
-            slot = refs[slots][...]
-        total = refs[-2][:, columns] if sums else jnp.zeros((rank, rows), jnp.float32)
+            tokens = operands[operand][:, pl.ds(pl.multiple_of(column_ref[0], quarter), quarter)]
+        if mode:
+            slot = rows_of(slot_rows, part)
+            total = rows_of(sums, part)
+        else:
+            if slots is None:
+                slot = operands[operand][row + rows : row + rows + PAD, :rows].astype(jnp.float32)[:1]
+            else:
+                slot = operands[slots][...].astype(jnp.float32)
+            slot = jnp.transpose(jnp.broadcast_to(slot, (held, rows))).astype(jnp.int32)
+            refs[1][part * rows : (part + 1) * rows] = slot
+            total = jnp.zeros((rows, held), jnp.float32)
         for w, side in zip(weights, which):
             product = jnp.dot(tokens, w[...], preferred_element_type=jnp.float32)
-            product = jnp.transpose(product[:, :held] + product[:, held:])
-            for j in range(resident):
-                chosen = slot == first_ref[side] + j
-                total += jnp.where(chosen, product[j * rank : (j + 1) * rank], 0.0)
-        out_ref[:, columns] = total
-
-
-def shrink_step(operands, places, weights, firsts, column, which, sums, rows, rank, resident):
+            chosen = slot == first_ref[side] + group
+            total = jnp.where(chosen, product[:, :held] + product[:, held:], total)
+        if mode < 2:
+            out_ref = outs[0] if mode else refs[0]
+            out_ref[part * rows : (part + 1) * rows] = total
+        else:
+            total = jnp.transpose(total)
+            gathered = total[:rank]
+            for j in range(1, resident):
+                gathered += total[j * rank : (j + 1) * rank]
+            at = part // 2 * rows
+            outs[part % 2][:, at : at + rows] = gathered
+
+
+def shrink_step(operands, places, weights, firsts, column, which, sums, slots, mode, rows, rank, resident):
     vmem = pl.BlockSpec(memory_space=pltpu.VMEM)
     smem = pl.BlockSpec(memory_space=pltpu.SMEM)
-    operands = [*operands, *weights, *sums]
+    operands = [*operands, *weights, *sums, *slots]
+    count, held = len(places) * rows, rank * resident
+    wide = jax.ShapeDtypeStruct((count, held), jnp.float32)
+    narrow = jax.ShapeDtypeStruct((rank, count // 2), jnp.float32)
+    shapes = [[wide, jax.ShapeDtypeStruct((count, held), jnp.int32)], [wide], [narrow, narrow]][mode]
     return pl.pallas_call(
-        lambda *refs: shrink_kernel(rank, resident, rows, which, places, len(sums), *refs),
+        lambda *refs: shrink_kernel(rank, resident, rows, which, places, mode, *refs),
         in_specs=[smem, smem] + [vmem] * len(operands),
-        out_specs=vmem,
-        out_shape=jax.ShapeDtypeStruct((rank, len(places) * rows), jnp.float32),
+        out_specs=[vmem] * len(shapes),
+        out_shape=shapes,
         compiler_params=pltpu.CompilerParams(vmem_limit_bytes=16 * 2**20),
         cost_estimate=pl.CostEstimate(flops=0, bytes_accessed=0, transcendentals=0),
         name="shrink_step",
@@ -240,21 +269,28 @@
 def expand_kernel(rank, groups, scale, count, slots_ref, slot_ref, *refs):
     parts = refs[: 2 * len(groups)]
     bases, sums, out_ref = refs[2 * len(groups) : -1 - count], refs[-1 - count : -1], refs[-1]
-    shrunk = sum(ref[...] for ref in sums[1:]) + sums[0][...] if count > 1 else sums[0][...]
-    slot = slot_ref[...]
+    shrunk = sums[0][...]
+    for ref in sums[1:]:
+        shrunk += ref[...]
+    rows, held = out_ref.shape[0], slot_ref.shape[1]
+    shrunk = jnp.transpose(jnp.concatenate([shrunk] * (held // rank), axis=0))
+    slot = slot_ref[:rows]
     update = 0.0
     at = 0
-    for i, count in enumerate(groups):
+    for i, depth in enumerate(groups):
         spread = jnp.concatenate(
-            [jnp.where(slot == slots_ref[at + j], shrunk, 0.0) for j in range(count)], axis=0
+            [
+                jnp.where(slot[:, :lanes] == slots_ref[:, at + j : at + j + lanes], shrunk[:, :lanes], 0.0)
+                for j in range(0, depth, held)
+                for lanes in [min(held, depth - j)]
+            ],
+            axis=1,
         )
-        at += count
+        at += depth
         high = spread.astype(jnp.bfloat16)
         low = (spread - high.astype(jnp.float32)).astype(jnp.bfloat16)
         for left, right in ((high, parts[2 * i]), (low, parts[2 * i]), (high, parts[2 * i + 1])):
-            update += lax.dot_general(
-                left, right[...], (((0,), (0,)), ((), ())), preferred_element_type=jnp.float32
-            )
+            update += jnp.dot(left, right[...], preferred_element_type=jnp.float32)
     total = scale * update
     for base in bases:
         total += base[...]
@@ -262,21 +298,19 @@
 
 
 def expand_step(slots, slot, shrunk, parts, bases, rank, scale):
-    groups = [high.shape[0] // rank for high, _ in parts]
+    groups = [high.shape[0] for high, _ in parts]
     flat = [term for pair in parts for term in pair]
-    operands = [slot, *flat, *bases, *shrunk]
-    rows, span = bases[0].shape
-    depth = rank * sum(groups)
+    operands = [slots, slot, *flat, *bases, *shrunk]
+    vmem = pl.BlockSpec(memory_space=pltpu.VMEM)
     return pl.pallas_call(
         lambda *refs: expand_kernel(rank, groups, scale, len(shrunk), *refs),
-        in_specs=[pl.BlockSpec(memory_space=pltpu.SMEM)]
-        + [pl.BlockSpec(memory_space=pltpu.VMEM)] * len(operands),
-        out_specs=pl.BlockSpec(memory_space=pltpu.VMEM),
-        out_shape=jax.ShapeDtypeStruct((rows, span), jnp.bfloat16),
+        in_specs=[vmem] * len(operands),
+        out_specs=vmem,
+        out_shape=jax.ShapeDtypeStruct(bases[0].shape, jnp.bfloat16),
         compiler_params=pltpu.CompilerParams(vmem_limit_bytes=16 * 2**20),
         cost_estimate=pl.CostEstimate(flops=0, bytes_accessed=0, transcendentals=0),
         name="expand_step",
-    )(slots, *operands)
+    )(*operands)
 
 
 def per_device(tokens, token_adapter_index, table, value_matrix, shrink_weight, expand_weight):
@@ -302,15 +336,12 @@
         rows_there = lax.dynamic_slice_in_dim(weight, (2 * g + side) * quarter, quarter, 0)
         return (rows_there * SHRINK_GAIN).astype(jnp.float16)
 
-    give = shrink_rows(shrink_weight, 1 - c)
-    given = over_core(give)
-    shrink_later, expand_later, _ = barrier((shrink_weight, expand_weight, give))
     half_expand = lax.dynamic_slice_in_dim(
-        expand_later.reshape(held, span), g * (held // 2), held // 2, 0
+        expand_weight.reshape(held, span), g * (held // 2), held // 2, 0
     )
     half_expand = (half_expand * EXPAND_GAIN).astype(jnp.float16)
     blocks = [half_expand[:, i * LANES : (i + 1) * LANES] for i in range(span // LANES)]
-    mine = jnp.concatenate([shrink_rows(shrink_later, c), *blocks], axis=0)
+    mine = jnp.concatenate([shrink_rows(shrink_weight, c), *blocks], axis=0)
     four = spots == 4
     if four:
         mine_line = FourLine(mine, half)
@@ -319,35 +350,48 @@
         mine_line = Line(mine, spots, half)
         mine_line.advance()
 
-    later, _ = barrier((tokens, mine))
-    places = [2 * (1 - g) + 1 - c, 2 * (1 - g) + c, 2 * g + 1 - c]
-    slot, sent, kept = pack(later, table, token_adapter_index[None, :], places, quarter)
-    theirs = over_group(sent)
+    later_weight, _ = barrier((shrink_weight, mine))
+    given = over_core(shrink_rows(later_weight, 1 - c))
     if four:
         given_line = FourLine(given, half)
         given_line.first()
     else:
         given_line = Line(given, spots, half)
         given_line.advance()
+
+    later, _ = barrier((tokens, given))
+    places = [2 * (1 - g) + 1 - c, 2 * (1 - g) + c, 2 * g + 1 - c]
+    slot, sent, kept = pack(later, table, token_adapter_index[None, :], places, quarter)
+    theirs = over_group(sent)
     came_theirs = over_core(theirs[: rows + PAD])
 
     source = jnp.asarray(sources(spots))[half]
     firsts = resident * (2 * source[:, None] + jnp.stack([c, 1 - c])[None, :]).reshape(-1)
-    base_tokens = tokens
-    if four:
+    axes = ("tensor", "sub")
+    two = lax.axis_size("tensor") == 2 and lax.axis_size("sub") == 1
+    x = lax.axis_index("tensor")
+    if four and two:
+        tokens_1, mine_line.end, mine_line.middle = barrier((tokens, mine_line.end, mine_line.middle))
         mine_line.second()
+        (away,) = base_product(tokens_1, value_matrix, [1 - x], span)
+        given_line.end, given_line.middle, away = barrier((given_line.end, given_line.middle, away))
         given_line.second()
-        given_line.far_middle, base_tokens, kept = barrier((given_line.far_middle, tokens, kept))
-    came_own = over_core(kept)
-
-    axes = ("tensor", "sub")
-    if lax.axis_size("tensor") == 2 and lax.axis_size("sub") == 1:
-        x = lax.axis_index("tensor")
-        away, own_base = base_product(base_tokens, value_matrix, [1 - x, x], span)
+        tokens_2, _ = barrier((tokens, given_line.end))
+        (own_base,) = base_product(tokens_2, value_matrix, [x], span)
+        mine_line.far_middle, own_base = barrier((mine_line.far_middle, own_base))
+        mine_line.far_end, kept = barrier((mine_line.far_end, kept))
+        given_line.far_middle, away = barrier((given_line.far_middle, away))
+        bases = [own_base, lax.ppermute(away, "tensor", swap)]
+    elif two:
+        away, own_base = base_product(tokens, value_matrix, [1 - x, x], span)
         bases = [own_base, lax.ppermute(away, "tensor", swap)]
     else:
-        partial = jnp.dot(base_tokens, value_matrix, preferred_element_type=jnp.float32)
+        if four:
+            mine_line.second()
+            given_line.second()
+        partial = jnp.dot(tokens, value_matrix, preferred_element_type=jnp.float32)
         bases = [lax.psum_scatter(partial, axes, scatter_dimension=1, tiled=True)]
+    came_own = over_core(kept)
 
     if four:
         mine_line.third()
@@ -366,41 +410,43 @@
             weights += [side_by_side(mine_pieces[i][:quarter]), side_by_side(given_pieces[i])]
         return weights
 
-    def products(operands, places, weights, start, sums):
+    def products(operands, places, weights, start, sums=(), slots=(), mode=0):
         which = list(range(start, start + len(weights)))
         return shrink_step(
-            operands, places, weights, firsts, column, which, sums, rows, rank, resident
+            operands, places, weights, firsts, column, which, sums, slots, mode, rows, rank, resident
         )
 
     here_parts = ((tokens, slot, came_own), ((0, 0, 1), (2, 0, None)))
     there_parts = ((theirs, came_theirs), ((0, rows + PAD, None), (1, 0, None)))
     all_parts = (
         (tokens, slot, came_own, theirs, came_theirs),
-        ((0, 0, 1), (3, rows + PAD, None), (2, 0, None), (4, 0, None)),
+        ((0, 0, 1), (2, 0, None), (3, rows + PAD, None), (4, 0, None)),
     )
-
     last = len(mine_pieces) - 1
-    here_sum = there_sum = None
-    for start in range(0, last, 3):
-        weights = weights_of(start, min(start + 3, last))
-        here_sum = products(*here_parts, weights, 2 * start, [] if start == 0 else [here_sum])
-        there_sum = products(*there_parts, weights, 2 * start, [] if start == 0 else [there_sum])
+    some = min(3, last)
+    here_sum, here_slot = products(*here_parts, weights_of(0, some), 0)
+    there_sum, there_slot = products(*there_parts, weights_of(0, some), 0)
     late_mine, late_given = mine_pieces, given_pieces
     if four:
+        mine_line.last, here_sum = barrier((mine_line.last, here_sum))
+        mine_pieces = mine_line.pieces()
         mine_line.last, given_line.last, here_sum, there_sum = barrier(
             (mine_line.last, given_line.last, here_sum, there_sum)
         )
         late_mine, late_given = mine_line.pieces(), given_line.pieces()
-    total = jnp.concatenate(
-        [here_sum[:, :rows], there_sum[:, :rows], here_sum[:, rows:], there_sum[:, rows:]], axis=1
+    sums, slots_of = (here_sum, there_sum), (here_slot, there_slot)
+    for start in range(some, last, 3):
+        weights = weights_of(start, min(start + 3, last))
+        sums = products(*all_parts, weights, 2 * start, sums, slots_of, 1)
+    sums = products(*all_parts, [side_by_side(late_mine[last][:quarter])], 2 * last, sums, slots_of, 1)
+    (almost,) = sums
+    if four:
+        given_line.last, almost = barrier((given_line.last, almost))
+        late_given = given_line.pieces()
+    stays, leaves = products(
+        *all_parts, [side_by_side(late_given[last])], 2 * last + 1, (almost,), slots_of, 2
     )
-    total = products(*all_parts, [side_by_side(late_mine[last][:quarter])], 2 * last, [total])
-    if four:
-        given_line.last, total = barrier((given_line.last, total))
-        late_given = given_line.pieces()
-    almost = total
-    total = products(*all_parts, [side_by_side(late_given[last])], 2 * last + 1, [total])
-    both_sum = total[:, : 2 * rows] + over_core(total[:, 2 * rows :])
+    both_sum = stays + over_core(leaves)
     own_sum, other_sum = both_sum[:, :rows], both_sum[:, rows:]
     if len(bases) == 2:
         across = [(i, 3 - i) for i in range(4)]
@@ -418,16 +464,16 @@
         return jnp.concatenate([cut[i] for i in range(span // LANES)], axis=1)
 
     here = jnp.concatenate([expand_of(piece) for piece in mine_pieces], axis=0)
-    across, _ = barrier((over_group(here), almost))
+    across, _ = barrier((over_group(here), both_sum))
     beside = over_core(jnp.concatenate([here, across], axis=0))
     terms = [two_terms(here), two_terms(across), two_terms(beside)]
     steps = jnp.arange(resident // 2, dtype=jnp.int32)
     sides = jnp.stack([c, 1 - c])[:, None, None, None]
     halves = jnp.stack([g, 1 - g])[None, :, None, None] * (resident // 2)
     slots = (2 * source[:, None] + sides) * resident + halves + steps
-    slots = slots.astype(jnp.int32).reshape(-1)
+    slots = jnp.repeat(slots.astype(jnp.int32).reshape(1, -1), rank, axis=1)
     scale = SCALING / (SHRINK_GAIN * EXPAND_GAIN)
-    return expand_step(slots, slot, shrunk, terms, bases, rank, scale)
+    return expand_step(slots, here_slot, shrunk, terms, bases, rank, scale)
 
 
 def solution(mesh):

time: 67.6 us -> 66.2 us (0.979)
  starting transfers between devices: 21.9 us -> 23.1 us
  waiting for transfers between devices: 16.8 us -> 15.6 us
  other arithmetic: 7.93 us -> 6.82 us
    ppermute x10, waiting for transfers between devices: 13.3 us -> 10.4 us  [send(): lax.ppermute(value, 'adapter', [(2 * s + c, 2 * d + c) for s, d in moves...]
    ppermute x10, starting transfers between devices: 13.4 us -> 15.5 us  [send(): lax.ppermute(value, 'adapter', [(2 * s + c, 2 * d + c) for s, d in moves...]
    ppermute x5, waiting for transfers between devices: 0.51 us -> 2.23 us  [over_core(): return lax.ppermute(value, 'adapter', core_pairs)]
    ppermute x3, waiting for transfers between devices: 1.55 us -> 0.54 us  [over_group(): return lax.ppermute(value, 'group', swap)]
    ppermute x1, starting transfers between devices: 2.51 us -> 1.5 us  [per_device(): lax.ppermute(other_sum, ('group', 'tensor'), across)]
    ppermute x1, waiting for transfers between devices: 0.51 us -> 1.52 us  [per_device(): lax.ppermute(own_sum, 'tensor', swap)]
    ppermute x3, starting transfers between devices: 2.6 us -> 3.61 us  [over_group(): return lax.ppermute(value, 'group', swap)]
    unnamed x4, other arithmetic: 1.96 us -> 1 us
  transfers between devices with their start and end apart: 21 -> 21, of which waited for: 8 -> 10; matrix products, arithmetic and copies ran while one was open for 11% -> 8% of each run, Pallas kernels for 26% -> 26%
where the time goes in v5:
time: 66.2 us; the launch traced here: 65.7 us
  starting transfers between devices  23.1 us (35%)
  Pallas kernels  19.1 us (29%)
  waiting for transfers between devices  15.6 us (24%)
  other arithmetic  6.82 us (10%)
    ppermute x10, starting transfers between devices, send(): lax.ppermute(value, 'adapter', [(2 * s + c, 2 * d + c) for s, d in moves...  15.5 us
    ppermute x10, waiting for transfers between devices, send(): lax.ppermute(value, 'adapter', [(2 * s + c, 2 * d + c) for s, d in moves...  10.4 us
    pallas_call x4, Pallas kernels, shrink_step(): pl.pallas_call(lambda *refs: shrink_kernel(rank, resident, rows, which, p...  7.3 us
    pallas_call x2, Pallas kernels, base_product(): pl.pallas_call(lambda *refs: product_kernel(span, pieces, *refs), in_spec...  6.66 us
    ppermute x3, starting transfers between devices, over_group(): return lax.ppermute(value, 'group', swap)  3.61 us
    pallas_call x1, Pallas kernels, pack(): pl.pallas_call(lambda *refs: pack_kernel(rows, *refs), grid_spec=pltpu.Pr...  3.36 us
    convert_element_type x13, other arithmetic, two_terms(): return (high.astype(jnp.bfloat16), (wide - high).astype(jnp.bfloat16))  2.34 us
    ppermute x5, waiting for transfers between devices, over_core(): return lax.ppermute(value, 'adapter', core_pairs)  2.23 us
  transfers between devices with their start and end apart: 21, of which 10 were waited for; matrix products, arithmetic and copies ran while one was open for 8% of the time, Pallas kernels for 26%

profile of v5, /device:TPU:0, one launch (start us, length us, event | category | flops | bytes accessed | tf_op | source)
XLA Modules:
  0.0 65.7 jit_solution(1664122958523239377)
XLA Ops:
  0.0 1.1 %reduce-precision_convert_fusion.10 = (bf16[1024,128]{1,0:T(8,128)(2,1)S(1)}, f16[1024,128]{1,0:T(8,128)(2,1)S(1)}) fusion(f32[4096,128]{1,0:T(8,128)} %param.11, s32[]{:T(128)S(6)} %select_n.56), kind=kLoop, calls=%fused_computation.22 | loop fusion | flops 655360 | bytes 1048580 | tf_op jit(solution)/shard_map/convert_element_type | solution.py:91
  1.2 0.9 %constant_dynamic-update-slice_fusion.6 = (f16[512,512]{1,0:T(8,128)(2,1)S(1)}, f16[64,512]{1,0:T(8,128)(2,1)S(1)}) fusion(f32[128,512]{1,0:T(8,128)} %bitcast.14, s32[]{:T(128)S(6)} %select_n.57), kind=kLoop, calls=%fused_computation.59 | loop fusion | flops 65535 | bytes 262148
  2.2 3.1 %collective-permute-start.1 = (f16[1280,128]{1,0:T(8,128)(2,1)S(1)}, f16[1280,128]{1,0:T(8,128)(2,1)S(1)}, u32[]{:S(2)}, u32[]{:S(2)}) collective-permute-start(f16[1280,128]{1,0:T(8,128)(2,1)S(1)} %constant_dynamic-update-slice_fusion), channel_id=1, source_target_pairs={{0,4},{2,6},{4,0},{6,2},{8,12},{10,14},{12,8},{14,10},{1,5},{3,7},... | collective-permute-start | bytes 983048 | tf_op jit(solution)/shard_map/ppermute | solution.py:36
  5.3 0.7 %collective-permute-start.2 = (f16[1280,128]{1,0:T(8,128)(2,1)S(1)}, f16[1280,128]{1,0:T(8,128)(2,1)S(1)}, u32[]{:S(2)}, u32[]{:S(2)}) collective-permute-start(f16[1280,128]{1,0:T(8,128)(2,1)S(1)} %constant_dynamic-update-slice_fusion), channel_id=1, source_target_pairs={{4,8},{6,10},{8,4},{10,6},{5,9},{7,11},{9,5},{11,7},{20,24},{22,26... | collective-permute-start | bytes 983048 | tf_op jit(solution)/shard_map/ppermute | solution.py:36
  6.0 1.1 %multiply_convert_fusion = f16[1024,128]{1,0:T(8,128)(2,1)S(1)} fusion(f32[4096,128]{1,0:T(8,128)} %param.11, s32[]{:T(128)S(6)} %select_n.58), kind=kLoop, calls=%fused_computation.41 | loop fusion | flops 262144 | bytes 786436 | tf_op jit(solution)/shard_map/convert_element_type | solution.py:337
  7.2 0.7 %fusion.12 = s32[4]{0:T(128)S(1)} fusion(s32[4,4]{1,0:T(4,128)} %constant.59.clone, s32[]{:T(128)S(6)} %select_n.54), kind=kLoop, calls=%fused_computation.66 | loop fusion | flops 4 | bytes 36 | tf_op jit(solution)/shard_map/mul | solution.py:473
  9.3 3.4 %pack.1 = (s32[1,256]{1,0:T(1,128)}, bf16[544,1024]{1,0:T(8,128)(2,1)}, bf16[272,1024]{1,0:T(8,128)(2,1)}) custom-call(s32[3]{0:T(128)} %pad_add_fusion.1.refs_0_, s32[64]{0:T(128)} %refs_1_.1, s32[1,256]{1,0:T(1,128)} %bitcast.15, bf16[256,4096]{1,0:T(8,128)(2,1)} %refs_2_.9, bf16[256,4096]{1,0:T(8,128)(2,1)} %refs_2_.9, bf16[256,4096]{1,0:T(8,128)(2,1)} %refs_2_.9), custom_call_target="tpu_custom_call" | custom-call | tf_op jit(solution)/shard_map/pack/pallas_call | solution.py:183
  12.6 1.5 %collective-permute-start.11 = (bf16[544,1024]{1,0:T(8,128)(2,1)}, bf16[544,1024]{1,0:T(8,128)(2,1)S(1)}, u32[]{:S(2)}, u32[]{:S(2)}) collective-permute-start(bf16[544,1024]{1,0:T(8,128)(2,1)} %get-tuple-element.54), channel_id=1, source_target_pairs={{0,16},{16,0},{1,17},{17,1},{2,18},{18,2},{3,19},{19,3},{4,20},{20... | collective-permute-start | bytes 3342344 | tf_op jit(solution)/shard_map/ppermute | solution.py:333
  14.2 4.4 %collective-permute-start.5 = (f16[1024,128]{1,0:T(8,128)(2,1)S(1)}, f16[1024,128]{1,0:T(8,128)(2,1)S(1)}, u32[]{:S(2)}, u32[]{:S(2)}) collective-permute-start(f16[1024,128]{1,0:T(8,128)(2,1)S(1)} %collective-permute-done), channel_id=1, source_target_pairs={{0,4},{2,6},{4,0},{6,2},{8,12},{10,14},{12,8},{14,10},{1,5},{3,7},... | collective-permute-start | bytes 786440 | tf_op jit(solution)/shard_map/ppermute | solution.py:36
  19.5 0.7 %collective-permute-start.8 = (f16[1280,128]{1,0:T(8,128)(2,1)S(1)}, f16[1280,128]{1,0:T(8,128)(2,1)S(1)}, u32[]{:S(2)}, u32[]{:S(2)}) collective-permute-start(f16[1280,128]{1,0:T(8,128)(2,1)S(1)} %collective-permute-done.1), channel_id=1, source_target_pairs={{4,8},{6,10},{8,4},{10,6},{5,9},{7,11},{9,5},{11,7},{20,24},{22,26... | collective-permute-start | bytes 983048 | tf_op jit(solution)/shard_map/ppermute | solution.py:36
  20.2 1.3 %collective-permute-start.3 = (f16[1280,128]{1,0:T(8,128)(2,1)S(1)}, f16[1280,128]{1,0:T(8,128)(2,1)S(1)}, u32[]{:S(2)}, u32[]{:S(2)}) collective-permute-start(f16[1280,128]{1,0:T(8,128)(2,1)S(1)} %collective-permute-done.2), channel_id=1, source_target_pairs={{4,0},{6,2},{8,12},{10,14},{5,1},{7,3},{9,13},{11,15},{20,16},{22,... | collective-permute-start | bytes 983048 | tf_op jit(solution)/shard_map/ppermute | solution.py:36
  21.5 3.3 %base_product.2 = f32[256,512]{1,0:T(8,128)S(1)} custom-call(s32[1]{0:T(128)} %bitcast.11.refs_0_, bf16[256,4096]{1,0:T(8,128)(2,1)} %refs_2_.9, bf16[4096,1024]{1,0:T(8,128)(2,1)} %refs_2_.7), custom_call_target="tpu_custom_call" | custom-call | tf_op jit(solution)/shard_map/base_product/pallas_call | solution.py:136
  25.9 1.3 %collective-permute-start.7 = (f16[1024,128]{1,0:T(8,128)(2,1)S(1)}, f16[1024,128]{1,0:T(8,128)(2,1)S(1)}, u32[]{:S(2)}, u32[]{:S(2)}) collective-permute-start(f16[1024,128]{1,0:T(8,128)(2,1)S(1)} %collective-permute-done.6), channel_id=1, source_target_pairs={{4,0},{6,2},{8,12},{10,14},{5,1},{7,3},{9,13},{11,15},{20,16},{22,... | collective-permute-start | bytes 786440 | tf_op jit(solution)/shard_map/ppermute | solution.py:36
  27.2 3.3 %base_product.3.refs_8_ = f32[256,512]{1,0:T(8,128)S(1)} custom-call(s32[1]{0:T(128)} %bitcast.12.refs_0_, bf16[256,4096]{1,0:T(8,128)(2,1)} %refs_2_.9, bf16[4096,1024]{1,0:T(8,128)(2,1)} %refs_2_.7), custom_call_target="tpu_custom_call" | custom-call | tf_op jit(solution)/shard_map/base_product/pallas_call | solution.py:136
  30.7 2.9 %collective-permute-done.3 = f16[1280,128]{1,0:T(8,128)(2,1)S(1)} collective-permute-done((f16[1280,128]{1,0:T(8,128)(2,1)S(1)}, f16[1280,128]{1,0:T(8,128)(2,1)S(1)}, u32[]{:S(2)}, u32[]{:S(2)}) %collective-permute-start.3) | collective-permute-done | bytes 327712 | tf_op jit(solution)/shard_map/ppermute | solution.py:36
  34.0 1.4 %collective-permute-start.9 = (f16[1280,128]{1,0:T(8,128)(2,1)S(1)}, f16[1280,128]{1,0:T(8,128)(2,1)S(1)}, u32[]{:S(2)}, u32[]{:S(2)}) collective-permute-start(f16[1280,128]{1,0:T(8,128)(2,1)S(1)} %collective-permute-done.8), channel_id=1, source_target_pairs={{4,0},{6,2},{8,12},{10,14},{5,1},{7,3},{9,13},{11,15},{20,16},{22,... | collective-permute-start | bytes 983048 | tf_op jit(solution)/shard_map/ppermute | solution.py:36
  35.5 1.3 %collective-permute-start.14 = (f16[1024,128]{1,0:T(8,128)(2,1)S(1)}, f16[1024,128]{1,0:T(8,128)(2,1)S(1)}, u32[]{:S(2)}, u32[]{:S(2)}) collective-permute-start(f16[1024,128]{1,0:T(8,128)(2,1)S(1)} %collective-permute-done.13), channel_id=1, source_target_pairs={{4,0},{6,2},{8,12},{10,14},{5,1},{7,3},{9,13},{11,15},{20,16},{22,... | collective-permute-start | bytes 786440 | tf_op jit(solution)/shard_map/ppermute | solution.py:36
  36.8 2.3 %collective-permute-done.7 = f16[1024,128]{1,0:T(8,128)(2,1)S(1)} collective-permute-done((f16[1024,128]{1,0:T(8,128)(2,1)S(1)}, f16[1024,128]{1,0:T(8,128)(2,1)S(1)}, u32[]{:S(2)}, u32[]{:S(2)}) %collective-permute-start.7) | collective-permute-done | bytes 262176 | tf_op jit(solution)/shard_map/ppermute | solution.py:36
  39.0 1.5 %collective-permute-start.17 = (f32[256,512]{1,0:T(8,128)S(1)}, f32[256,512]{1,0:T(8,128)S(1)}, u32[]{:S(2)}, u32[]{:S(2)}) collective-permute-start(f32[256,512]{1,0:T(8,128)S(1)} %base_product.2), channel_id=1, source_target_pairs={{0,1},{1,0},{2,3},{3,2},{4,5},{5,4},{6,7},{7,6},{8,9},{9,8},{10,11... | collective-permute-start | bytes 1572872 | tf_op jit(solution)/shard_map/ppermute | solution.py:384
  40.8 2.4 %shrink_step.4 = (f32[512,128]{1,0:T(8,128)S(1)}, s32[512,128]{1,0:T(8,128)S(1)}) custom-call(s32[8]{0:T(128)S(1)} %mul.74.refs_0_, s32[1]{0:T(128)} %bitcast.5.refs_1_, bf16[256,4096]{1,0:T(8,128)(2,1)S(1)} %copy-done, s32[1,256]{1,0:T(1,128)S(1)} %copy-done.1, bf16[272,1024]{1,0:T(8,128)(2,1)S(1)} %collective-permute-done.4.refs_4_, ...), custom_call_target="tpu_custom_call" | custom-call | tf_op jit(solution)/shard_map/shrink_step/pallas_call | solution.py:258
  43.2 4.0 %collective-permute-done.9 = f16[1280,128]{1,0:T(8,128)(2,1)S(1)} collective-permute-done((f16[1280,128]{1,0:T(8,128)(2,1)S(1)}, f16[1280,128]{1,0:T(8,128)(2,1)S(1)}, u32[]{:S(2)}, u32[]{:S(2)}) %collective-permute-start.9) | collective-permute-done | bytes 327712 | tf_op jit(solution)/shard_map/ppermute | solution.py:36
  48.2 1.1 %collective-permute-done.12.refs_3_.refs_6_ = bf16[272,1024]{1,0:T(8,128)(2,1)S(1)} collective-permute-done((bf16[272,1024]{1,0:T(8,128)(2,1)S(1)}, bf16[272,1024]{1,0:T(8,128)(2,1)S(1)}, u32[]{:S(2)}, u32[]{:S(2)}) %collective-permute-start.12) | collective-permute-done | bytes 557088 | tf_op jit(solution)/shard_map/ppermute | solution.py:330
  49.2 2.3 %shrink_step.5 = (f32[512,128]{1,0:T(8,128)S(1)}, s32[512,128]{1,0:T(8,128)S(1)}) custom-call(s32[8]{0:T(128)S(1)} %mul.74.refs_0_, s32[1]{0:T(128)} %bitcast.5.refs_1_, bf16[544,1024]{1,0:T(8,128)(2,1)S(1)} %collective-permute-done.11.refs_2_.refs_5_, bf16[272,1024]{1,0:T(8,128)(2,1)S(1)} %collective-permute-done.12.refs_3_.refs_6_, ...), custom_call_target="tpu_custom_call" | custom-call | tf_op jit(solution)/shard_map/shrink_step/pallas_call | solution.py:258
  51.6 1.0 %collective-permute-done.14 = f16[1024,128]{1,0:T(8,128)(2,1)S(1)} collective-permute-done((f16[1024,128]{1,0:T(8,128)(2,1)S(1)}, f16[1024,128]{1,0:T(8,128)(2,1)S(1)}, u32[]{:S(2)}, u32[]{:S(2)}) %collective-permute-start.14) | collective-permute-done | bytes 262176 | tf_op jit(solution)/shard_map/ppermute | solution.py:36
  52.8 1.3 %shrink_step.6.refs_8_ = f32[1024,128]{1,0:T(8,128)S(1)} custom-call(s32[8]{0:T(128)S(1)} %mul.74.refs_0_, s32[1]{0:T(128)} %bitcast.5.refs_1_, bf16[256,4096]{1,0:T(8,128)(2,1)S(1)} %copy-done, s32[1,256]{1,0:T(1,128)S(1)} %copy-done.1, bf16[272,1024]{1,0:T(8,128)(2,1)S(1)} %collective-permute-done.4.refs_4_, ...), custom_call_target="tpu_custom_call" | custom-call | tf_op jit(solution)/shard_map/shrink_step/pallas_call | solution.py:258
  54.3 1.4 %shrink_step.7 = (f32[16,512]{1,0:T(8,128)S(1)}, f32[16,512]{1,0:T(8,128)S(1)}) custom-call(s32[8]{0:T(128)S(1)} %mul.74.refs_0_, s32[1]{0:T(128)} %bitcast.5.refs_1_, bf16[256,4096]{1,0:T(8,128)(2,1)S(1)} %copy-done, s32[1,256]{1,0:T(1,128)S(1)} %copy-done.1, bf16[272,1024]{1,0:T(8,128)(2,1)S(1)} %collective-permute-done.4.refs_4_, ...), custom_call_target="tpu_custom_call" | custom-call | tf_op jit(solution)/shard_map/shrink_step/pallas_call | solution.py:258
  55.7 1.2 %collective-permute-done.15 = f32[16,512]{1,0:T(8,128)S(1)} collective-permute-done((f32[16,512]{1,0:T(8,128)S(1)}, f32[16,512]{1,0:T(8,128)S(1)}, u32[]{:S(2)}, u32[]{:S(2)}) %collective-permute-start.15) | collective-permute-done | bytes 32800 | tf_op jit(solution)/shard_map/ppermute | solution.py:330
  57.2 1.5 %collective-permute-start.18 = (f32[16,256]{1,0:T(8,128)S(1)}, f32[16,256]{1,0:T(8,128)S(1)}, u32[]{:S(2)}, u32[]{:S(2)}) collective-permute-start(f32[16,256]{1,0:T(8,128)S(1)} %get-tuple-element.107), channel_id=1, source_target_pairs={{0,17},{1,16},{16,1},{17,0},{2,19},{3,18},{18,3},{19,2},{4,21},{5,... | collective-permute-start | bytes 49160 | tf_op jit(solution)/shard_map/ppermute | solution.py:455
  58.7 1.5 %collective-permute-start.19 = (f32[16,256]{1,0:T(8,128)S(1)}, f32[16,256]{1,0:T(8,128)S(1)}, u32[]{:S(2)}, u32[]{:S(2)}) collective-permute-start(f32[16,256]{1,0:T(8,128)S(1)} %get-tuple-element.107), channel_id=1, source_target_pairs={{0,16},{16,0},{1,17},{17,1},{2,18},{18,2},{3,19},{19,3},{4,20},{20... | collective-permute-start | bytes 49160 | tf_op jit(solution)/shard_map/ppermute | solution.py:333
  61.1 0.9 %collective-permute-done.18.refs_11_ = f32[16,256]{1,0:T(8,128)S(1)} collective-permute-done((f32[16,256]{1,0:T(8,128)S(1)}, f32[16,256]{1,0:T(8,128)S(1)}, u32[]{:S(2)}, u32[]{:S(2)}) %collective-permute-start.18) | collective-permute-done | bytes 16416 | tf_op jit(solution)/shard_map/ppermute | solution.py:455
  62.5 1.5 %collective-permute-done.20.refs_13_ = f32[16,256]{1,0:T(8,128)S(1)} collective-permute-done((f32[16,256]{1,0:T(8,128)S(1)}, f32[16,256]{1,0:T(8,128)S(1)}, u32[]{:S(2)}, u32[]{:S(2)}) %collective-permute-start.20) | collective-permute-done | bytes 16416 | tf_op jit(solution)/shard_map/ppermute | solution.py:457
  64.0 1.7 %expand_step.1 = bf16[256,512]{1,0:T(8,128)(2,1)} custom-call(s32[1,1024]{1,0:T(1,128)S(1)} %broadcast_in_dim.14.refs_0_, s32[512,128]{1,0:T(8,128)S(1)} %get-tuple-element.49.refs_10_.refs_9_.refs_1_, bf16[256,512]{1,0:T(8,128)(2,1)S(1)} %reduce-precision_convert_fusion.4.refs_2_, bf16[256,512]{1,0:T(8,128)(2,1)S(1)} %get-tuple-element.73.refs_3_, ...), custom_call_target="tpu_custom_call" | custom-call | tf_op jit(solution)/shard_map/expand_step/pallas_call | solution.py:305
  (72 shorter events, 7.4 us)
Async XLA Ops:
  2.2 17.2 %collective-permute-start.1 = (f16[1280,128]{1,0:T(8,128)(2,1)S(1)}, f16[1280,128]{1,0:T(8,128)(2,1)S(1)}, u32[]{:S(2)}, u32[]{:S(2)}) collective-permute-start(f16[1280,128]{1,0:T(8,128)(2,1)S(1)} %constant_dynamic-update-slice_fusion), channel_id=1, source_target_pairs={{0,4},{2,6},{4,0},{6,2},{8,12},{10,14},{12,8},{14,10},{1,5},{3,7},... | collective-permute-start | bytes 983048 | tf_op jit(solution)/shard_map/ppermute | solution.py:36
  5.3 14.2 %collective-permute-start.2 = (f16[1280,128]{1,0:T(8,128)(2,1)S(1)}, f16[1280,128]{1,0:T(8,128)(2,1)S(1)}, u32[]{:S(2)}, u32[]{:S(2)}) collective-permute-start(f16[1280,128]{1,0:T(8,128)(2,1)S(1)} %constant_dynamic-update-slice_fusion), channel_id=1, source_target_pairs={{4,8},{6,10},{8,4},{10,6},{5,9},{7,11},{9,5},{11,7},{20,24},{22,26... | collective-permute-start | bytes 983048 | tf_op jit(solution)/shard_map/ppermute | solution.py:36
  7.1 2.2 %collective-permute-start = (f16[1024,128]{1,0:T(8,128)(2,1)S(1)}, f16[1024,128]{1,0:T(8,128)(2,1)S(1)}, u32[]{:S(2)}, u32[]{:S(2)}) collective-permute-start(f16[1024,128]{1,0:T(8,128)(2,1)S(1)} %multiply_convert_fusion), channel_id=1, source_target_pairs={{0,2},{2,0},{4,6},{6,4},{8,10},{10,8},{12,14},{14,12},{1,3},{3,1},... | collective-permute-start | bytes 786440 | tf_op jit(solution)/shard_map/ppermute | solution.py:330
  12.6 34.5 %collective-permute-start.11 = (bf16[544,1024]{1,0:T(8,128)(2,1)}, bf16[544,1024]{1,0:T(8,128)(2,1)S(1)}, u32[]{:S(2)}, u32[]{:S(2)}) collective-permute-start(bf16[544,1024]{1,0:T(8,128)(2,1)} %get-tuple-element.54), channel_id=1, source_target_pairs={{0,16},{16,0},{1,17},{17,1},{2,18},{18,2},{3,19},{19,3},{4,20},{20... | collective-permute-start | bytes 3342344 | tf_op jit(solution)/shard_map/ppermute | solution.py:333
  14.2 11.0 %collective-permute-start.5 = (f16[1024,128]{1,0:T(8,128)(2,1)S(1)}, f16[1024,128]{1,0:T(8,128)(2,1)S(1)}, u32[]{:S(2)}, u32[]{:S(2)}) collective-permute-start(f16[1024,128]{1,0:T(8,128)(2,1)S(1)} %collective-permute-done), channel_id=1, source_target_pairs={{0,4},{2,6},{4,0},{6,2},{8,12},{10,14},{12,8},{14,10},{1,5},{3,7},... | collective-permute-start | bytes 786440 | tf_op jit(solution)/shard_map/ppermute | solution.py:36
  18.5 6.7 %collective-permute-start.6 = (f16[1024,128]{1,0:T(8,128)(2,1)S(1)}, f16[1024,128]{1,0:T(8,128)(2,1)S(1)}, u32[]{:S(2)}, u32[]{:S(2)}) collective-permute-start(f16[1024,128]{1,0:T(8,128)(2,1)S(1)} %collective-permute-done), channel_id=1, source_target_pairs={{4,8},{6,10},{8,4},{10,6},{5,9},{7,11},{9,5},{11,7},{20,24},{22,26... | collective-permute-start | bytes 786440 | tf_op jit(solution)/shard_map/ppermute | solution.py:36
  19.5 14.5 %collective-permute-start.8 = (f16[1280,128]{1,0:T(8,128)(2,1)S(1)}, f16[1280,128]{1,0:T(8,128)(2,1)S(1)}, u32[]{:S(2)}, u32[]{:S(2)}) collective-permute-start(f16[1280,128]{1,0:T(8,128)(2,1)S(1)} %collective-permute-done.1), channel_id=1, source_target_pairs={{4,8},{6,10},{8,4},{10,6},{5,9},{7,11},{9,5},{11,7},{20,24},{22,26... | collective-permute-start | bytes 983048 | tf_op jit(solution)/shard_map/ppermute | solution.py:36
  20.2 13.5 %collective-permute-start.3 = (f16[1280,128]{1,0:T(8,128)(2,1)S(1)}, f16[1280,128]{1,0:T(8,128)(2,1)S(1)}, u32[]{:S(2)}, u32[]{:S(2)}) collective-permute-start(f16[1280,128]{1,0:T(8,128)(2,1)S(1)} %collective-permute-done.2), channel_id=1, source_target_pairs={{4,0},{6,2},{8,12},{10,14},{5,1},{7,3},{9,13},{11,15},{20,16},{22,... | collective-permute-start | bytes 983048 | tf_op jit(solution)/shard_map/ppermute | solution.py:36
  25.2 10.3 %collective-permute-start.13 = (f16[1024,128]{1,0:T(8,128)(2,1)S(1)}, f16[1024,128]{1,0:T(8,128)(2,1)S(1)}, u32[]{:S(2)}, u32[]{:S(2)}) collective-permute-start(f16[1024,128]{1,0:T(8,128)(2,1)S(1)} %collective-permute-done.5), channel_id=1, source_target_pairs={{4,8},{6,10},{8,4},{10,6},{5,9},{7,11},{9,5},{11,7},{20,24},{22,26... | collective-permute-start | bytes 786440 | tf_op jit(solution)/shard_map/ppermute | solution.py:36
  25.9 13.2 %collective-permute-start.7 = (f16[1024,128]{1,0:T(8,128)(2,1)S(1)}, f16[1024,128]{1,0:T(8,128)(2,1)S(1)}, u32[]{:S(2)}, u32[]{:S(2)}) collective-permute-start(f16[1024,128]{1,0:T(8,128)(2,1)S(1)} %collective-permute-done.6), channel_id=1, source_target_pairs={{4,0},{6,2},{8,12},{10,14},{5,1},{7,3},{9,13},{11,15},{20,16},{22,... | collective-permute-start | bytes 786440 | tf_op jit(solution)/shard_map/ppermute | solution.py:36
  30.6 3.3 %copy-start.2 = (bf16[272,1024]{1,0:T(8,128)(2,1)S(1)}, bf16[272,1024]{1,0:T(8,128)(2,1)}, u32[]{:S(2)}) copy-start(bf16[272,1024]{1,0:T(8,128)(2,1)} %get-tuple-element.43) | copy-start | bytes 1671172
  33.8 7.1 %copy-start = (bf16[256,4096]{1,0:T(8,128)(2,1)S(1)}, bf16[256,4096]{1,0:T(8,128)(2,1)}, u32[]{:S(2)}) copy-start(bf16[256,4096]{1,0:T(8,128)(2,1)} %refs_2_.9) | copy-start | bytes 6291460
  33.8 7.1 %copy-start.1 = (s32[1,256]{1,0:T(1,128)S(1)}, s32[1,256]{1,0:T(1,128)}, u32[]{:S(2)}) copy-start(s32[1,256]{1,0:T(1,128)} %get-tuple-element.40.refs_3_) | copy-start | bytes 3076
  33.9 6.9 %collective-permute-start.4 = (bf16[272,1024]{1,0:T(8,128)(2,1)S(1)}, bf16[272,1024]{1,0:T(8,128)(2,1)S(1)}, u32[]{:S(2)}, u32[]{:S(2)}) collective-permute-start(bf16[272,1024]{1,0:T(8,128)(2,1)S(1)} %copy-done.2), channel_id=1, source_target_pairs={{0,2},{2,0},{4,6},{6,4},{8,10},{10,8},{12,14},{14,12},{1,3},{3,1},... | collective-permute-start | bytes 1671176 | tf_op jit(solution)/shard_map/ppermute | solution.py:330
  34.0 13.2 %collective-permute-start.9 = (f16[1280,128]{1,0:T(8,128)(2,1)S(1)}, f16[1280,128]{1,0:T(8,128)(2,1)S(1)}, u32[]{:S(2)}, u32[]{:S(2)}) collective-permute-start(f16[1280,128]{1,0:T(8,128)(2,1)S(1)} %collective-permute-done.8), channel_id=1, source_target_pairs={{4,0},{6,2},{8,12},{10,14},{5,1},{7,3},{9,13},{11,15},{20,16},{22,... | collective-permute-start | bytes 983048 | tf_op jit(solution)/shard_map/ppermute | solution.py:36
  35.5 17.1 %collective-permute-start.14 = (f16[1024,128]{1,0:T(8,128)(2,1)S(1)}, f16[1024,128]{1,0:T(8,128)(2,1)S(1)}, u32[]{:S(2)}, u32[]{:S(2)}) collective-permute-start(f16[1024,128]{1,0:T(8,128)(2,1)S(1)} %collective-permute-done.13), channel_id=1, source_target_pairs={{4,0},{6,2},{8,12},{10,14},{5,1},{7,3},{9,13},{11,15},{20,16},{22,... | collective-permute-start | bytes 786440 | tf_op jit(solution)/shard_map/ppermute | solution.py:36
  39.0 22.0 %collective-permute-start.17 = (f32[256,512]{1,0:T(8,128)S(1)}, f32[256,512]{1,0:T(8,128)S(1)}, u32[]{:S(2)}, u32[]{:S(2)}) collective-permute-start(f32[256,512]{1,0:T(8,128)S(1)} %base_product.2), channel_id=1, source_target_pairs={{0,1},{1,0},{2,3},{3,2},{4,5},{5,4},{6,7},{7,6},{8,9},{9,8},{10,11... | collective-permute-start | bytes 1572872 | tf_op jit(solution)/shard_map/ppermute | solution.py:384
  47.2 2.0 %collective-permute-start.12 = (bf16[272,1024]{1,0:T(8,128)(2,1)S(1)}, bf16[272,1024]{1,0:T(8,128)(2,1)S(1)}, u32[]{:S(2)}, u32[]{:S(2)}) collective-permute-start(bf16[272,1024]{1,0:T(8,128)(2,1)S(1)} %slice.141), channel_id=1, source_target_pairs={{0,2},{2,0},{4,6},{6,4},{8,10},{10,8},{12,14},{14,12},{1,3},{3,1},... | collective-permute-start | bytes 1671176 | tf_op jit(solution)/shard_map/ppermute | solution.py:330
  47.6 9.3 %collective-permute-start.10 = (f16[256,512]{1,0:T(8,128)(2,1)S(1)}, f16[256,512]{1,0:T(8,128)(2,1)S(1)}, u32[]{:S(2)}, u32[]{:S(2)}) collective-permute-start(f16[256,512]{1,0:T(8,128)(2,1)S(1)} %get-tuple-element.74), channel_id=1, source_target_pairs={{0,16},{16,0},{1,17},{17,1},{2,18},{18,2},{3,19},{19,3},{4,20},{20... | collective-permute-start | bytes 786440 | tf_op jit(solution)/shard_map/ppermute | solution.py:333
  55.6 1.3 %collective-permute-start.15 = (f32[16,512]{1,0:T(8,128)S(1)}, f32[16,512]{1,0:T(8,128)S(1)}, u32[]{:S(2)}, u32[]{:S(2)}) collective-permute-start(f32[16,512]{1,0:T(8,128)S(1)} %get-tuple-element.67), channel_id=1, source_target_pairs={{0,2},{2,0},{4,6},{6,4},{8,10},{10,8},{12,14},{14,12},{1,3},{3,1},... | collective-permute-start | bytes 98312 | tf_op jit(solution)/shard_map/ppermute | solution.py:330
  57.0 3.9 %collective-permute-start.16 = (f16[512,512]{1,0:T(8,128)(2,1)S(1)}, f16[512,512]{1,0:T(8,128)(2,1)S(1)}, u32[]{:S(2)}, u32[]{:S(2)}) collective-permute-start(f16[512,512]{1,0:T(8,128)(2,1)S(1)} %constant_dynamic-update-slice_fusion.5), channel_id=1, source_target_pairs={{0,2},{2,0},{4,6},{6,4},{8,10},{10,8},{12,14},{14,12},{1,3},{3,1},... | collective-permute-start | bytes 1572872 | tf_op jit(solution)/shard_map/ppermute | solution.py:330
  57.2 4.7 %collective-permute-start.18 = (f32[16,256]{1,0:T(8,128)S(1)}, f32[16,256]{1,0:T(8,128)S(1)}, u32[]{:S(2)}, u32[]{:S(2)}) collective-permute-start(f32[16,256]{1,0:T(8,128)S(1)} %get-tuple-element.107), channel_id=1, source_target_pairs={{0,17},{1,16},{16,1},{17,0},{2,19},{3,18},{18,3},{19,2},{4,21},{5,... | collective-permute-start | bytes 49160 | tf_op jit(solution)/shard_map/ppermute | solution.py:455
  58.7 3.7 %collective-permute-start.19 = (f32[16,256]{1,0:T(8,128)S(1)}, f32[16,256]{1,0:T(8,128)S(1)}, u32[]{:S(2)}, u32[]{:S(2)}) collective-permute-start(f32[16,256]{1,0:T(8,128)S(1)} %get-tuple-element.107), channel_id=1, source_target_pairs={{0,16},{16,0},{1,17},{17,1},{2,18},{18,2},{3,19},{19,3},{4,20},{20... | collective-permute-start | bytes 49160 | tf_op jit(solution)/shard_map/ppermute | solution.py:333
  60.3 3.7 %collective-permute-start.20 = (f32[16,256]{1,0:T(8,128)S(1)}, f32[16,256]{1,0:T(8,128)S(1)}, u32[]{:S(2)}, u32[]{:S(2)}) collective-permute-start(f32[16,256]{1,0:T(8,128)S(1)} %get-tuple-element.108.refs_10_), channel_id=1, source_target_pairs={{0,1},{1,0},{2,3},{3,2},{4,5},{5,4},{6,7},{7,6},{8,9},{9,8},{10,11... | collective-permute-start | bytes 49160 | tf_op jit(solution)/shard_map/ppermute | solution.py:457

commit v6 on v5

--- a/solution.py
+++ b/solution.py
@@ -150,52 +150,90 @@
     )(jnp.stack(places), tokens, matrix)
 
 
+def lay_out_kernel(shrink_at_ref, expand_at_ref, shrink_ref, expand_ref, out_ref, sems):
+    count = expand_ref.shape[0] // 2
+    blocks = expand_ref.shape[1] // LANES
+    quarter = out_ref.shape[0] - blocks * count
+    rows = pl.ds(pl.multiple_of(shrink_at_ref[0] * quarter, 8), quarter)
+    copies = [pltpu.make_async_copy(shrink_ref.at[rows], out_ref.at[pl.ds(0, quarter)], sems.at[0])]
+    held = pl.ds(pl.multiple_of(expand_at_ref[0] * count, 8), count)
+    for i in range(blocks):
+        copies.append(
+            pltpu.make_async_copy(
+                expand_ref.at[held, pl.ds(i * LANES, LANES)],
+                out_ref.at[pl.ds(quarter + i * count, count)],
+                sems.at[i + 1],
+            )
+        )
+    for copy in copies:
+        copy.start()
+    for copy in copies:
+        copy.wait()
+
+
+def lay_out(shrink, expand, shrink_at, expand_at, quarter):
+    held, span = expand.shape
+    smem, hbm = pl.BlockSpec(memory_space=pltpu.SMEM), pl.BlockSpec(memory_space=pltpu.HBM)
+    rows = quarter + held // 2 * (span // LANES)
+    return pl.pallas_call(
+        lay_out_kernel,
+        in_specs=[smem, smem, hbm, hbm],
+        out_specs=pl.BlockSpec(memory_space=pltpu.VMEM),
+        out_shape=jax.ShapeDtypeStruct((rows, LANES), jnp.float32),
+        scratch_shapes=[pltpu.SemaphoreType.DMA((span // LANES + 1,))],
+        compiler_params=pltpu.CompilerParams(vmem_limit_bytes=16 * 2**20),
+        cost_estimate=pl.CostEstimate(flops=0, bytes_accessed=0, transcendentals=0),
+        name="lay_out",
+    )(jnp.reshape(shrink_at, (1,)), jnp.reshape(expand_at, (1,)), shrink, expand)
+
+
 PAD = 16
 
 
-def pack_kernel(rows, place_ref, table_ref, index_ref, away_ref, *refs):
-    own_ref, core_ref, slot_ref, sent_ref, kept_ref = refs
+def pack_kernel(rows, quarter, *refs):
+    column_refs, (table_ref, index_ref, tokens_ref, slot_ref, sent_ref, kept_ref, sems) = refs[:3], refs[3:]
+    step = rows + PAD
+    places = ((sent_ref, 0), (sent_ref, step), (kept_ref, 0))
+    copies = []
+    for i, (out_ref, start) in enumerate(places):
+        column = pl.multiple_of(column_refs[i][0] * quarter, LANES)
+        copies.append(
+            pltpu.make_async_copy(
+                tokens_ref.at[:, pl.ds(column, quarter)], out_ref.at[pl.ds(start, rows)], sems.at[i]
+            )
+        )
+        copies[i].start()
     index = index_ref[...]
     slot = jnp.zeros_like(index)
     for j in range(table_ref.shape[0]):
         slot += jnp.where(index == j, table_ref[j], 0)
     slot_ref[...] = slot
     tail = jnp.broadcast_to(slot.astype(jnp.float32), (PAD, rows)).astype(sent_ref.dtype)
-    width = core_ref.shape[1]
-    step = rows + PAD
-    for source, out_ref, start in ((away_ref, sent_ref, 0), (own_ref, sent_ref, step), (core_ref, kept_ref, 0)):
-        out_ref[start : start + rows] = source[...]
+    for out_ref, start in places:
         out_ref[start + rows : start + step, :rows] = tail
-        if width > rows:
-            out_ref[start + rows : start + step, rows:] = jnp.zeros((PAD, width - rows), out_ref.dtype)
+        if quarter > rows:
+            out_ref[start + rows : start + step, rows:] = jnp.zeros((PAD, quarter - rows), out_ref.dtype)
+    for copy in copies:
+        copy.wait()
 
 
 def pack(tokens, table, index, places, quarter):
     rows = tokens.shape[0]
-
-    def column(i):
-        return pl.BlockSpec((rows, quarter), lambda _, place: (0, place[i]))
-
-    def whole(*shape):
-        return pl.BlockSpec(shape, lambda _, place: (0, 0))
-
-    shapes = [(1, rows), (2 * (rows + PAD), quarter), (rows + PAD, quarter)]
+    vmem, smem = pl.BlockSpec(memory_space=pltpu.VMEM), pl.BlockSpec(memory_space=pltpu.SMEM)
     return pl.pallas_call(
-        lambda *refs: pack_kernel(rows, *refs),
-        grid_spec=pltpu.PrefetchScalarGridSpec(
-            num_scalar_prefetch=1,
-            grid=(1,),
-            in_specs=[pl.BlockSpec(memory_space=pltpu.SMEM), whole(1, rows), *map(column, range(3))],
-            out_specs=[whole(*shape) for shape in shapes],
-        ),
+        lambda *refs: pack_kernel(rows, quarter, *refs),
+        in_specs=[smem] * 4 + [vmem, pl.BlockSpec(memory_space=pltpu.HBM)],
+        out_specs=[vmem] * 3,
         out_shape=[
-            jax.ShapeDtypeStruct(shapes[0], jnp.int32),
-            jax.ShapeDtypeStruct(shapes[1], tokens.dtype),
-            jax.ShapeDtypeStruct(shapes[2], tokens.dtype),
+            jax.ShapeDtypeStruct((1, rows), jnp.int32),
+            jax.ShapeDtypeStruct((2 * (rows + PAD), quarter), tokens.dtype),
+            jax.ShapeDtypeStruct((rows + PAD, quarter), tokens.dtype),
         ],
+        scratch_shapes=[pltpu.SemaphoreType.DMA((3,))],
+        compiler_params=pltpu.CompilerParams(vmem_limit_bytes=16 * 2**20),
         cost_estimate=pl.CostEstimate(flops=0, bytes_accessed=0, transcendentals=0),
         name="pack",
-    )(jnp.stack(places), table, index, tokens, tokens, tokens)
+    )(*[jnp.reshape(place, (1,)) for place in places], table, index, tokens)
 
 
 def shrink_kernel(rank, resident, rows, which, places, mode, first_ref, column_ref, *refs):
@@ -336,12 +374,9 @@
         rows_there = lax.dynamic_slice_in_dim(weight, (2 * g + side) * quarter, quarter, 0)
         return (rows_there * SHRINK_GAIN).astype(jnp.float16)
 
-    half_expand = lax.dynamic_slice_in_dim(
-        expand_weight.reshape(held, span), g * (held // 2), held // 2, 0
-    )
-    half_expand = (half_expand * EXPAND_GAIN).astype(jnp.float16)
-    blocks = [half_expand[:, i * LANES : (i + 1) * LANES] for i in range(span // LANES)]
-    mine = jnp.concatenate([shrink_rows(shrink_weight, c), *blocks], axis=0)
+    laid = lay_out(shrink_weight, expand_weight.reshape(held, span), 2 * g + c, g, quarter)
+    is_shrink = lax.broadcasted_iota(jnp.int32, laid.shape, 0) < quarter
+    mine = (laid * jnp.where(is_shrink, SHRINK_GAIN, EXPAND_GAIN)).astype(jnp.float16)
     four = spots == 4
     if four:
         mine_line = FourLine(mine, half)

time: 66.2 us -> 64.6 us (0.976)
  Pallas kernels: 19.1 us -> 16.6 us
  local copies, waits for them, and re-layouts: 0.6 us -> 3.06 us
  other arithmetic: 6.82 us -> 5.86 us
    pallas_call x1 -> x2, Pallas kernels: 3.36 us -> 0.88 us  [the longest x1 0.77 us: pack(): pl.pallas_call(lambda *refs: pack_kernel(rows, quarter, *refs), in_specs=...]
    unnamed x10 -> x14, local copies, waits for them, and re-layouts: 0.11 us -> 2.57 us
    convert_element_type x13 -> x12, other arithmetic: 2.34 us -> 1.25 us  [two_terms(): return (high.astype(jnp.bfloat16), (wide - high).astype(jnp.bfloat16))]
    convert_element_type x1, other arithmetic: 1.1 us -> 1.8 us  [shrink_rows(): return (rows_there * SHRINK_GAIN).astype(jnp.float16)]
  transfers between devices with their start and end apart: 21 -> 21, of which waited for: 10 -> 10; matrix products, arithmetic and copies ran while one was open for 8% -> 10% of each run, Pallas kernels for 26% -> 23%
where the time goes in v6:
time: 64.6 us; the launch traced here: 64.2 us
  starting transfers between devices  23.1 us (36%)
  Pallas kernels  16.6 us (26%)
  waiting for transfers between devices  15 us (23%)
  other arithmetic  5.86 us (9%)
  local copies, waits for them, and re-layouts  3.06 us (5%)
    ppermute x10, starting transfers between devices, send(): lax.ppermute(value, 'adapter', [(2 * s + c, 2 * d + c) for s, d in moves...  15.5 us
    ppermute x10, waiting for transfers between devices, send(): lax.ppermute(value, 'adapter', [(2 * s + c, 2 * d + c) for s, d in moves...  9.85 us
    pallas_call x4, Pallas kernels, shrink_step(): pl.pallas_call(lambda *refs: shrink_kernel(rank, resident, rows, which, p...  7.3 us
    pallas_call x2, Pallas kernels, base_product(): pl.pallas_call(lambda *refs: product_kernel(span, pieces, *refs), in_spec...  6.66 us
    ppermute x3, starting transfers between devices, over_group(): return lax.ppermute(value, 'group', swap)  3.68 us
    unnamed x14, local copies, waits for them, and re-layouts  2.57 us
    ppermute x5, waiting for transfers between devices, over_core(): return lax.ppermute(value, 'adapter', core_pairs)  2.22 us
    convert_element_type x1, other arithmetic, shrink_rows(): return (rows_there * SHRINK_GAIN).astype(jnp.float16)  1.8 us
  transfers between devices with their start and end apart: 21, of which 10 were waited for; matrix products, arithmetic and copies ran while one was open for 10% of the time, Pallas kernels for 23%

profile of v6, /device:TPU:0, one launch (start us, length us, event | category | flops | bytes accessed | tf_op | source)
XLA Modules:
  0.0 64.2 jit_solution(6508645976826686333)
XLA Ops:
  0.0 1.6 %copy-done.2 = f32[4096,128]{1,0:T(8,128)S(1)} copy-done((f32[4096,128]{1,0:T(8,128)S(1)}, f32[4096,128]{1,0:T(8,128)}, u32[]{:S(2)}) %copy-start.2) | copy-done | bytes 2097176
  1.6 0.9 %copy-done.3 = f32[8,16,512]{2,1,0:T(8,128)S(1)} copy-done((f32[8,16,512]{2,1,0:T(8,128)S(1)}, f32[8,16,512]{2,1,0:T(8,128)}, u32[]{:S(2)}) %copy-start.3) | copy-done | bytes 262168
  2.9 3.1 %collective-permute-start.1 = (f16[1280,128]{1,0:T(8,128)(2,1)S(1)}, f16[1280,128]{1,0:T(8,128)(2,1)S(1)}, u32[]{:S(2)}, u32[]{:S(2)}) collective-permute-start(f16[1280,128]{1,0:T(8,128)(2,1)S(1)} %multiply_convert_fusion), channel_id=1, source_target_pairs={{0,4},{2,6},{4,0},{6,2},{8,12},{10,14},{12,8},{14,10},{1,5},{3,7},... | collective-permute-start | bytes 983048 | tf_op jit(solution)/shard_map/ppermute | solution.py:36
  6.0 0.7 %collective-permute-start.2 = (f16[1280,128]{1,0:T(8,128)(2,1)S(1)}, f16[1280,128]{1,0:T(8,128)(2,1)S(1)}, u32[]{:S(2)}, u32[]{:S(2)}) collective-permute-start(f16[1280,128]{1,0:T(8,128)(2,1)S(1)} %multiply_convert_fusion), channel_id=1, source_target_pairs={{4,8},{6,10},{8,4},{10,6},{5,9},{7,11},{9,5},{11,7},{20,24},{22,26... | collective-permute-start | bytes 983048 | tf_op jit(solution)/shard_map/ppermute | solution.py:36
  6.7 1.8 %multiply_convert_fusion.1 = f16[1024,128]{1,0:T(8,128)(2,1)} fusion(f32[4096,128]{1,0:T(8,128)} %shrink_ref.1, s32[]{:T(128)S(6)} %select_n.56), kind=kLoop, calls=%fused_computation.42 | loop fusion | flops 262144 | bytes 786436 | tf_op jit(solution)/shard_map/convert_element_type | solution.py:375
  8.6 0.7 %multiply_bitcast_fusion = s32[4]{0:T(128)S(1)} fusion(s32[4,4]{1,0:T(4,128)} %constant.57.clone, s32[]{:T(128)S(6)} %select_n.53), kind=kLoop, calls=%fused_computation.62 | loop fusion | flops 4 | bytes 36 | tf_op jit(solution)/shard_map/mul | solution.py:508
  10.9 0.8 %pack.1 = (s32[1,256]{1,0:T(1,128)S(1)}, bf16[544,1024]{1,0:T(8,128)(2,1)S(1)}, bf16[272,1024]{1,0:T(8,128)(2,1)S(1)}) custom-call(s32[1]{0:T(128)} %bitcast.6.refs_0_, s32[1]{0:T(128)} %bitcast.7.refs_1_, s32[1]{0:T(128)} %bitcast.8.refs_2_, s32[64]{0:T(128)S(1)} %copy-done.5, s32[1,256]{1,0:T(1,128)S(1)} %bitcast.16, bf16[256,4096]{1,0:T(8,128)(2,1)S(1)} %copy-done), custom_call_target="tpu_custom_call" | custom-call | tf_op jit(solution)/shard_map/pack/pallas_call | solution.py:223
  11.6 1.6 %collective-permute-start.11 = (bf16[544,1024]{1,0:T(8,128)(2,1)S(1)}, bf16[544,1024]{1,0:T(8,128)(2,1)S(1)}, u32[]{:S(2)}, u32[]{:S(2)}) collective-permute-start(bf16[544,1024]{1,0:T(8,128)(2,1)S(1)} %get-tuple-element.54), channel_id=1, source_target_pairs={{0,16},{16,0},{1,17},{17,1},{2,18},{18,2},{3,19},{19,3},{4,20},{20... | collective-permute-start | bytes 3342344 | tf_op jit(solution)/shard_map/ppermute | solution.py:371
  13.2 4.4 %collective-permute-start.5 = (f16[1024,128]{1,0:T(8,128)(2,1)S(1)}, f16[1024,128]{1,0:T(8,128)(2,1)S(1)}, u32[]{:S(2)}, u32[]{:S(2)}) collective-permute-start(f16[1024,128]{1,0:T(8,128)(2,1)S(1)} %collective-permute-done), channel_id=1, source_target_pairs={{0,4},{2,6},{4,0},{6,2},{8,12},{10,14},{12,8},{14,10},{1,5},{3,7},... | collective-permute-start | bytes 786440 | tf_op jit(solution)/shard_map/ppermute | solution.py:36
  18.5 0.7 %collective-permute-start.8 = (f16[1280,128]{1,0:T(8,128)(2,1)S(1)}, f16[1280,128]{1,0:T(8,128)(2,1)S(1)}, u32[]{:S(2)}, u32[]{:S(2)}) collective-permute-start(f16[1280,128]{1,0:T(8,128)(2,1)S(1)} %collective-permute-done.1), channel_id=1, source_target_pairs={{4,8},{6,10},{8,4},{10,6},{5,9},{7,11},{9,5},{11,7},{20,24},{22,26... | collective-permute-start | bytes 983048 | tf_op jit(solution)/shard_map/ppermute | solution.py:36
  19.2 1.3 %collective-permute-start.3 = (f16[1280,128]{1,0:T(8,128)(2,1)S(1)}, f16[1280,128]{1,0:T(8,128)(2,1)S(1)}, u32[]{:S(2)}, u32[]{:S(2)}) collective-permute-start(f16[1280,128]{1,0:T(8,128)(2,1)S(1)} %collective-permute-done.2), channel_id=1, source_target_pairs={{4,0},{6,2},{8,12},{10,14},{5,1},{7,3},{9,13},{11,15},{20,16},{22,... | collective-permute-start | bytes 983048 | tf_op jit(solution)/shard_map/ppermute | solution.py:36
  20.6 3.3 %base_product.2 = f32[256,512]{1,0:T(8,128)S(1)} custom-call(s32[1]{0:T(128)} %bitcast.12.refs_0_, bf16[256,4096]{1,0:T(8,128)(2,1)} %refs_2_.9, bf16[4096,1024]{1,0:T(8,128)(2,1)} %refs_2_.7), custom_call_target="tpu_custom_call" | custom-call | tf_op jit(solution)/shard_map/base_product/pallas_call | solution.py:136
  25.0 1.3 %collective-permute-start.7 = (f16[1024,128]{1,0:T(8,128)(2,1)S(1)}, f16[1024,128]{1,0:T(8,128)(2,1)S(1)}, u32[]{:S(2)}, u32[]{:S(2)}) collective-permute-start(f16[1024,128]{1,0:T(8,128)(2,1)S(1)} %collective-permute-done.6), channel_id=1, source_target_pairs={{4,0},{6,2},{8,12},{10,14},{5,1},{7,3},{9,13},{11,15},{20,16},{22,... | collective-permute-start | bytes 786440 | tf_op jit(solution)/shard_map/ppermute | solution.py:36
  26.3 3.3 %base_product.3.refs_8_ = f32[256,512]{1,0:T(8,128)S(1)} custom-call(s32[1]{0:T(128)} %bitcast.13.refs_0_, bf16[256,4096]{1,0:T(8,128)(2,1)} %refs_2_.9, bf16[4096,1024]{1,0:T(8,128)(2,1)} %refs_2_.7), custom_call_target="tpu_custom_call" | custom-call | tf_op jit(solution)/shard_map/base_product/pallas_call | solution.py:136
  29.8 2.9 %collective-permute-done.3 = f16[1280,128]{1,0:T(8,128)(2,1)S(1)} collective-permute-done((f16[1280,128]{1,0:T(8,128)(2,1)S(1)}, f16[1280,128]{1,0:T(8,128)(2,1)S(1)}, u32[]{:S(2)}, u32[]{:S(2)}) %collective-permute-start.3) | collective-permute-done | bytes 327712 | tf_op jit(solution)/shard_map/ppermute | solution.py:36
  33.1 1.4 %collective-permute-start.9 = (f16[1280,128]{1,0:T(8,128)(2,1)S(1)}, f16[1280,128]{1,0:T(8,128)(2,1)S(1)}, u32[]{:S(2)}, u32[]{:S(2)}) collective-permute-start(f16[1280,128]{1,0:T(8,128)(2,1)S(1)} %collective-permute-done.8), channel_id=1, source_target_pairs={{4,0},{6,2},{8,12},{10,14},{5,1},{7,3},{9,13},{11,15},{20,16},{22,... | collective-permute-start | bytes 983048 | tf_op jit(solution)/shard_map/ppermute | solution.py:36
  34.6 1.3 %collective-permute-start.14 = (f16[1024,128]{1,0:T(8,128)(2,1)S(1)}, f16[1024,128]{1,0:T(8,128)(2,1)S(1)}, u32[]{:S(2)}, u32[]{:S(2)}) collective-permute-start(f16[1024,128]{1,0:T(8,128)(2,1)S(1)} %collective-permute-done.13), channel_id=1, source_target_pairs={{4,0},{6,2},{8,12},{10,14},{5,1},{7,3},{9,13},{11,15},{20,16},{22,... | collective-permute-start | bytes 786440 | tf_op jit(solution)/shard_map/ppermute | solution.py:36
  35.9 2.3 %collective-permute-done.7 = f16[1024,128]{1,0:T(8,128)(2,1)S(1)} collective-permute-done((f16[1024,128]{1,0:T(8,128)(2,1)S(1)}, f16[1024,128]{1,0:T(8,128)(2,1)S(1)}, u32[]{:S(2)}, u32[]{:S(2)}) %collective-permute-start.7) | collective-permute-done | bytes 262176 | tf_op jit(solution)/shard_map/ppermute | solution.py:36
  38.1 1.5 %collective-permute-start.17 = (f32[256,512]{1,0:T(8,128)S(1)}, f32[256,512]{1,0:T(8,128)S(1)}, u32[]{:S(2)}, u32[]{:S(2)}) collective-permute-start(f32[256,512]{1,0:T(8,128)S(1)} %base_product.2), channel_id=1, source_target_pairs={{0,1},{1,0},{2,3},{3,2},{4,5},{5,4},{6,7},{7,6},{8,9},{9,8},{10,11... | collective-permute-start | bytes 1572872 | tf_op jit(solution)/shard_map/ppermute | solution.py:419
  39.9 2.4 %shrink_step.4 = (f32[512,128]{1,0:T(8,128)S(1)}, s32[512,128]{1,0:T(8,128)S(1)}) custom-call(s32[8]{0:T(128)S(1)} %mul.67.refs_0_, s32[1]{0:T(128)} %bitcast.5.refs_1_, bf16[256,4096]{1,0:T(8,128)(2,1)S(1)} %copy-done.1, s32[1,256]{1,0:T(1,128)S(1)} %get-tuple-element.40.refs_3_, bf16[272,1024]{1,0:T(8,128)(2,1)S(1)} %collective-permute-done.4.refs_4_, ...), custom_call_target="tpu_custom_call" | custom-call | tf_op jit(solution)/shard_map/shrink_step/pallas_call | solution.py:296
  42.3 3.5 %collective-permute-done.9 = f16[1280,128]{1,0:T(8,128)(2,1)S(1)} collective-permute-done((f16[1280,128]{1,0:T(8,128)(2,1)S(1)}, f16[1280,128]{1,0:T(8,128)(2,1)S(1)}, u32[]{:S(2)}, u32[]{:S(2)}) %collective-permute-start.9) | collective-permute-done | bytes 327712 | tf_op jit(solution)/shard_map/ppermute | solution.py:36
  46.8 1.0 %collective-permute-done.12.refs_3_.refs_6_ = bf16[272,1024]{1,0:T(8,128)(2,1)S(1)} collective-permute-done((bf16[272,1024]{1,0:T(8,128)(2,1)S(1)}, bf16[272,1024]{1,0:T(8,128)(2,1)S(1)}, u32[]{:S(2)}, u32[]{:S(2)}) %collective-permute-start.12) | collective-permute-done | bytes 557088 | tf_op jit(solution)/shard_map/ppermute | solution.py:368
  47.8 2.3 %shrink_step.5 = (f32[512,128]{1,0:T(8,128)S(1)}, s32[512,128]{1,0:T(8,128)S(1)}) custom-call(s32[8]{0:T(128)S(1)} %mul.67.refs_0_, s32[1]{0:T(128)} %bitcast.5.refs_1_, bf16[544,1024]{1,0:T(8,128)(2,1)S(1)} %collective-permute-done.11.refs_2_.refs_5_, bf16[272,1024]{1,0:T(8,128)(2,1)S(1)} %collective-permute-done.12.refs_3_.refs_6_, ...), custom_call_target="tpu_custom_call" | custom-call | tf_op jit(solution)/shard_map/shrink_step/pallas_call | solution.py:296
  50.1 0.9 %collective-permute-done.14 = f16[1024,128]{1,0:T(8,128)(2,1)S(1)} collective-permute-done((f16[1024,128]{1,0:T(8,128)(2,1)S(1)}, f16[1024,128]{1,0:T(8,128)(2,1)S(1)}, u32[]{:S(2)}, u32[]{:S(2)}) %collective-permute-start.14) | collective-permute-done | bytes 262176 | tf_op jit(solution)/shard_map/ppermute | solution.py:36
  51.2 1.3 %shrink_step.6.refs_8_ = f32[1024,128]{1,0:T(8,128)S(1)} custom-call(s32[8]{0:T(128)S(1)} %mul.67.refs_0_, s32[1]{0:T(128)} %bitcast.5.refs_1_, bf16[256,4096]{1,0:T(8,128)(2,1)S(1)} %copy-done.1, s32[1,256]{1,0:T(1,128)S(1)} %get-tuple-element.40.refs_3_, bf16[272,1024]{1,0:T(8,128)(2,1)S(1)} %collective-permute-done.4.refs_4_, ...), custom_call_target="tpu_custom_call" | custom-call | tf_op jit(solution)/shard_map/shrink_step/pallas_call | solution.py:296
  52.7 1.4 %shrink_step.7 = (f32[16,512]{1,0:T(8,128)S(1)}, f32[16,512]{1,0:T(8,128)S(1)}) custom-call(s32[8]{0:T(128)S(1)} %mul.67.refs_0_, s32[1]{0:T(128)} %bitcast.5.refs_1_, bf16[256,4096]{1,0:T(8,128)(2,1)S(1)} %copy-done.1, s32[1,256]{1,0:T(1,128)S(1)} %get-tuple-element.40.refs_3_, bf16[272,1024]{1,0:T(8,128)(2,1)S(1)} %collective-permute-done.4.refs_4_, ...), custom_call_target="tpu_custom_call" | custom-call | tf_op jit(solution)/shard_map/shrink_step/pallas_call | solution.py:296
  54.2 1.2 %collective-permute-done.15 = f32[16,512]{1,0:T(8,128)S(1)} collective-permute-done((f32[16,512]{1,0:T(8,128)S(1)}, f32[16,512]{1,0:T(8,128)S(1)}, u32[]{:S(2)}, u32[]{:S(2)}) %collective-permute-start.15) | collective-permute-done | bytes 32800 | tf_op jit(solution)/shard_map/ppermute | solution.py:368
  55.7 1.5 %collective-permute-start.18 = (f32[16,256]{1,0:T(8,128)S(1)}, f32[16,256]{1,0:T(8,128)S(1)}, u32[]{:S(2)}, u32[]{:S(2)}) collective-permute-start(f32[16,256]{1,0:T(8,128)S(1)} %get-tuple-element.109), channel_id=1, source_target_pairs={{0,17},{1,16},{16,1},{17,0},{2,19},{3,18},{18,3},{19,2},{4,21},{5,... | collective-permute-start | bytes 49160 | tf_op jit(solution)/shard_map/ppermute | solution.py:490
  57.2 1.5 %collective-permute-start.19 = (f32[16,256]{1,0:T(8,128)S(1)}, f32[16,256]{1,0:T(8,128)S(1)}, u32[]{:S(2)}, u32[]{:S(2)}) collective-permute-start(f32[16,256]{1,0:T(8,128)S(1)} %get-tuple-element.109), channel_id=1, source_target_pairs={{0,16},{16,0},{1,17},{17,1},{2,18},{18,2},{3,19},{19,3},{4,20},{20... | collective-permute-start | bytes 49160 | tf_op jit(solution)/shard_map/ppermute | solution.py:371
  59.5 0.9 %collective-permute-done.18.refs_11_ = f32[16,256]{1,0:T(8,128)S(1)} collective-permute-done((f32[16,256]{1,0:T(8,128)S(1)}, f32[16,256]{1,0:T(8,128)S(1)}, u32[]{:S(2)}, u32[]{:S(2)}) %collective-permute-start.18) | collective-permute-done | bytes 16416 | tf_op jit(solution)/shard_map/ppermute | solution.py:490
  60.9 1.5 %collective-permute-done.20.refs_13_ = f32[16,256]{1,0:T(8,128)S(1)} collective-permute-done((f32[16,256]{1,0:T(8,128)S(1)}, f32[16,256]{1,0:T(8,128)S(1)}, u32[]{:S(2)}, u32[]{:S(2)}) %collective-permute-start.20) | collective-permute-done | bytes 16416 | tf_op jit(solution)/shard_map/ppermute | solution.py:492
  62.4 1.8 %expand_step.1 = bf16[256,512]{1,0:T(8,128)(2,1)} custom-call(s32[1,1024]{1,0:T(1,128)S(1)} %broadcast_in_dim.22.refs_0_, s32[512,128]{1,0:T(8,128)S(1)} %get-tuple-element.49.refs_10_.refs_9_.refs_1_, bf16[256,512]{1,0:T(8,128)(2,1)S(1)} %reduce-precision_convert_fusion.4.refs_2_, bf16[256,512]{1,0:T(8,128)(2,1)S(1)} %get-tuple-element.71.refs_3_, ...), custom_call_target="tpu_custom_call" | custom-call | tf_op jit(solution)/shard_map/expand_step/pallas_call | solution.py:343
  (78 shorter events, 7.7 us)
Async XLA Ops:
  0.0 1.6 %copy-start.2 = (f32[4096,128]{1,0:T(8,128)S(1)}, f32[4096,128]{1,0:T(8,128)}, u32[]{:S(2)}) copy-start(f32[4096,128]{1,0:T(8,128)} %shrink_ref.1) | copy-start | bytes 6291460
  1.6 0.9 %copy-start.3 = (f32[8,16,512]{2,1,0:T(8,128)S(1)}, f32[8,16,512]{2,1,0:T(8,128)}, u32[]{:S(2)}) copy-start(f32[8,16,512]{2,1,0:T(8,128)} %param.12) | copy-start | bytes 786436
  2.7 8.2 %copy-start = (bf16[256,4096]{1,0:T(8,128)(2,1)S(1)}, bf16[256,4096]{1,0:T(8,128)(2,1)}, u32[]{:S(2)}) copy-start(bf16[256,4096]{1,0:T(8,128)(2,1)} %refs_2_.9) | copy-start | bytes 6291460
  2.7 8.1 %copy-start.4 = (s32[256]{0:T(256)S(1)}, s32[256]{0:T(256)}, u32[]{:S(2)}) copy-start(s32[256]{0:T(256)} %param.8) | copy-start | bytes 3076
  2.7 8.1 %copy-start.5 = (s32[64]{0:T(128)S(1)}, s32[64]{0:T(128)}, u32[]{:S(2)}) copy-start(s32[64]{0:T(128)} %refs_3_.1) | copy-start | bytes 772
  2.9 15.6 %collective-permute-start.1 = (f16[1280,128]{1,0:T(8,128)(2,1)S(1)}, f16[1280,128]{1,0:T(8,128)(2,1)S(1)}, u32[]{:S(2)}, u32[]{:S(2)}) collective-permute-start(f16[1280,128]{1,0:T(8,128)(2,1)S(1)} %multiply_convert_fusion), channel_id=1, source_target_pairs={{0,4},{2,6},{4,0},{6,2},{8,12},{10,14},{12,8},{14,10},{1,5},{3,7},... | collective-permute-start | bytes 983048 | tf_op jit(solution)/shard_map/ppermute | solution.py:36
  6.0 12.5 %collective-permute-start.2 = (f16[1280,128]{1,0:T(8,128)(2,1)S(1)}, f16[1280,128]{1,0:T(8,128)(2,1)S(1)}, u32[]{:S(2)}, u32[]{:S(2)}) collective-permute-start(f16[1280,128]{1,0:T(8,128)(2,1)S(1)} %multiply_convert_fusion), channel_id=1, source_target_pairs={{4,8},{6,10},{8,4},{10,6},{5,9},{7,11},{9,5},{11,7},{20,24},{22,26... | collective-permute-start | bytes 983048 | tf_op jit(solution)/shard_map/ppermute | solution.py:36
  8.5 2.3 %collective-permute-start = (f16[1024,128]{1,0:T(8,128)(2,1)}, f16[1024,128]{1,0:T(8,128)(2,1)S(1)}, u32[]{:S(2)}, u32[]{:S(2)}) collective-permute-start(f16[1024,128]{1,0:T(8,128)(2,1)} %multiply_convert_fusion.1), channel_id=1, source_target_pairs={{0,2},{2,0},{4,6},{6,4},{8,10},{10,8},{12,14},{14,12},{1,3},{3,1},... | collective-permute-start | bytes 786440 | tf_op jit(solution)/shard_map/ppermute | solution.py:368
  10.8 9.7 %copy-start.6 = (f16[512,512]{1,0:T(8,128)(2,1)S(1)}, f16[512,512]{1,0:T(8,128)(2,1)}, u32[]{:S(2)}) copy-start(f16[512,512]{1,0:T(8,128)(2,1)} %maximum_dynamic-update-slice_fusion.3) | copy-start | bytes 1572868
  11.6 34.1 %collective-permute-start.11 = (bf16[544,1024]{1,0:T(8,128)(2,1)S(1)}, bf16[544,1024]{1,0:T(8,128)(2,1)S(1)}, u32[]{:S(2)}, u32[]{:S(2)}) collective-permute-start(bf16[544,1024]{1,0:T(8,128)(2,1)S(1)} %get-tuple-element.54), channel_id=1, source_target_pairs={{0,16},{16,0},{1,17},{17,1},{2,18},{18,2},{3,19},{19,3},{4,20},{20... | collective-permute-start | bytes 3342344 | tf_op jit(solution)/shard_map/ppermute | solution.py:371
  13.2 11.1 %collective-permute-start.5 = (f16[1024,128]{1,0:T(8,128)(2,1)S(1)}, f16[1024,128]{1,0:T(8,128)(2,1)S(1)}, u32[]{:S(2)}, u32[]{:S(2)}) collective-permute-start(f16[1024,128]{1,0:T(8,128)(2,1)S(1)} %collective-permute-done), channel_id=1, source_target_pairs={{0,4},{2,6},{4,0},{6,2},{8,12},{10,14},{12,8},{14,10},{1,5},{3,7},... | collective-permute-start | bytes 786440 | tf_op jit(solution)/shard_map/ppermute | solution.py:36
  17.6 6.7 %collective-permute-start.6 = (f16[1024,128]{1,0:T(8,128)(2,1)S(1)}, f16[1024,128]{1,0:T(8,128)(2,1)S(1)}, u32[]{:S(2)}, u32[]{:S(2)}) collective-permute-start(f16[1024,128]{1,0:T(8,128)(2,1)S(1)} %collective-permute-done), channel_id=1, source_target_pairs={{4,8},{6,10},{8,4},{10,6},{5,9},{7,11},{9,5},{11,7},{20,24},{22,26... | collective-permute-start | bytes 786440 | tf_op jit(solution)/shard_map/ppermute | solution.py:36
  18.5 14.5 %collective-permute-start.8 = (f16[1280,128]{1,0:T(8,128)(2,1)S(1)}, f16[1280,128]{1,0:T(8,128)(2,1)S(1)}, u32[]{:S(2)}, u32[]{:S(2)}) collective-permute-start(f16[1280,128]{1,0:T(8,128)(2,1)S(1)} %collective-permute-done.1), channel_id=1, source_target_pairs={{4,8},{6,10},{8,4},{10,6},{5,9},{7,11},{9,5},{11,7},{20,24},{22,26... | collective-permute-start | bytes 983048 | tf_op jit(solution)/shard_map/ppermute | solution.py:36
  19.2 13.5 %collective-permute-start.3 = (f16[1280,128]{1,0:T(8,128)(2,1)S(1)}, f16[1280,128]{1,0:T(8,128)(2,1)S(1)}, u32[]{:S(2)}, u32[]{:S(2)}) collective-permute-start(f16[1280,128]{1,0:T(8,128)(2,1)S(1)} %collective-permute-done.2), channel_id=1, source_target_pairs={{4,0},{6,2},{8,12},{10,14},{5,1},{7,3},{9,13},{11,15},{20,16},{22,... | collective-permute-start | bytes 983048 | tf_op jit(solution)/shard_map/ppermute | solution.py:36
  24.3 10.3 %collective-permute-start.13 = (f16[1024,128]{1,0:T(8,128)(2,1)S(1)}, f16[1024,128]{1,0:T(8,128)(2,1)S(1)}, u32[]{:S(2)}, u32[]{:S(2)}) collective-permute-start(f16[1024,128]{1,0:T(8,128)(2,1)S(1)} %collective-permute-done.5), channel_id=1, source_target_pairs={{4,8},{6,10},{8,4},{10,6},{5,9},{7,11},{9,5},{11,7},{20,24},{22,26... | collective-permute-start | bytes 786440 | tf_op jit(solution)/shard_map/ppermute | solution.py:36
  25.0 13.2 %collective-permute-start.7 = (f16[1024,128]{1,0:T(8,128)(2,1)S(1)}, f16[1024,128]{1,0:T(8,128)(2,1)S(1)}, u32[]{:S(2)}, u32[]{:S(2)}) collective-permute-start(f16[1024,128]{1,0:T(8,128)(2,1)S(1)} %collective-permute-done.6), channel_id=1, source_target_pairs={{4,0},{6,2},{8,12},{10,14},{5,1},{7,3},{9,13},{11,15},{20,16},{22,... | collective-permute-start | bytes 786440 | tf_op jit(solution)/shard_map/ppermute | solution.py:36
  32.9 7.0 %copy-start.1 = (bf16[256,4096]{1,0:T(8,128)(2,1)S(1)}, bf16[256,4096]{1,0:T(8,128)(2,1)}, u32[]{:S(2)}) copy-start(bf16[256,4096]{1,0:T(8,128)(2,1)} %refs_2_.9) | copy-start | bytes 6291460
  33.0 6.9 %collective-permute-start.4 = (bf16[272,1024]{1,0:T(8,128)(2,1)S(1)}, bf16[272,1024]{1,0:T(8,128)(2,1)S(1)}, u32[]{:S(2)}, u32[]{:S(2)}) collective-permute-start(bf16[272,1024]{1,0:T(8,128)(2,1)S(1)} %get-tuple-element.43), channel_id=1, source_target_pairs={{0,2},{2,0},{4,6},{6,4},{8,10},{10,8},{12,14},{14,12},{1,3},{3,1},... | collective-permute-start | bytes 1671176 | tf_op jit(solution)/shard_map/ppermute | solution.py:368
  33.1 12.7 %collective-permute-start.9 = (f16[1280,128]{1,0:T(8,128)(2,1)S(1)}, f16[1280,128]{1,0:T(8,128)(2,1)S(1)}, u32[]{:S(2)}, u32[]{:S(2)}) collective-permute-start(f16[1280,128]{1,0:T(8,128)(2,1)S(1)} %collective-permute-done.8), channel_id=1, source_target_pairs={{4,0},{6,2},{8,12},{10,14},{5,1},{7,3},{9,13},{11,15},{20,16},{22,... | collective-permute-start | bytes 983048 | tf_op jit(solution)/shard_map/ppermute | solution.py:36
  34.6 16.5 %collective-permute-start.14 = (f16[1024,128]{1,0:T(8,128)(2,1)S(1)}, f16[1024,128]{1,0:T(8,128)(2,1)S(1)}, u32[]{:S(2)}, u32[]{:S(2)}) collective-permute-start(f16[1024,128]{1,0:T(8,128)(2,1)S(1)} %collective-permute-done.13), channel_id=1, source_target_pairs={{4,0},{6,2},{8,12},{10,14},{5,1},{7,3},{9,13},{11,15},{20,16},{22,... | collective-permute-start | bytes 786440 | tf_op jit(solution)/shard_map/ppermute | solution.py:36
  38.1 21.3 %collective-permute-start.17 = (f32[256,512]{1,0:T(8,128)S(1)}, f32[256,512]{1,0:T(8,128)S(1)}, u32[]{:S(2)}, u32[]{:S(2)}) collective-permute-start(f32[256,512]{1,0:T(8,128)S(1)} %base_product.2), channel_id=1, source_target_pairs={{0,1},{1,0},{2,3},{3,2},{4,5},{5,4},{6,7},{7,6},{8,9},{9,8},{10,11... | collective-permute-start | bytes 1572872 | tf_op jit(solution)/shard_map/ppermute | solution.py:419
  45.8 2.0 %collective-permute-start.12 = (bf16[272,1024]{1,0:T(8,128)(2,1)S(1)}, bf16[272,1024]{1,0:T(8,128)(2,1)S(1)}, u32[]{:S(2)}, u32[]{:S(2)}) collective-permute-start(bf16[272,1024]{1,0:T(8,128)(2,1)S(1)} %slice.145), channel_id=1, source_target_pairs={{0,2},{2,0},{4,6},{6,4},{8,10},{10,8},{12,14},{14,12},{1,3},{3,1},... | collective-permute-start | bytes 1671176 | tf_op jit(solution)/shard_map/ppermute | solution.py:368
  46.2 9.2 %collective-permute-start.10 = (f16[256,512]{1,0:T(8,128)(2,1)S(1)}, f16[256,512]{1,0:T(8,128)(2,1)S(1)}, u32[]{:S(2)}, u32[]{:S(2)}) collective-permute-start(f16[256,512]{1,0:T(8,128)(2,1)S(1)} %get-tuple-element.72), channel_id=1, source_target_pairs={{0,16},{16,0},{1,17},{17,1},{2,18},{18,2},{3,19},{19,3},{4,20},{20... | collective-permute-start | bytes 786440 | tf_op jit(solution)/shard_map/ppermute | solution.py:371
  54.1 1.3 %collective-permute-start.15 = (f32[16,512]{1,0:T(8,128)S(1)}, f32[16,512]{1,0:T(8,128)S(1)}, u32[]{:S(2)}, u32[]{:S(2)}) collective-permute-start(f32[16,512]{1,0:T(8,128)S(1)} %get-tuple-element.67), channel_id=1, source_target_pairs={{0,2},{2,0},{4,6},{6,4},{8,10},{10,8},{12,14},{14,12},{1,3},{3,1},... | collective-permute-start | bytes 98312 | tf_op jit(solution)/shard_map/ppermute | solution.py:368
  55.4 3.9 %collective-permute-start.16 = (f16[512,512]{1,0:T(8,128)(2,1)S(1)}, f16[512,512]{1,0:T(8,128)(2,1)S(1)}, u32[]{:S(2)}, u32[]{:S(2)}) collective-permute-start(f16[512,512]{1,0:T(8,128)(2,1)S(1)} %constant_dynamic-update-slice_fusion), channel_id=1, source_target_pairs={{0,2},{2,0},{4,6},{6,4},{8,10},{10,8},{12,14},{14,12},{1,3},{3,1},... | collective-permute-start | bytes 1572872 | tf_op jit(solution)/shard_map/ppermute | solution.py:368
  55.7 4.7 %collective-permute-start.18 = (f32[16,256]{1,0:T(8,128)S(1)}, f32[16,256]{1,0:T(8,128)S(1)}, u32[]{:S(2)}, u32[]{:S(2)}) collective-permute-start(f32[16,256]{1,0:T(8,128)S(1)} %get-tuple-element.109), channel_id=1, source_target_pairs={{0,17},{1,16},{16,1},{17,0},{2,19},{3,18},{18,3},{19,2},{4,21},{5,... | collective-permute-start | bytes 49160 | tf_op jit(solution)/shard_map/ppermute | solution.py:490
  57.2 3.7 %collective-permute-start.19 = (f32[16,256]{1,0:T(8,128)S(1)}, f32[16,256]{1,0:T(8,128)S(1)}, u32[]{:S(2)}, u32[]{:S(2)}) collective-permute-start(f32[16,256]{1,0:T(8,128)S(1)} %get-tuple-element.109), channel_id=1, source_target_pairs={{0,16},{16,0},{1,17},{17,1},{2,18},{18,2},{3,19},{19,3},{4,20},{20... | collective-permute-start | bytes 49160 | tf_op jit(solution)/shard_map/ppermute | solution.py:371
  58.7 3.7 %collective-permute-start.20 = (f32[16,256]{1,0:T(8,128)S(1)}, f32[16,256]{1,0:T(8,128)S(1)}, u32[]{:S(2)}, u32[]{:S(2)}) collective-permute-start(f32[16,256]{1,0:T(8,128)S(1)} %get-tuple-element.110.refs_10_), channel_id=1, source_target_pairs={{0,1},{1,0},{2,3},{3,2},{4,5},{5,4},{6,7},{7,6},{8,9},{9,8},{10,11... | collective-permute-start | bytes 49160 | tf_op jit(solution)/shard_map/ppermute | solution.py:492

commit v7 on v6

--- a/solution.py
+++ b/solution.py
@@ -473,14 +473,8 @@
     for start in range(some, last, 3):
         weights = weights_of(start, min(start + 3, last))
         sums = products(*all_parts, weights, 2 * start, sums, slots_of, 1)
-    sums = products(*all_parts, [side_by_side(late_mine[last][:quarter])], 2 * last, sums, slots_of, 1)
-    (almost,) = sums
-    if four:
-        given_line.last, almost = barrier((given_line.last, almost))
-        late_given = given_line.pieces()
-    stays, leaves = products(
-        *all_parts, [side_by_side(late_given[last])], 2 * last + 1, (almost,), slots_of, 2
-    )
+    weights = [side_by_side(late_mine[last][:quarter]), side_by_side(late_given[last])]
+    stays, leaves = products(*all_parts, weights, 2 * last, sums, slots_of, 2)
     both_sum = stays + over_core(leaves)
     own_sum, other_sum = both_sum[:, :rows], both_sum[:, rows:]
     if len(bases) == 2:

time: 64.6 us -> 64 us (level)
  Pallas kernels: 16.6 us -> 15.9 us
    pallas_call x4 -> x3, Pallas kernels: 7.3 us -> 6.57 us  [shrink_step(): pl.pallas_call(lambda *refs: shrink_kernel(rank, resident, rows, which, p...]
  transfers between devices with their start and end apart: 21 -> 21, of which waited for: 10 -> 11; matrix products, arithmetic and copies ran while one was open for 10% -> 10% of each run, Pallas kernels for 23% -> 22%
where the time goes in v7:
time: 64 us; the launch traced here: 63.6 us
  starting transfers between devices  22.9 us (36%)
  Pallas kernels  15.9 us (25%)
  waiting for transfers between devices  15.4 us (24%)
  other arithmetic  5.86 us (9%)
  local copies, waits for them, and re-layouts  3.06 us (5%)
    ppermute x10, starting transfers between devices, send(): lax.ppermute(value, 'adapter', [(2 * s + c, 2 * d + c) for s, d in moves...  15.5 us
    ppermute x10, waiting for transfers between devices, send(): lax.ppermute(value, 'adapter', [(2 * s + c, 2 * d + c) for s, d in moves...  9.85 us
    pallas_call x2, Pallas kernels, base_product(): pl.pallas_call(lambda *refs: product_kernel(span, pieces, *refs), in_spec...  6.66 us
    pallas_call x3, Pallas kernels, shrink_step(): pl.pallas_call(lambda *refs: shrink_kernel(rank, resident, rows, which, p...  6.57 us
    ppermute x3, starting transfers between devices, over_group(): return lax.ppermute(value, 'group', swap)  3.68 us
    unnamed x14, local copies, waits for them, and re-layouts  2.57 us
    ppermute x5, waiting for transfers between devices, over_core(): return lax.ppermute(value, 'adapter', core_pairs)  2.22 us
    convert_element_type x1, other arithmetic, shrink_rows(): return (rows_there * SHRINK_GAIN).astype(jnp.float16)  1.8 us
  transfers between devices with their start and end apart: 21, of which 11 were waited for; matrix products, arithmetic and copies ran while one was open for 10% of the time, Pallas kernels for 22%

profile of v7, /device:TPU:0, one launch (start us, length us, event | category | flops | bytes accessed | tf_op | source)
XLA Modules:
  0.0 63.6 jit_solution(7346421202491442488)
XLA Ops:
  0.0 1.6 %copy-done.2 = f32[4096,128]{1,0:T(8,128)S(1)} copy-done((f32[4096,128]{1,0:T(8,128)S(1)}, f32[4096,128]{1,0:T(8,128)}, u32[]{:S(2)}) %copy-start.2) | copy-done | bytes 2097176
  1.6 0.9 %copy-done.3 = f32[8,16,512]{2,1,0:T(8,128)S(1)} copy-done((f32[8,16,512]{2,1,0:T(8,128)S(1)}, f32[8,16,512]{2,1,0:T(8,128)}, u32[]{:S(2)}) %copy-start.3) | copy-done | bytes 262168
  2.9 3.1 %collective-permute-start.1 = (f16[1280,128]{1,0:T(8,128)(2,1)S(1)}, f16[1280,128]{1,0:T(8,128)(2,1)S(1)}, u32[]{:S(2)}, u32[]{:S(2)}) collective-permute-start(f16[1280,128]{1,0:T(8,128)(2,1)S(1)} %multiply_convert_fusion), channel_id=1, source_target_pairs={{0,4},{2,6},{4,0},{6,2},{8,12},{10,14},{12,8},{14,10},{1,5},{3,7},... | collective-permute-start | bytes 983048 | tf_op jit(solution)/shard_map/ppermute | solution.py:36
  6.0 0.7 %collective-permute-start.2 = (f16[1280,128]{1,0:T(8,128)(2,1)S(1)}, f16[1280,128]{1,0:T(8,128)(2,1)S(1)}, u32[]{:S(2)}, u32[]{:S(2)}) collective-permute-start(f16[1280,128]{1,0:T(8,128)(2,1)S(1)} %multiply_convert_fusion), channel_id=1, source_target_pairs={{4,8},{6,10},{8,4},{10,6},{5,9},{7,11},{9,5},{11,7},{20,24},{22,26... | collective-permute-start | bytes 983048 | tf_op jit(solution)/shard_map/ppermute | solution.py:36
  6.7 1.8 %multiply_convert_fusion.1 = f16[1024,128]{1,0:T(8,128)(2,1)} fusion(f32[4096,128]{1,0:T(8,128)} %shrink_ref.1, s32[]{:T(128)S(6)} %select_n.56), kind=kLoop, calls=%fused_computation.42 | loop fusion | flops 262144 | bytes 786436 | tf_op jit(solution)/shard_map/convert_element_type | solution.py:375
  8.6 0.7 %multiply_bitcast_fusion = s32[4]{0:T(128)S(1)} fusion(s32[4,4]{1,0:T(4,128)} %constant.57.clone, s32[]{:T(128)S(6)} %select_n.53), kind=kLoop, calls=%fused_computation.62 | loop fusion | flops 4 | bytes 36 | tf_op jit(solution)/shard_map/mul | solution.py:502
  10.9 0.8 %pack.1 = (s32[1,256]{1,0:T(1,128)S(1)}, bf16[544,1024]{1,0:T(8,128)(2,1)S(1)}, bf16[272,1024]{1,0:T(8,128)(2,1)S(1)}) custom-call(s32[1]{0:T(128)} %bitcast.6.refs_0_, s32[1]{0:T(128)} %bitcast.7.refs_1_, s32[1]{0:T(128)} %bitcast.8.refs_2_, s32[64]{0:T(128)S(1)} %copy-done.5, s32[1,256]{1,0:T(1,128)S(1)} %bitcast.16, bf16[256,4096]{1,0:T(8,128)(2,1)S(1)} %copy-done), custom_call_target="tpu_custom_call" | custom-call | tf_op jit(solution)/shard_map/pack/pallas_call | solution.py:223
  11.6 1.6 %collective-permute-start.11 = (bf16[544,1024]{1,0:T(8,128)(2,1)S(1)}, bf16[544,1024]{1,0:T(8,128)(2,1)S(1)}, u32[]{:S(2)}, u32[]{:S(2)}) collective-permute-start(bf16[544,1024]{1,0:T(8,128)(2,1)S(1)} %get-tuple-element.52), channel_id=1, source_target_pairs={{0,16},{16,0},{1,17},{17,1},{2,18},{18,2},{3,19},{19,3},{4,20},{20... | collective-permute-start | bytes 3342344 | tf_op jit(solution)/shard_map/ppermute | solution.py:371
  13.2 4.4 %collective-permute-start.5 = (f16[1024,128]{1,0:T(8,128)(2,1)S(1)}, f16[1024,128]{1,0:T(8,128)(2,1)S(1)}, u32[]{:S(2)}, u32[]{:S(2)}) collective-permute-start(f16[1024,128]{1,0:T(8,128)(2,1)S(1)} %collective-permute-done), channel_id=1, source_target_pairs={{0,4},{2,6},{4,0},{6,2},{8,12},{10,14},{12,8},{14,10},{1,5},{3,7},... | collective-permute-start | bytes 786440 | tf_op jit(solution)/shard_map/ppermute | solution.py:36
  18.5 0.7 %collective-permute-start.8 = (f16[1280,128]{1,0:T(8,128)(2,1)S(1)}, f16[1280,128]{1,0:T(8,128)(2,1)S(1)}, u32[]{:S(2)}, u32[]{:S(2)}) collective-permute-start(f16[1280,128]{1,0:T(8,128)(2,1)S(1)} %collective-permute-done.1), channel_id=1, source_target_pairs={{4,8},{6,10},{8,4},{10,6},{5,9},{7,11},{9,5},{11,7},{20,24},{22,26... | collective-permute-start | bytes 983048 | tf_op jit(solution)/shard_map/ppermute | solution.py:36
  19.2 1.3 %collective-permute-start.3 = (f16[1280,128]{1,0:T(8,128)(2,1)S(1)}, f16[1280,128]{1,0:T(8,128)(2,1)S(1)}, u32[]{:S(2)}, u32[]{:S(2)}) collective-permute-start(f16[1280,128]{1,0:T(8,128)(2,1)S(1)} %collective-permute-done.2), channel_id=1, source_target_pairs={{4,0},{6,2},{8,12},{10,14},{5,1},{7,3},{9,13},{11,15},{20,16},{22,... | collective-permute-start | bytes 983048 | tf_op jit(solution)/shard_map/ppermute | solution.py:36
  20.6 3.3 %base_product.2 = f32[256,512]{1,0:T(8,128)S(1)} custom-call(s32[1]{0:T(128)} %bitcast.12.refs_0_, bf16[256,4096]{1,0:T(8,128)(2,1)} %refs_2_.7, bf16[4096,1024]{1,0:T(8,128)(2,1)} %refs_2_.6), custom_call_target="tpu_custom_call" | custom-call | tf_op jit(solution)/shard_map/base_product/pallas_call | solution.py:136
  24.3 0.7 %collective-permute-start.13 = (f16[1024,128]{1,0:T(8,128)(2,1)S(1)}, f16[1024,128]{1,0:T(8,128)(2,1)S(1)}, u32[]{:S(2)}, u32[]{:S(2)}) collective-permute-start(f16[1024,128]{1,0:T(8,128)(2,1)S(1)} %collective-permute-done.5), channel_id=1, source_target_pairs={{4,8},{6,10},{8,4},{10,6},{5,9},{7,11},{9,5},{11,7},{20,24},{22,26... | collective-permute-start | bytes 786440 | tf_op jit(solution)/shard_map/ppermute | solution.py:36
  25.0 1.3 %collective-permute-start.7 = (f16[1024,128]{1,0:T(8,128)(2,1)S(1)}, f16[1024,128]{1,0:T(8,128)(2,1)S(1)}, u32[]{:S(2)}, u32[]{:S(2)}) collective-permute-start(f16[1024,128]{1,0:T(8,128)(2,1)S(1)} %collective-permute-done.6), channel_id=1, source_target_pairs={{4,0},{6,2},{8,12},{10,14},{5,1},{7,3},{9,13},{11,15},{20,16},{22,... | collective-permute-start | bytes 786440 | tf_op jit(solution)/shard_map/ppermute | solution.py:36
  26.3 3.3 %base_product.3.refs_8_ = f32[256,512]{1,0:T(8,128)S(1)} custom-call(s32[1]{0:T(128)} %bitcast.13.refs_0_, bf16[256,4096]{1,0:T(8,128)(2,1)} %refs_2_.7, bf16[4096,1024]{1,0:T(8,128)(2,1)} %refs_2_.6), custom_call_target="tpu_custom_call" | custom-call | tf_op jit(solution)/shard_map/base_product/pallas_call | solution.py:136
  29.8 2.9 %collective-permute-done.3 = f16[1280,128]{1,0:T(8,128)(2,1)S(1)} collective-permute-done((f16[1280,128]{1,0:T(8,128)(2,1)S(1)}, f16[1280,128]{1,0:T(8,128)(2,1)S(1)}, u32[]{:S(2)}, u32[]{:S(2)}) %collective-permute-start.3) | collective-permute-done | bytes 327712 | tf_op jit(solution)/shard_map/ppermute | solution.py:36
  33.1 1.4 %collective-permute-start.9 = (f16[1280,128]{1,0:T(8,128)(2,1)S(1)}, f16[1280,128]{1,0:T(8,128)(2,1)S(1)}, u32[]{:S(2)}, u32[]{:S(2)}) collective-permute-start(f16[1280,128]{1,0:T(8,128)(2,1)S(1)} %collective-permute-done.8), channel_id=1, source_target_pairs={{4,0},{6,2},{8,12},{10,14},{5,1},{7,3},{9,13},{11,15},{20,16},{22,... | collective-permute-start | bytes 983048 | tf_op jit(solution)/shard_map/ppermute | solution.py:36
  34.6 1.3 %collective-permute-start.14 = (f16[1024,128]{1,0:T(8,128)(2,1)S(1)}, f16[1024,128]{1,0:T(8,128)(2,1)S(1)}, u32[]{:S(2)}, u32[]{:S(2)}) collective-permute-start(f16[1024,128]{1,0:T(8,128)(2,1)S(1)} %collective-permute-done.13), channel_id=1, source_target_pairs={{4,0},{6,2},{8,12},{10,14},{5,1},{7,3},{9,13},{11,15},{20,16},{22,... | collective-permute-start | bytes 786440 | tf_op jit(solution)/shard_map/ppermute | solution.py:36
  35.9 2.3 %collective-permute-done.7 = f16[1024,128]{1,0:T(8,128)(2,1)S(1)} collective-permute-done((f16[1024,128]{1,0:T(8,128)(2,1)S(1)}, f16[1024,128]{1,0:T(8,128)(2,1)S(1)}, u32[]{:S(2)}, u32[]{:S(2)}) %collective-permute-start.7) | collective-permute-done | bytes 262176 | tf_op jit(solution)/shard_map/ppermute | solution.py:36
  38.1 1.5 %collective-permute-start.17 = (f32[256,512]{1,0:T(8,128)S(1)}, f32[256,512]{1,0:T(8,128)S(1)}, u32[]{:S(2)}, u32[]{:S(2)}) collective-permute-start(f32[256,512]{1,0:T(8,128)S(1)} %base_product.2), channel_id=1, source_target_pairs={{0,1},{1,0},{2,3},{3,2},{4,5},{5,4},{6,7},{7,6},{8,9},{9,8},{10,11... | collective-permute-start | bytes 1572872 | tf_op jit(solution)/shard_map/ppermute | solution.py:419
  39.9 2.3 %shrink_step.3 = (f32[512,128]{1,0:T(8,128)S(1)}, s32[512,128]{1,0:T(8,128)S(1)}) custom-call(s32[8]{0:T(128)S(1)} %mul.67.refs_0_, s32[1]{0:T(128)} %bitcast.5.refs_1_, bf16[256,4096]{1,0:T(8,128)(2,1)S(1)} %copy-done.1, s32[1,256]{1,0:T(1,128)S(1)} %get-tuple-element.38.refs_3_, bf16[272,1024]{1,0:T(8,128)(2,1)S(1)} %collective-permute-done.4.refs_4_, ...), custom_call_target="tpu_custom_call" | custom-call | tf_op jit(solution)/shard_map/shrink_step/pallas_call | solution.py:296
  42.3 3.5 %collective-permute-done.9 = f16[1280,128]{1,0:T(8,128)(2,1)S(1)} collective-permute-done((f16[1280,128]{1,0:T(8,128)(2,1)S(1)}, f16[1280,128]{1,0:T(8,128)(2,1)S(1)}, u32[]{:S(2)}, u32[]{:S(2)}) %collective-permute-start.9) | collective-permute-done | bytes 327712 | tf_op jit(solution)/shard_map/ppermute | solution.py:36
  46.8 1.0 %collective-permute-done.12.refs_3_.refs_6_ = bf16[272,1024]{1,0:T(8,128)(2,1)S(1)} collective-permute-done((bf16[272,1024]{1,0:T(8,128)(2,1)S(1)}, bf16[272,1024]{1,0:T(8,128)(2,1)S(1)}, u32[]{:S(2)}, u32[]{:S(2)}) %collective-permute-start.12) | collective-permute-done | bytes 557088 | tf_op jit(solution)/shard_map/ppermute | solution.py:368
  47.8 2.3 %shrink_step.4 = (f32[512,128]{1,0:T(8,128)S(1)}, s32[512,128]{1,0:T(8,128)S(1)}) custom-call(s32[8]{0:T(128)S(1)} %mul.67.refs_0_, s32[1]{0:T(128)} %bitcast.5.refs_1_, bf16[544,1024]{1,0:T(8,128)(2,1)S(1)} %collective-permute-done.11.refs_2_.refs_5_, bf16[272,1024]{1,0:T(8,128)(2,1)S(1)} %collective-permute-done.12.refs_3_.refs_6_, ...), custom_call_target="tpu_custom_call" | custom-call | tf_op jit(solution)/shard_map/shrink_step/pallas_call | solution.py:296
  50.1 0.9 %collective-permute-done.14 = f16[1024,128]{1,0:T(8,128)(2,1)S(1)} collective-permute-done((f16[1024,128]{1,0:T(8,128)(2,1)S(1)}, f16[1024,128]{1,0:T(8,128)(2,1)S(1)}, u32[]{:S(2)}, u32[]{:S(2)}) %collective-permute-start.14) | collective-permute-done | bytes 262176 | tf_op jit(solution)/shard_map/ppermute | solution.py:36
  51.4 1.9 %shrink_step.5 = (f32[16,512]{1,0:T(8,128)S(1)}, f32[16,512]{1,0:T(8,128)S(1)}) custom-call(s32[8]{0:T(128)S(1)} %mul.67.refs_0_, s32[1]{0:T(128)} %bitcast.5.refs_1_, bf16[256,4096]{1,0:T(8,128)(2,1)S(1)} %copy-done.1, s32[1,256]{1,0:T(1,128)S(1)} %get-tuple-element.38.refs_3_, bf16[272,1024]{1,0:T(8,128)(2,1)S(1)} %collective-permute-done.4.refs_4_, ...), custom_call_target="tpu_custom_call" | custom-call | tf_op jit(solution)/shard_map/shrink_step/pallas_call | solution.py:296
  53.4 1.2 %collective-permute-done.15 = f32[16,512]{1,0:T(8,128)S(1)} collective-permute-done((f32[16,512]{1,0:T(8,128)S(1)}, f32[16,512]{1,0:T(8,128)S(1)}, u32[]{:S(2)}, u32[]{:S(2)}) %collective-permute-start.15) | collective-permute-done | bytes 32800 | tf_op jit(solution)/shard_map/ppermute | solution.py:368
  55.1 1.5 %collective-permute-start.18 = (f32[16,256]{1,0:T(8,128)S(1)}, f32[16,256]{1,0:T(8,128)S(1)}, u32[]{:S(2)}, u32[]{:S(2)}) collective-permute-start(f32[16,256]{1,0:T(8,128)S(1)} %get-tuple-element.105), channel_id=1, source_target_pairs={{0,17},{1,16},{16,1},{17,0},{2,19},{3,18},{18,3},{19,2},{4,21},{5,... | collective-permute-start | bytes 49160 | tf_op jit(solution)/shard_map/ppermute | solution.py:484
  56.6 1.5 %collective-permute-start.19 = (f32[16,256]{1,0:T(8,128)S(1)}, f32[16,256]{1,0:T(8,128)S(1)}, u32[]{:S(2)}, u32[]{:S(2)}) collective-permute-start(f32[16,256]{1,0:T(8,128)S(1)} %get-tuple-element.105), channel_id=1, source_target_pairs={{0,16},{16,0},{1,17},{17,1},{2,18},{18,2},{3,19},{19,3},{4,20},{20... | collective-permute-start | bytes 49160 | tf_op jit(solution)/shard_map/ppermute | solution.py:371
  58.9 0.9 %collective-permute-done.18.refs_11_ = f32[16,256]{1,0:T(8,128)S(1)} collective-permute-done((f32[16,256]{1,0:T(8,128)S(1)}, f32[16,256]{1,0:T(8,128)S(1)}, u32[]{:S(2)}, u32[]{:S(2)}) %collective-permute-start.18) | collective-permute-done | bytes 16416 | tf_op jit(solution)/shard_map/ppermute | solution.py:484
  60.4 1.5 %collective-permute-done.20.refs_13_ = f32[16,256]{1,0:T(8,128)S(1)} collective-permute-done((f32[16,256]{1,0:T(8,128)S(1)}, f32[16,256]{1,0:T(8,128)S(1)}, u32[]{:S(2)}, u32[]{:S(2)}) %collective-permute-start.20) | collective-permute-done | bytes 16416 | tf_op jit(solution)/shard_map/ppermute | solution.py:486
  61.9 1.8 %expand_step.1 = bf16[256,512]{1,0:T(8,128)(2,1)} custom-call(s32[1,1024]{1,0:T(1,128)S(1)} %broadcast_in_dim.22.refs_0_, s32[512,128]{1,0:T(8,128)S(1)} %get-tuple-element.47.refs_11_.refs_1_, bf16[256,512]{1,0:T(8,128)(2,1)S(1)} %reduce-precision_convert_fusion.4.refs_2_, bf16[256,512]{1,0:T(8,128)(2,1)S(1)} %get-tuple-element.67.refs_3_, ...), custom_call_target="tpu_custom_call" | custom-call | tf_op jit(solution)/shard_map/expand_step/pallas_call | solution.py:343
  (77 shorter events, 7.3 us)
Async XLA Ops:
  0.0 1.6 %copy-start.2 = (f32[4096,128]{1,0:T(8,128)S(1)}, f32[4096,128]{1,0:T(8,128)}, u32[]{:S(2)}) copy-start(f32[4096,128]{1,0:T(8,128)} %shrink_ref.1) | copy-start | bytes 6291460
  1.6 0.9 %copy-start.3 = (f32[8,16,512]{2,1,0:T(8,128)S(1)}, f32[8,16,512]{2,1,0:T(8,128)}, u32[]{:S(2)}) copy-start(f32[8,16,512]{2,1,0:T(8,128)} %param.12) | copy-start | bytes 786436
  2.7 8.2 %copy-start = (bf16[256,4096]{1,0:T(8,128)(2,1)S(1)}, bf16[256,4096]{1,0:T(8,128)(2,1)}, u32[]{:S(2)}) copy-start(bf16[256,4096]{1,0:T(8,128)(2,1)} %refs_2_.7) | copy-start | bytes 6291460
  2.7 8.1 %copy-start.4 = (s32[256]{0:T(256)S(1)}, s32[256]{0:T(256)}, u32[]{:S(2)}) copy-start(s32[256]{0:T(256)} %param.8) | copy-start | bytes 3076
  2.7 8.1 %copy-start.5 = (s32[64]{0:T(128)S(1)}, s32[64]{0:T(128)}, u32[]{:S(2)}) copy-start(s32[64]{0:T(128)} %refs_3_.1) | copy-start | bytes 772
  2.9 15.6 %collective-permute-start.1 = (f16[1280,128]{1,0:T(8,128)(2,1)S(1)}, f16[1280,128]{1,0:T(8,128)(2,1)S(1)}, u32[]{:S(2)}, u32[]{:S(2)}) collective-permute-start(f16[1280,128]{1,0:T(8,128)(2,1)S(1)} %multiply_convert_fusion), channel_id=1, source_target_pairs={{0,4},{2,6},{4,0},{6,2},{8,12},{10,14},{12,8},{14,10},{1,5},{3,7},... | collective-permute-start | bytes 983048 | tf_op jit(solution)/shard_map/ppermute | solution.py:36
  6.0 12.5 %collective-permute-start.2 = (f16[1280,128]{1,0:T(8,128)(2,1)S(1)}, f16[1280,128]{1,0:T(8,128)(2,1)S(1)}, u32[]{:S(2)}, u32[]{:S(2)}) collective-permute-start(f16[1280,128]{1,0:T(8,128)(2,1)S(1)} %multiply_convert_fusion), channel_id=1, source_target_pairs={{4,8},{6,10},{8,4},{10,6},{5,9},{7,11},{9,5},{11,7},{20,24},{22,26... | collective-permute-start | bytes 983048 | tf_op jit(solution)/shard_map/ppermute | solution.py:36
  8.5 2.3 %collective-permute-start = (f16[1024,128]{1,0:T(8,128)(2,1)}, f16[1024,128]{1,0:T(8,128)(2,1)S(1)}, u32[]{:S(2)}, u32[]{:S(2)}) collective-permute-start(f16[1024,128]{1,0:T(8,128)(2,1)} %multiply_convert_fusion.1), channel_id=1, source_target_pairs={{0,2},{2,0},{4,6},{6,4},{8,10},{10,8},{12,14},{14,12},{1,3},{3,1},... | collective-permute-start | bytes 786440 | tf_op jit(solution)/shard_map/ppermute | solution.py:368
  10.8 9.7 %copy-start.6 = (f16[512,512]{1,0:T(8,128)(2,1)S(1)}, f16[512,512]{1,0:T(8,128)(2,1)}, u32[]{:S(2)}) copy-start(f16[512,512]{1,0:T(8,128)(2,1)} %maximum_dynamic-update-slice_fusion.3) | copy-start | bytes 1572868
  11.6 34.1 %collective-permute-start.11 = (bf16[544,1024]{1,0:T(8,128)(2,1)S(1)}, bf16[544,1024]{1,0:T(8,128)(2,1)S(1)}, u32[]{:S(2)}, u32[]{:S(2)}) collective-permute-start(bf16[544,1024]{1,0:T(8,128)(2,1)S(1)} %get-tuple-element.52), channel_id=1, source_target_pairs={{0,16},{16,0},{1,17},{17,1},{2,18},{18,2},{3,19},{19,3},{4,20},{20... | collective-permute-start | bytes 3342344 | tf_op jit(solution)/shard_map/ppermute | solution.py:371
  13.2 11.1 %collective-permute-start.5 = (f16[1024,128]{1,0:T(8,128)(2,1)S(1)}, f16[1024,128]{1,0:T(8,128)(2,1)S(1)}, u32[]{:S(2)}, u32[]{:S(2)}) collective-permute-start(f16[1024,128]{1,0:T(8,128)(2,1)S(1)} %collective-permute-done), channel_id=1, source_target_pairs={{0,4},{2,6},{4,0},{6,2},{8,12},{10,14},{12,8},{14,10},{1,5},{3,7},... | collective-permute-start | bytes 786440 | tf_op jit(solution)/shard_map/ppermute | solution.py:36
  17.6 6.7 %collective-permute-start.6 = (f16[1024,128]{1,0:T(8,128)(2,1)S(1)}, f16[1024,128]{1,0:T(8,128)(2,1)S(1)}, u32[]{:S(2)}, u32[]{:S(2)}) collective-permute-start(f16[1024,128]{1,0:T(8,128)(2,1)S(1)} %collective-permute-done), channel_id=1, source_target_pairs={{4,8},{6,10},{8,4},{10,6},{5,9},{7,11},{9,5},{11,7},{20,24},{22,26... | collective-permute-start | bytes 786440 | tf_op jit(solution)/shard_map/ppermute | solution.py:36
  18.5 14.5 %collective-permute-start.8 = (f16[1280,128]{1,0:T(8,128)(2,1)S(1)}, f16[1280,128]{1,0:T(8,128)(2,1)S(1)}, u32[]{:S(2)}, u32[]{:S(2)}) collective-permute-start(f16[1280,128]{1,0:T(8,128)(2,1)S(1)} %collective-permute-done.1), channel_id=1, source_target_pairs={{4,8},{6,10},{8,4},{10,6},{5,9},{7,11},{9,5},{11,7},{20,24},{22,26... | collective-permute-start | bytes 983048 | tf_op jit(solution)/shard_map/ppermute | solution.py:36
  19.2 13.5 %collective-permute-start.3 = (f16[1280,128]{1,0:T(8,128)(2,1)S(1)}, f16[1280,128]{1,0:T(8,128)(2,1)S(1)}, u32[]{:S(2)}, u32[]{:S(2)}) collective-permute-start(f16[1280,128]{1,0:T(8,128)(2,1)S(1)} %collective-permute-done.2), channel_id=1, source_target_pairs={{4,0},{6,2},{8,12},{10,14},{5,1},{7,3},{9,13},{11,15},{20,16},{22,... | collective-permute-start | bytes 983048 | tf_op jit(solution)/shard_map/ppermute | solution.py:36
  24.3 10.3 %collective-permute-start.13 = (f16[1024,128]{1,0:T(8,128)(2,1)S(1)}, f16[1024,128]{1,0:T(8,128)(2,1)S(1)}, u32[]{:S(2)}, u32[]{:S(2)}) collective-permute-start(f16[1024,128]{1,0:T(8,128)(2,1)S(1)} %collective-permute-done.5), channel_id=1, source_target_pairs={{4,8},{6,10},{8,4},{10,6},{5,9},{7,11},{9,5},{11,7},{20,24},{22,26... | collective-permute-start | bytes 786440 | tf_op jit(solution)/shard_map/ppermute | solution.py:36
  25.0 13.2 %collective-permute-start.7 = (f16[1024,128]{1,0:T(8,128)(2,1)S(1)}, f16[1024,128]{1,0:T(8,128)(2,1)S(1)}, u32[]{:S(2)}, u32[]{:S(2)}) collective-permute-start(f16[1024,128]{1,0:T(8,128)(2,1)S(1)} %collective-permute-done.6), channel_id=1, source_target_pairs={{4,0},{6,2},{8,12},{10,14},{5,1},{7,3},{9,13},{11,15},{20,16},{22,... | collective-permute-start | bytes 786440 | tf_op jit(solution)/shard_map/ppermute | solution.py:36
  32.9 7.0 %copy-start.1 = (bf16[256,4096]{1,0:T(8,128)(2,1)S(1)}, bf16[256,4096]{1,0:T(8,128)(2,1)}, u32[]{:S(2)}) copy-start(bf16[256,4096]{1,0:T(8,128)(2,1)} %refs_2_.7) | copy-start | bytes 6291460
  33.0 6.9 %collective-permute-start.4 = (bf16[272,1024]{1,0:T(8,128)(2,1)S(1)}, bf16[272,1024]{1,0:T(8,128)(2,1)S(1)}, u32[]{:S(2)}, u32[]{:S(2)}) collective-permute-start(bf16[272,1024]{1,0:T(8,128)(2,1)S(1)} %get-tuple-element.41), channel_id=1, source_target_pairs={{0,2},{2,0},{4,6},{6,4},{8,10},{10,8},{12,14},{14,12},{1,3},{3,1},... | collective-permute-start | bytes 1671176 | tf_op jit(solution)/shard_map/ppermute | solution.py:368
  33.1 12.7 %collective-permute-start.9 = (f16[1280,128]{1,0:T(8,128)(2,1)S(1)}, f16[1280,128]{1,0:T(8,128)(2,1)S(1)}, u32[]{:S(2)}, u32[]{:S(2)}) collective-permute-start(f16[1280,128]{1,0:T(8,128)(2,1)S(1)} %collective-permute-done.8), channel_id=1, source_target_pairs={{4,0},{6,2},{8,12},{10,14},{5,1},{7,3},{9,13},{11,15},{20,16},{22,... | collective-permute-start | bytes 983048 | tf_op jit(solution)/shard_map/ppermute | solution.py:36
  34.6 16.5 %collective-permute-start.14 = (f16[1024,128]{1,0:T(8,128)(2,1)S(1)}, f16[1024,128]{1,0:T(8,128)(2,1)S(1)}, u32[]{:S(2)}, u32[]{:S(2)}) collective-permute-start(f16[1024,128]{1,0:T(8,128)(2,1)S(1)} %collective-permute-done.13), channel_id=1, source_target_pairs={{4,0},{6,2},{8,12},{10,14},{5,1},{7,3},{9,13},{11,15},{20,16},{22,... | collective-permute-start | bytes 786440 | tf_op jit(solution)/shard_map/ppermute | solution.py:36
  38.1 20.8 %collective-permute-start.17 = (f32[256,512]{1,0:T(8,128)S(1)}, f32[256,512]{1,0:T(8,128)S(1)}, u32[]{:S(2)}, u32[]{:S(2)}) collective-permute-start(f32[256,512]{1,0:T(8,128)S(1)} %base_product.2), channel_id=1, source_target_pairs={{0,1},{1,0},{2,3},{3,2},{4,5},{5,4},{6,7},{7,6},{8,9},{9,8},{10,11... | collective-permute-start | bytes 1572872 | tf_op jit(solution)/shard_map/ppermute | solution.py:419
  45.8 2.0 %collective-permute-start.12 = (bf16[272,1024]{1,0:T(8,128)(2,1)S(1)}, bf16[272,1024]{1,0:T(8,128)(2,1)S(1)}, u32[]{:S(2)}, u32[]{:S(2)}) collective-permute-start(bf16[272,1024]{1,0:T(8,128)(2,1)S(1)} %slice.145), channel_id=1, source_target_pairs={{0,2},{2,0},{4,6},{6,4},{8,10},{10,8},{12,14},{14,12},{1,3},{3,1},... | collective-permute-start | bytes 1671176 | tf_op jit(solution)/shard_map/ppermute | solution.py:368
  46.2 8.8 %collective-permute-start.10 = (f16[256,512]{1,0:T(8,128)(2,1)S(1)}, f16[256,512]{1,0:T(8,128)(2,1)S(1)}, u32[]{:S(2)}, u32[]{:S(2)}) collective-permute-start(f16[256,512]{1,0:T(8,128)(2,1)S(1)} %get-tuple-element.68), channel_id=1, source_target_pairs={{0,16},{16,0},{1,17},{17,1},{2,18},{18,2},{3,19},{19,3},{4,20},{20... | collective-permute-start | bytes 786440 | tf_op jit(solution)/shard_map/ppermute | solution.py:371
  53.3 1.3 %collective-permute-start.15 = (f32[16,512]{1,0:T(8,128)S(1)}, f32[16,512]{1,0:T(8,128)S(1)}, u32[]{:S(2)}, u32[]{:S(2)}) collective-permute-start(f32[16,512]{1,0:T(8,128)S(1)} %get-tuple-element.63), channel_id=1, source_target_pairs={{0,2},{2,0},{4,6},{6,4},{8,10},{10,8},{12,14},{14,12},{1,3},{3,1},... | collective-permute-start | bytes 98312 | tf_op jit(solution)/shard_map/ppermute | solution.py:368
  55.0 3.8 %collective-permute-start.16 = (f16[512,512]{1,0:T(8,128)(2,1)S(1)}, f16[512,512]{1,0:T(8,128)(2,1)S(1)}, u32[]{:S(2)}, u32[]{:S(2)}) collective-permute-start(f16[512,512]{1,0:T(8,128)(2,1)S(1)} %constant_dynamic-update-slice_fusion), channel_id=1, source_target_pairs={{0,2},{2,0},{4,6},{6,4},{8,10},{10,8},{12,14},{14,12},{1,3},{3,1},... | collective-permute-start | bytes 1572872 | tf_op jit(solution)/shard_map/ppermute | solution.py:368
  55.1 4.7 %collective-permute-start.18 = (f32[16,256]{1,0:T(8,128)S(1)}, f32[16,256]{1,0:T(8,128)S(1)}, u32[]{:S(2)}, u32[]{:S(2)}) collective-permute-start(f32[16,256]{1,0:T(8,128)S(1)} %get-tuple-element.105), channel_id=1, source_target_pairs={{0,17},{1,16},{16,1},{17,0},{2,19},{3,18},{18,3},{19,2},{4,21},{5,... | collective-permute-start | bytes 49160 | tf_op jit(solution)/shard_map/ppermute | solution.py:484
  56.6 3.7 %collective-permute-start.19 = (f32[16,256]{1,0:T(8,128)S(1)}, f32[16,256]{1,0:T(8,128)S(1)}, u32[]{:S(2)}, u32[]{:S(2)}) collective-permute-start(f32[16,256]{1,0:T(8,128)S(1)} %get-tuple-element.105), channel_id=1, source_target_pairs={{0,16},{16,0},{1,17},{17,1},{2,18},{18,2},{3,19},{19,3},{4,20},{20... | collective-permute-start | bytes 49160 | tf_op jit(solution)/shard_map/ppermute | solution.py:371
  58.2 3.7 %collective-permute-start.20 = (f32[16,256]{1,0:T(8,128)S(1)}, f32[16,256]{1,0:T(8,128)S(1)}, u32[]{:S(2)}, u32[]{:S(2)}) collective-permute-start(f32[16,256]{1,0:T(8,128)S(1)} %get-tuple-element.106.refs_10_), channel_id=1, source_target_pairs={{0,1},{1,0},{2,3},{3,2},{4,5},{5,4},{6,7},{7,6},{8,9},{9,8},{10,11... | collective-permute-start | bytes 49160 | tf_op jit(solution)/shard_map/ppermute | solution.py:486

commit v8 on v7

--- a/solution.py
+++ b/solution.py
@@ -236,7 +236,15 @@
     )(*[jnp.reshape(place, (1,)) for place in places], table, index, tokens)
 
 
-def shrink_kernel(rank, resident, rows, which, places, mode, first_ref, column_ref, *refs):
+def flip(value, by):
+    return 1 - value if by else value
+
+
+def first_slot(source_ref, spot, piece, core, resident):
+    return resident * (2 * source_ref[spot, piece] + core)
+
+
+def shrink_kernel(rank, resident, rows, which, places, mode, source_ref, spot_ref, core_ref, column_ref, *refs):
     held = rank * resident
     count = 1 + max(max(p[0], p[2] or 0) for p in places)
     operands, refs = refs[:count], refs[count:]
@@ -271,7 +279,8 @@
             total = jnp.zeros((rows, held), jnp.float32)
         for w, side in zip(weights, which):
             product = jnp.dot(tokens, w[...], preferred_element_type=jnp.float32)
-            chosen = slot == first_ref[side] + group
+            first = first_slot(source_ref, spot_ref[0], side // 2, flip(core_ref[0], side % 2), resident)
+            chosen = slot == first + group
             total = jnp.where(chosen, product[:, :held] + product[:, held:], total)
         if mode < 2:
             out_ref = outs[0] if mode else refs[0]
@@ -285,7 +294,7 @@
             outs[part % 2][:, at : at + rows] = gathered
 
 
-def shrink_step(operands, places, weights, firsts, column, which, sums, slots, mode, rows, rank, resident):
+def shrink_step(operands, places, weights, facts, which, sums, slots, mode, rows, rank, resident):
     vmem = pl.BlockSpec(memory_space=pltpu.VMEM)
     smem = pl.BlockSpec(memory_space=pltpu.SMEM)
     operands = [*operands, *weights, *sums, *slots]
@@ -295,13 +304,13 @@
     shapes = [[wide, jax.ShapeDtypeStruct((count, held), jnp.int32)], [wide], [narrow, narrow]][mode]
     return pl.pallas_call(
         lambda *refs: shrink_kernel(rank, resident, rows, which, places, mode, *refs),
-        in_specs=[smem, smem] + [vmem] * len(operands),
+        in_specs=[smem] * 4 + [vmem] * len(operands),
         out_specs=[vmem] * len(shapes),
         out_shape=shapes,
         compiler_params=pltpu.CompilerParams(vmem_limit_bytes=16 * 2**20),
         cost_estimate=pl.CostEstimate(flops=0, bytes_accessed=0, transcendentals=0),
         name="shrink_step",
-    )(firsts, jnp.reshape(column, (1,)), *operands)
+    )(*facts[:3], facts[4], *operands)
 
 
 def expand_kernel(rank, groups, scale, count, slots_ref, slot_ref, *refs):
@@ -400,8 +409,6 @@
     theirs = over_group(sent)
     came_theirs = over_core(theirs[: rows + PAD])
 
-    source = jnp.asarray(sources(spots))[half]
-    firsts = resident * (2 * source[:, None] + jnp.stack([c, 1 - c])[None, :]).reshape(-1)
     axes = ("tensor", "sub")
     two = lax.axis_size("tensor") == 2 and lax.axis_size("sub") == 1
     x = lax.axis_index("tensor")
@@ -437,7 +444,8 @@
             given_line.advance()
     mine_pieces, given_pieces = mine_line.pieces(), given_line.pieces()
 
-    column = (2 * g + c) * quarter
+    scalars = (half, c, g, (2 * g + c) * quarter)
+    facts = [jnp.asarray(sources(spots))] + [jnp.reshape(value, (1,)) for value in scalars]
 
     def weights_of(start, stop):
         weights = []
@@ -448,7 +456,7 @@
     def products(operands, places, weights, start, sums=(), slots=(), mode=0):
         which = list(range(start, start + len(weights)))
         return shrink_step(
-            operands, places, weights, firsts, column, which, sums, slots, mode, rows, rank, resident
+            operands, places, weights, facts, which, sums, slots, mode, rows, rank, resident
         )
 
     here_parts = ((tokens, slot, came_own), ((0, 0, 1), (2, 0, None)))
@@ -496,6 +504,8 @@
     across, _ = barrier((over_group(here), both_sum))
     beside = over_core(jnp.concatenate([here, across], axis=0))
     terms = [two_terms(here), two_terms(across), two_terms(beside)]
+    late_half = half
+    source = jnp.asarray(sources(spots))[late_half]
     steps = jnp.arange(resident // 2, dtype=jnp.int32)
     sides = jnp.stack([c, 1 - c])[:, None, None, None]
     halves = jnp.stack([g, 1 - g])[None, :, None, None] * (resident // 2)

time: 64 us -> 63.5 us (level)
  other arithmetic: 5.86 us -> 5.09 us
    mul x2, other arithmetic: 0.76 us -> 0.08 us  [per_device(): slots = (2 * source[:, None] + sides) * resident + halves + steps]
    unnamed x14 -> x16, local copies, waits for them, and re-layouts: 2.57 us -> 2.57 us
  transfers between devices with their start and end apart: 21 -> 21, of which waited for: 11 -> 11; matrix products, arithmetic and copies ran while one was open for 10% -> 8% of each run, Pallas kernels for 22% -> 22%
where the time goes in v8:
time: 63.5 us; the launch traced here: 63.1 us
  starting transfers between devices  23.1 us (36%)
  Pallas kernels  16 us (25%)
  waiting for transfers between devices  15.4 us (24%)
  other arithmetic  5.09 us (8%)
  local copies, waits for them, and re-layouts  2.98 us (5%)
    ppermute x10, starting transfers between devices, send(): lax.ppermute(value, 'adapter', [(2 * s + c, 2 * d + c) for s, d in moves...  15.5 us
    ppermute x10, waiting for transfers between devices, send(): lax.ppermute(value, 'adapter', [(2 * s + c, 2 * d + c) for s, d in moves...  9.8 us
    pallas_call x2, Pallas kernels, base_product(): pl.pallas_call(lambda *refs: product_kernel(span, pieces, *refs), in_spec...  6.66 us
    pallas_call x3, Pallas kernels, shrink_step(): pl.pallas_call(lambda *refs: shrink_kernel(rank, resident, rows, which, p...  6.65 us
    ppermute x3, starting transfers between devices, over_group(): return lax.ppermute(value, 'group', swap)  3.68 us
    unnamed x16, local copies, waits for them, and re-layouts  2.57 us
    ppermute x5, waiting for transfers between devices, over_core(): return lax.ppermute(value, 'adapter', core_pairs)  2.33 us
    convert_element_type x1, other arithmetic, shrink_rows(): return (rows_there * SHRINK_GAIN).astype(jnp.float16)  1.8 us
  transfers between devices with their start and end apart: 21, of which 11 were waited for; matrix products, arithmetic and copies ran while one was open for 8% of the time, Pallas kernels for 22%

profile of v8, /device:TPU:0, one launch (start us, length us, event | category | flops | bytes accessed | tf_op | source)
XLA Modules:
  0.0 63.1 jit_solution(14723932721167894490)
XLA Ops:
  0.0 1.6 %copy-done.2 = f32[4096,128]{1,0:T(8,128)S(1)} copy-done((f32[4096,128]{1,0:T(8,128)S(1)}, f32[4096,128]{1,0:T(8,128)}, u32[]{:S(2)}) %copy-start.2) | copy-done | bytes 2097176
  1.6 0.9 %copy-done.3 = f32[8,16,512]{2,1,0:T(8,128)S(1)} copy-done((f32[8,16,512]{2,1,0:T(8,128)S(1)}, f32[8,16,512]{2,1,0:T(8,128)}, u32[]{:S(2)}) %copy-start.3) | copy-done | bytes 262168
  2.9 3.1 %collective-permute-start.1 = (f16[1280,128]{1,0:T(8,128)(2,1)S(1)}, f16[1280,128]{1,0:T(8,128)(2,1)S(1)}, u32[]{:S(2)}, u32[]{:S(2)}) collective-permute-start(f16[1280,128]{1,0:T(8,128)(2,1)S(1)} %multiply_convert_fusion), channel_id=1, source_target_pairs={{0,4},{2,6},{4,0},{6,2},{8,12},{10,14},{12,8},{14,10},{1,5},{3,7},... | collective-permute-start | bytes 983048 | tf_op jit(solution)/shard_map/ppermute | solution.py:36
  6.0 0.7 %collective-permute-start.2 = (f16[1280,128]{1,0:T(8,128)(2,1)S(1)}, f16[1280,128]{1,0:T(8,128)(2,1)S(1)}, u32[]{:S(2)}, u32[]{:S(2)}) collective-permute-start(f16[1280,128]{1,0:T(8,128)(2,1)S(1)} %multiply_convert_fusion), channel_id=1, source_target_pairs={{4,8},{6,10},{8,4},{10,6},{5,9},{7,11},{9,5},{11,7},{20,24},{22,26... | collective-permute-start | bytes 983048 | tf_op jit(solution)/shard_map/ppermute | solution.py:36
  6.7 1.8 %multiply_convert_fusion.1 = f16[1024,128]{1,0:T(8,128)(2,1)} fusion(f32[4096,128]{1,0:T(8,128)} %shrink_ref.1, s32[]{:T(128)S(6)} %select_n.56), kind=kLoop, calls=%fused_computation.42 | loop fusion | flops 262144 | bytes 786436 | tf_op jit(solution)/shard_map/convert_element_type | solution.py:384
  10.3 0.8 %pack.1 = (s32[1,256]{1,0:T(1,128)S(1)}, bf16[544,1024]{1,0:T(8,128)(2,1)S(1)}, bf16[272,1024]{1,0:T(8,128)(2,1)S(1)}) custom-call(s32[1]{0:T(128)} %bitcast.7.refs_0_, s32[1]{0:T(128)} %bitcast.8.refs_1_, s32[1]{0:T(128)} %bitcast.9.refs_2_, s32[64]{0:T(128)S(1)} %copy-done.6, s32[1,256]{1,0:T(1,128)S(1)} %bitcast.17, bf16[256,4096]{1,0:T(8,128)(2,1)S(1)} %copy-done), custom_call_target="tpu_custom_call" | custom-call | tf_op jit(solution)/shard_map/pack/pallas_call | solution.py:223
  11.1 1.6 %collective-permute-start.11 = (bf16[544,1024]{1,0:T(8,128)(2,1)S(1)}, bf16[544,1024]{1,0:T(8,128)(2,1)S(1)}, u32[]{:S(2)}, u32[]{:S(2)}) collective-permute-start(bf16[544,1024]{1,0:T(8,128)(2,1)S(1)} %get-tuple-element.52), channel_id=1, source_target_pairs={{0,16},{16,0},{1,17},{17,1},{2,18},{18,2},{3,19},{19,3},{4,20},{20... | collective-permute-start | bytes 3342344 | tf_op jit(solution)/shard_map/ppermute | solution.py:380
  12.7 4.4 %collective-permute-start.5 = (f16[1024,128]{1,0:T(8,128)(2,1)S(1)}, f16[1024,128]{1,0:T(8,128)(2,1)S(1)}, u32[]{:S(2)}, u32[]{:S(2)}) collective-permute-start(f16[1024,128]{1,0:T(8,128)(2,1)S(1)} %collective-permute-done), channel_id=1, source_target_pairs={{0,4},{2,6},{4,0},{6,2},{8,12},{10,14},{12,8},{14,10},{1,5},{3,7},... | collective-permute-start | bytes 786440 | tf_op jit(solution)/shard_map/ppermute | solution.py:36
  18.0 0.7 %collective-permute-start.8 = (f16[1280,128]{1,0:T(8,128)(2,1)S(1)}, f16[1280,128]{1,0:T(8,128)(2,1)S(1)}, u32[]{:S(2)}, u32[]{:S(2)}) collective-permute-start(f16[1280,128]{1,0:T(8,128)(2,1)S(1)} %collective-permute-done.1), channel_id=1, source_target_pairs={{4,8},{6,10},{8,4},{10,6},{5,9},{7,11},{9,5},{11,7},{20,24},{22,26... | collective-permute-start | bytes 983048 | tf_op jit(solution)/shard_map/ppermute | solution.py:36
  18.7 1.3 %collective-permute-start.3 = (f16[1280,128]{1,0:T(8,128)(2,1)S(1)}, f16[1280,128]{1,0:T(8,128)(2,1)S(1)}, u32[]{:S(2)}, u32[]{:S(2)}) collective-permute-start(f16[1280,128]{1,0:T(8,128)(2,1)S(1)} %collective-permute-done.2), channel_id=1, source_target_pairs={{4,0},{6,2},{8,12},{10,14},{5,1},{7,3},{9,13},{11,15},{20,16},{22,... | collective-permute-start | bytes 983048 | tf_op jit(solution)/shard_map/ppermute | solution.py:36
  20.0 3.3 %base_product.2 = f32[256,512]{1,0:T(8,128)S(1)} custom-call(s32[1]{0:T(128)} %bitcast.13.refs_0_, bf16[256,4096]{1,0:T(8,128)(2,1)} %refs_4_.3, bf16[4096,1024]{1,0:T(8,128)(2,1)} %refs_2_.3), custom_call_target="tpu_custom_call" | custom-call | tf_op jit(solution)/shard_map/base_product/pallas_call | solution.py:136
  23.5 0.7 %collective-permute-start.13 = (f16[1024,128]{1,0:T(8,128)(2,1)S(1)}, f16[1024,128]{1,0:T(8,128)(2,1)S(1)}, u32[]{:S(2)}, u32[]{:S(2)}) collective-permute-start(f16[1024,128]{1,0:T(8,128)(2,1)S(1)} %collective-permute-done.5), channel_id=1, source_target_pairs={{4,8},{6,10},{8,4},{10,6},{5,9},{7,11},{9,5},{11,7},{20,24},{22,26... | collective-permute-start | bytes 786440 | tf_op jit(solution)/shard_map/ppermute | solution.py:36
  24.2 1.3 %collective-permute-start.7 = (f16[1024,128]{1,0:T(8,128)(2,1)S(1)}, f16[1024,128]{1,0:T(8,128)(2,1)S(1)}, u32[]{:S(2)}, u32[]{:S(2)}) collective-permute-start(f16[1024,128]{1,0:T(8,128)(2,1)S(1)} %collective-permute-done.6), channel_id=1, source_target_pairs={{4,0},{6,2},{8,12},{10,14},{5,1},{7,3},{9,13},{11,15},{20,16},{22,... | collective-permute-start | bytes 786440 | tf_op jit(solution)/shard_map/ppermute | solution.py:36
  25.5 3.3 %base_product.3.refs_8_ = f32[256,512]{1,0:T(8,128)S(1)} custom-call(s32[1]{0:T(128)} %bitcast.14.refs_0_, bf16[256,4096]{1,0:T(8,128)(2,1)} %refs_4_.3, bf16[4096,1024]{1,0:T(8,128)(2,1)} %refs_2_.3), custom_call_target="tpu_custom_call" | custom-call | tf_op jit(solution)/shard_map/base_product/pallas_call | solution.py:136
  29.0 2.9 %collective-permute-done.3 = f16[1280,128]{1,0:T(8,128)(2,1)S(1)} collective-permute-done((f16[1280,128]{1,0:T(8,128)(2,1)S(1)}, f16[1280,128]{1,0:T(8,128)(2,1)S(1)}, u32[]{:S(2)}, u32[]{:S(2)}) %collective-permute-start.3) | collective-permute-done | bytes 327712 | tf_op jit(solution)/shard_map/ppermute | solution.py:36
  32.2 1.4 %collective-permute-start.9 = (f16[1280,128]{1,0:T(8,128)(2,1)S(1)}, f16[1280,128]{1,0:T(8,128)(2,1)S(1)}, u32[]{:S(2)}, u32[]{:S(2)}) collective-permute-start(f16[1280,128]{1,0:T(8,128)(2,1)S(1)} %collective-permute-done.8), channel_id=1, source_target_pairs={{4,0},{6,2},{8,12},{10,14},{5,1},{7,3},{9,13},{11,15},{20,16},{22,... | collective-permute-start | bytes 983048 | tf_op jit(solution)/shard_map/ppermute | solution.py:36
  33.7 1.3 %collective-permute-start.14 = (f16[1024,128]{1,0:T(8,128)(2,1)S(1)}, f16[1024,128]{1,0:T(8,128)(2,1)S(1)}, u32[]{:S(2)}, u32[]{:S(2)}) collective-permute-start(f16[1024,128]{1,0:T(8,128)(2,1)S(1)} %collective-permute-done.13), channel_id=1, source_target_pairs={{4,0},{6,2},{8,12},{10,14},{5,1},{7,3},{9,13},{11,15},{20,16},{22,... | collective-permute-start | bytes 786440 | tf_op jit(solution)/shard_map/ppermute | solution.py:36
  35.0 2.3 %collective-permute-done.7 = f16[1024,128]{1,0:T(8,128)(2,1)S(1)} collective-permute-done((f16[1024,128]{1,0:T(8,128)(2,1)S(1)}, f16[1024,128]{1,0:T(8,128)(2,1)S(1)}, u32[]{:S(2)}, u32[]{:S(2)}) %collective-permute-start.7) | collective-permute-done | bytes 262176 | tf_op jit(solution)/shard_map/ppermute | solution.py:36
  37.3 1.5 %collective-permute-start.17 = (f32[256,512]{1,0:T(8,128)S(1)}, f32[256,512]{1,0:T(8,128)S(1)}, u32[]{:S(2)}, u32[]{:S(2)}) collective-permute-start(f32[256,512]{1,0:T(8,128)S(1)} %base_product.2), channel_id=1, source_target_pairs={{0,1},{1,0},{2,3},{3,2},{4,5},{5,4},{6,7},{7,6},{8,9},{9,8},{10,11... | collective-permute-start | bytes 1572872 | tf_op jit(solution)/shard_map/ppermute | solution.py:426
  39.1 2.4 %shrink_step.3 = (f32[512,128]{1,0:T(8,128)S(1)}, s32[512,128]{1,0:T(8,128)S(1)}) custom-call(s32[4,4]{1,0:T(4,128)S(1)} %copy-done.4, s32[1]{0:T(128)} %bitcast.5.refs_1_, s32[1]{0:T(128)} %bitcast.1.refs_2_, s32[1]{0:T(128)} %bitcast.6.refs_3_, bf16[256,4096]{1,0:T(8,128)(2,1)S(1)} %copy-done.1, s32[1,256]{1,0:T(1,128)S(1)} %get-tuple-element.38.refs_5_, ...), custom_call_target="tpu_custom_call" | custom-call | tf_op jit(solution)/shard_map/shrink_step/pallas_call | solution.py:305
  41.5 3.8 %collective-permute-done.9 = f16[1280,128]{1,0:T(8,128)(2,1)S(1)} collective-permute-done((f16[1280,128]{1,0:T(8,128)(2,1)S(1)}, f16[1280,128]{1,0:T(8,128)(2,1)S(1)}, u32[]{:S(2)}, u32[]{:S(2)}) %collective-permute-start.9) | collective-permute-done | bytes 327712 | tf_op jit(solution)/shard_map/ppermute | solution.py:36
  45.7 0.8 %collective-permute-start.10 = (f16[256,512]{1,0:T(8,128)(2,1)S(1)}, f16[256,512]{1,0:T(8,128)(2,1)S(1)}, u32[]{:S(2)}, u32[]{:S(2)}) collective-permute-start(f16[256,512]{1,0:T(8,128)(2,1)S(1)} %get-tuple-element.68), channel_id=1, source_target_pairs={{0,16},{16,0},{1,17},{17,1},{2,18},{18,2},{3,19},{19,3},{4,20},{20... | collective-permute-start | bytes 786440 | tf_op jit(solution)/shard_map/ppermute | solution.py:380
  46.4 0.9 %collective-permute-done.12.refs_5_.refs_8_ = bf16[272,1024]{1,0:T(8,128)(2,1)S(1)} collective-permute-done((bf16[272,1024]{1,0:T(8,128)(2,1)S(1)}, bf16[272,1024]{1,0:T(8,128)(2,1)S(1)}, u32[]{:S(2)}, u32[]{:S(2)}) %collective-permute-start.12) | collective-permute-done | bytes 557088 | tf_op jit(solution)/shard_map/ppermute | solution.py:377
  47.3 2.4 %shrink_step.4 = (f32[512,128]{1,0:T(8,128)S(1)}, s32[512,128]{1,0:T(8,128)S(1)}) custom-call(s32[4,4]{1,0:T(4,128)S(1)} %copy-done.4, s32[1]{0:T(128)} %bitcast.5.refs_1_, s32[1]{0:T(128)} %bitcast.1.refs_2_, s32[1]{0:T(128)} %bitcast.6.refs_3_, bf16[544,1024]{1,0:T(8,128)(2,1)S(1)} %collective-permute-done.11.refs_4_.refs_7_, ...), custom_call_target="tpu_custom_call" | custom-call | tf_op jit(solution)/shard_map/shrink_step/pallas_call | solution.py:305
  49.7 0.8 %collective-permute-done.14 = f16[1024,128]{1,0:T(8,128)(2,1)S(1)} collective-permute-done((f16[1024,128]{1,0:T(8,128)(2,1)S(1)}, f16[1024,128]{1,0:T(8,128)(2,1)S(1)}, u32[]{:S(2)}, u32[]{:S(2)}) %collective-permute-start.14) | collective-permute-done | bytes 262176 | tf_op jit(solution)/shard_map/ppermute | solution.py:36
  50.9 1.9 %shrink_step.5 = (f32[16,512]{1,0:T(8,128)S(1)}, f32[16,512]{1,0:T(8,128)S(1)}) custom-call(s32[4,4]{1,0:T(4,128)S(1)} %copy-done.4, s32[1]{0:T(128)} %bitcast.5.refs_1_, s32[1]{0:T(128)} %bitcast.1.refs_2_, s32[1]{0:T(128)} %bitcast.6.refs_3_, bf16[256,4096]{1,0:T(8,128)(2,1)S(1)} %copy-done.1, s32[1,256]{1,0:T(1,128)S(1)} %get-tuple-element.38.refs_5_, ...), custom_call_target="tpu_custom_call" | custom-call | tf_op jit(solution)/shard_map/shrink_step/pallas_call | solution.py:305
  52.9 1.2 %collective-permute-done.15 = f32[16,512]{1,0:T(8,128)S(1)} collective-permute-done((f32[16,512]{1,0:T(8,128)S(1)}, f32[16,512]{1,0:T(8,128)S(1)}, u32[]{:S(2)}, u32[]{:S(2)}) %collective-permute-start.15) | collective-permute-done | bytes 32800 | tf_op jit(solution)/shard_map/ppermute | solution.py:377
  54.6 1.7 %collective-permute-start.18 = (f32[16,256]{1,0:T(8,128)S(1)}, f32[16,256]{1,0:T(8,128)S(1)}, u32[]{:S(2)}, u32[]{:S(2)}) collective-permute-start(f32[16,256]{1,0:T(8,128)S(1)} %get-tuple-element.105), channel_id=1, source_target_pairs={{0,17},{1,16},{16,1},{17,0},{2,19},{3,18},{18,3},{19,2},{4,21},{5,... | collective-permute-start | bytes 49160 | tf_op jit(solution)/shard_map/ppermute | solution.py:492
  56.3 1.3 %collective-permute-start.19 = (f32[16,256]{1,0:T(8,128)S(1)}, f32[16,256]{1,0:T(8,128)S(1)}, u32[]{:S(2)}, u32[]{:S(2)}) collective-permute-start(f32[16,256]{1,0:T(8,128)S(1)} %get-tuple-element.105), channel_id=1, source_target_pairs={{0,16},{16,0},{1,17},{17,1},{2,18},{18,2},{3,19},{19,3},{4,20},{20... | collective-permute-start | bytes 49160 | tf_op jit(solution)/shard_map/ppermute | solution.py:380
  58.4 1.0 %collective-permute-done.18.refs_11_ = f32[16,256]{1,0:T(8,128)S(1)} collective-permute-done((f32[16,256]{1,0:T(8,128)S(1)}, f32[16,256]{1,0:T(8,128)S(1)}, u32[]{:S(2)}, u32[]{:S(2)}) %collective-permute-start.18) | collective-permute-done | bytes 16416 | tf_op jit(solution)/shard_map/ppermute | solution.py:492
  60.0 1.3 %collective-permute-done.20.refs_13_ = f32[16,256]{1,0:T(8,128)S(1)} collective-permute-done((f32[16,256]{1,0:T(8,128)S(1)}, f32[16,256]{1,0:T(8,128)S(1)}, u32[]{:S(2)}, u32[]{:S(2)}) %collective-permute-start.20) | collective-permute-done | bytes 16416 | tf_op jit(solution)/shard_map/ppermute | solution.py:494
  61.4 1.8 %expand_step.1 = bf16[256,512]{1,0:T(8,128)(2,1)} custom-call(s32[1,1024]{1,0:T(1,128)S(1)} %broadcast_in_dim.21.refs_0_, s32[512,128]{1,0:T(8,128)S(1)} %get-tuple-element.47.refs_13_.refs_1_, bf16[256,512]{1,0:T(8,128)(2,1)S(1)} %reduce-precision_convert_fusion.4.refs_2_, bf16[256,512]{1,0:T(8,128)(2,1)S(1)} %get-tuple-element.67.refs_3_, ...), custom_call_target="tpu_custom_call" | custom-call | tf_op jit(solution)/shard_map/expand_step/pallas_call | solution.py:352
  (77 shorter events, 6.6 us)
Async XLA Ops:
  0.0 1.6 %copy-start.2 = (f32[4096,128]{1,0:T(8,128)S(1)}, f32[4096,128]{1,0:T(8,128)}, u32[]{:S(2)}) copy-start(f32[4096,128]{1,0:T(8,128)} %shrink_ref.1) | copy-start | bytes 6291460
  1.6 0.9 %copy-start.3 = (f32[8,16,512]{2,1,0:T(8,128)S(1)}, f32[8,16,512]{2,1,0:T(8,128)}, u32[]{:S(2)}) copy-start(f32[8,16,512]{2,1,0:T(8,128)} %param.13) | copy-start | bytes 786436
  2.5 6.2 %copy-start.4 = (s32[4,4]{1,0:T(4,128)S(1)}, s32[4,4]{1,0:T(4,128)}, u32[]{:S(2)}) copy-start(s32[4,4]{1,0:T(4,128)} %constant.56.clone.refs_0_) | copy-start | bytes 196
  2.7 7.6 %copy-start = (bf16[256,4096]{1,0:T(8,128)(2,1)S(1)}, bf16[256,4096]{1,0:T(8,128)(2,1)}, u32[]{:S(2)}) copy-start(bf16[256,4096]{1,0:T(8,128)(2,1)} %refs_4_.3) | copy-start | bytes 6291460
  2.7 7.6 %copy-start.5 = (s32[256]{0:T(256)S(1)}, s32[256]{0:T(256)}, u32[]{:S(2)}) copy-start(s32[256]{0:T(256)} %param.9) | copy-start | bytes 3076
  2.7 7.6 %copy-start.6 = (s32[64]{0:T(128)S(1)}, s32[64]{0:T(128)}, u32[]{:S(2)}) copy-start(s32[64]{0:T(128)} %refs_3_.1) | copy-start | bytes 772
  2.9 15.0 %collective-permute-start.1 = (f16[1280,128]{1,0:T(8,128)(2,1)S(1)}, f16[1280,128]{1,0:T(8,128)(2,1)S(1)}, u32[]{:S(2)}, u32[]{:S(2)}) collective-permute-start(f16[1280,128]{1,0:T(8,128)(2,1)S(1)} %multiply_convert_fusion), channel_id=1, source_target_pairs={{0,4},{2,6},{4,0},{6,2},{8,12},{10,14},{12,8},{14,10},{1,5},{3,7},... | collective-permute-start | bytes 983048 | tf_op jit(solution)/shard_map/ppermute | solution.py:36
  6.0 11.9 %collective-permute-start.2 = (f16[1280,128]{1,0:T(8,128)(2,1)S(1)}, f16[1280,128]{1,0:T(8,128)(2,1)S(1)}, u32[]{:S(2)}, u32[]{:S(2)}) collective-permute-start(f16[1280,128]{1,0:T(8,128)(2,1)S(1)} %multiply_convert_fusion), channel_id=1, source_target_pairs={{4,8},{6,10},{8,4},{10,6},{5,9},{7,11},{9,5},{11,7},{20,24},{22,26... | collective-permute-start | bytes 983048 | tf_op jit(solution)/shard_map/ppermute | solution.py:36
  8.5 1.7 %collective-permute-start = (f16[1024,128]{1,0:T(8,128)(2,1)}, f16[1024,128]{1,0:T(8,128)(2,1)S(1)}, u32[]{:S(2)}, u32[]{:S(2)}) collective-permute-start(f16[1024,128]{1,0:T(8,128)(2,1)} %multiply_convert_fusion.1), channel_id=1, source_target_pairs={{0,2},{2,0},{4,6},{6,4},{8,10},{10,8},{12,14},{14,12},{1,3},{3,1},... | collective-permute-start | bytes 786440 | tf_op jit(solution)/shard_map/ppermute | solution.py:377
  10.3 9.7 %copy-start.7 = (f16[512,512]{1,0:T(8,128)(2,1)S(1)}, f16[512,512]{1,0:T(8,128)(2,1)}, u32[]{:S(2)}) copy-start(f16[512,512]{1,0:T(8,128)(2,1)} %maximum_dynamic-update-slice_fusion.3) | copy-start | bytes 1572868
  11.1 34.1 %collective-permute-start.11 = (bf16[544,1024]{1,0:T(8,128)(2,1)S(1)}, bf16[544,1024]{1,0:T(8,128)(2,1)S(1)}, u32[]{:S(2)}, u32[]{:S(2)}) collective-permute-start(bf16[544,1024]{1,0:T(8,128)(2,1)S(1)} %get-tuple-element.52), channel_id=1, source_target_pairs={{0,16},{16,0},{1,17},{17,1},{2,18},{18,2},{3,19},{19,3},{4,20},{20... | collective-permute-start | bytes 3342344 | tf_op jit(solution)/shard_map/ppermute | solution.py:380
  12.7 10.8 %collective-permute-start.5 = (f16[1024,128]{1,0:T(8,128)(2,1)S(1)}, f16[1024,128]{1,0:T(8,128)(2,1)S(1)}, u32[]{:S(2)}, u32[]{:S(2)}) collective-permute-start(f16[1024,128]{1,0:T(8,128)(2,1)S(1)} %collective-permute-done), channel_id=1, source_target_pairs={{0,4},{2,6},{4,0},{6,2},{8,12},{10,14},{12,8},{14,10},{1,5},{3,7},... | collective-permute-start | bytes 786440 | tf_op jit(solution)/shard_map/ppermute | solution.py:36
  17.0 6.4 %collective-permute-start.6 = (f16[1024,128]{1,0:T(8,128)(2,1)S(1)}, f16[1024,128]{1,0:T(8,128)(2,1)S(1)}, u32[]{:S(2)}, u32[]{:S(2)}) collective-permute-start(f16[1024,128]{1,0:T(8,128)(2,1)S(1)} %collective-permute-done), channel_id=1, source_target_pairs={{4,8},{6,10},{8,4},{10,6},{5,9},{7,11},{9,5},{11,7},{20,24},{22,26... | collective-permute-start | bytes 786440 | tf_op jit(solution)/shard_map/ppermute | solution.py:36
  18.0 14.2 %collective-permute-start.8 = (f16[1280,128]{1,0:T(8,128)(2,1)S(1)}, f16[1280,128]{1,0:T(8,128)(2,1)S(1)}, u32[]{:S(2)}, u32[]{:S(2)}) collective-permute-start(f16[1280,128]{1,0:T(8,128)(2,1)S(1)} %collective-permute-done.1), channel_id=1, source_target_pairs={{4,8},{6,10},{8,4},{10,6},{5,9},{7,11},{9,5},{11,7},{20,24},{22,26... | collective-permute-start | bytes 983048 | tf_op jit(solution)/shard_map/ppermute | solution.py:36
  18.7 13.2 %collective-permute-start.3 = (f16[1280,128]{1,0:T(8,128)(2,1)S(1)}, f16[1280,128]{1,0:T(8,128)(2,1)S(1)}, u32[]{:S(2)}, u32[]{:S(2)}) collective-permute-start(f16[1280,128]{1,0:T(8,128)(2,1)S(1)} %collective-permute-done.2), channel_id=1, source_target_pairs={{4,0},{6,2},{8,12},{10,14},{5,1},{7,3},{9,13},{11,15},{20,16},{22,... | collective-permute-start | bytes 983048 | tf_op jit(solution)/shard_map/ppermute | solution.py:36
  23.5 10.2 %collective-permute-start.13 = (f16[1024,128]{1,0:T(8,128)(2,1)S(1)}, f16[1024,128]{1,0:T(8,128)(2,1)S(1)}, u32[]{:S(2)}, u32[]{:S(2)}) collective-permute-start(f16[1024,128]{1,0:T(8,128)(2,1)S(1)} %collective-permute-done.5), channel_id=1, source_target_pairs={{4,8},{6,10},{8,4},{10,6},{5,9},{7,11},{9,5},{11,7},{20,24},{22,26... | collective-permute-start | bytes 786440 | tf_op jit(solution)/shard_map/ppermute | solution.py:36
  24.2 13.2 %collective-permute-start.7 = (f16[1024,128]{1,0:T(8,128)(2,1)S(1)}, f16[1024,128]{1,0:T(8,128)(2,1)S(1)}, u32[]{:S(2)}, u32[]{:S(2)}) collective-permute-start(f16[1024,128]{1,0:T(8,128)(2,1)S(1)} %collective-permute-done.6), channel_id=1, source_target_pairs={{4,0},{6,2},{8,12},{10,14},{5,1},{7,3},{9,13},{11,15},{20,16},{22,... | collective-permute-start | bytes 786440 | tf_op jit(solution)/shard_map/ppermute | solution.py:36
  32.0 7.0 %copy-start.1 = (bf16[256,4096]{1,0:T(8,128)(2,1)S(1)}, bf16[256,4096]{1,0:T(8,128)(2,1)}, u32[]{:S(2)}) copy-start(bf16[256,4096]{1,0:T(8,128)(2,1)} %refs_4_.3) | copy-start | bytes 6291460
  32.1 6.9 %collective-permute-start.4 = (bf16[272,1024]{1,0:T(8,128)(2,1)S(1)}, bf16[272,1024]{1,0:T(8,128)(2,1)S(1)}, u32[]{:S(2)}, u32[]{:S(2)}) collective-permute-start(bf16[272,1024]{1,0:T(8,128)(2,1)S(1)} %get-tuple-element.41), channel_id=1, source_target_pairs={{0,2},{2,0},{4,6},{6,4},{8,10},{10,8},{12,14},{14,12},{1,3},{3,1},... | collective-permute-start | bytes 1671176 | tf_op jit(solution)/shard_map/ppermute | solution.py:377
  32.2 13.0 %collective-permute-start.9 = (f16[1280,128]{1,0:T(8,128)(2,1)S(1)}, f16[1280,128]{1,0:T(8,128)(2,1)S(1)}, u32[]{:S(2)}, u32[]{:S(2)}) collective-permute-start(f16[1280,128]{1,0:T(8,128)(2,1)S(1)} %collective-permute-done.8), channel_id=1, source_target_pairs={{4,0},{6,2},{8,12},{10,14},{5,1},{7,3},{9,13},{11,15},{20,16},{22,... | collective-permute-start | bytes 983048 | tf_op jit(solution)/shard_map/ppermute | solution.py:36
  33.7 16.8 %collective-permute-start.14 = (f16[1024,128]{1,0:T(8,128)(2,1)S(1)}, f16[1024,128]{1,0:T(8,128)(2,1)S(1)}, u32[]{:S(2)}, u32[]{:S(2)}) collective-permute-start(f16[1024,128]{1,0:T(8,128)(2,1)S(1)} %collective-permute-done.13), channel_id=1, source_target_pairs={{4,0},{6,2},{8,12},{10,14},{5,1},{7,3},{9,13},{11,15},{20,16},{22,... | collective-permute-start | bytes 786440 | tf_op jit(solution)/shard_map/ppermute | solution.py:36
  37.3 21.1 %collective-permute-start.17 = (f32[256,512]{1,0:T(8,128)S(1)}, f32[256,512]{1,0:T(8,128)S(1)}, u32[]{:S(2)}, u32[]{:S(2)}) collective-permute-start(f32[256,512]{1,0:T(8,128)S(1)} %base_product.2), channel_id=1, source_target_pairs={{0,1},{1,0},{2,3},{3,2},{4,5},{5,4},{6,7},{7,6},{8,9},{9,8},{10,11... | collective-permute-start | bytes 1572872 | tf_op jit(solution)/shard_map/ppermute | solution.py:426
  45.3 2.0 %collective-permute-start.12 = (bf16[272,1024]{1,0:T(8,128)(2,1)S(1)}, bf16[272,1024]{1,0:T(8,128)(2,1)S(1)}, u32[]{:S(2)}, u32[]{:S(2)}) collective-permute-start(bf16[272,1024]{1,0:T(8,128)(2,1)S(1)} %slice.145), channel_id=1, source_target_pairs={{0,2},{2,0},{4,6},{6,4},{8,10},{10,8},{12,14},{14,12},{1,3},{3,1},... | collective-permute-start | bytes 1671176 | tf_op jit(solution)/shard_map/ppermute | solution.py:377
  45.7 8.8 %collective-permute-start.10 = (f16[256,512]{1,0:T(8,128)(2,1)S(1)}, f16[256,512]{1,0:T(8,128)(2,1)S(1)}, u32[]{:S(2)}, u32[]{:S(2)}) collective-permute-start(f16[256,512]{1,0:T(8,128)(2,1)S(1)} %get-tuple-element.68), channel_id=1, source_target_pairs={{0,16},{16,0},{1,17},{17,1},{2,18},{18,2},{3,19},{19,3},{4,20},{20... | collective-permute-start | bytes 786440 | tf_op jit(solution)/shard_map/ppermute | solution.py:380
  52.8 1.3 %collective-permute-start.15 = (f32[16,512]{1,0:T(8,128)S(1)}, f32[16,512]{1,0:T(8,128)S(1)}, u32[]{:S(2)}, u32[]{:S(2)}) collective-permute-start(f32[16,512]{1,0:T(8,128)S(1)} %get-tuple-element.63), channel_id=1, source_target_pairs={{0,2},{2,0},{4,6},{6,4},{8,10},{10,8},{12,14},{14,12},{1,3},{3,1},... | collective-permute-start | bytes 98312 | tf_op jit(solution)/shard_map/ppermute | solution.py:377
  54.5 3.8 %collective-permute-start.16 = (f16[512,512]{1,0:T(8,128)(2,1)S(1)}, f16[512,512]{1,0:T(8,128)(2,1)S(1)}, u32[]{:S(2)}, u32[]{:S(2)}) collective-permute-start(f16[512,512]{1,0:T(8,128)(2,1)S(1)} %constant_dynamic-update-slice_fusion), channel_id=1, source_target_pairs={{0,2},{2,0},{4,6},{6,4},{8,10},{10,8},{12,14},{14,12},{1,3},{3,1},... | collective-permute-start | bytes 1572872 | tf_op jit(solution)/shard_map/ppermute | solution.py:377
  54.6 4.8 %collective-permute-start.18 = (f32[16,256]{1,0:T(8,128)S(1)}, f32[16,256]{1,0:T(8,128)S(1)}, u32[]{:S(2)}, u32[]{:S(2)}) collective-permute-start(f32[16,256]{1,0:T(8,128)S(1)} %get-tuple-element.105), channel_id=1, source_target_pairs={{0,17},{1,16},{16,1},{17,0},{2,19},{3,18},{18,3},{19,2},{4,21},{5,... | collective-permute-start | bytes 49160 | tf_op jit(solution)/shard_map/ppermute | solution.py:492
  56.3 3.7 %collective-permute-start.19 = (f32[16,256]{1,0:T(8,128)S(1)}, f32[16,256]{1,0:T(8,128)S(1)}, u32[]{:S(2)}, u32[]{:S(2)}) collective-permute-start(f32[16,256]{1,0:T(8,128)S(1)} %get-tuple-element.105), channel_id=1, source_target_pairs={{0,16},{16,0},{1,17},{17,1},{2,18},{18,2},{3,19},{19,3},{4,20},{20... | collective-permute-start | bytes 49160 | tf_op jit(solution)/shard_map/ppermute | solution.py:380
  57.6 3.7 %collective-permute-start.20 = (f32[16,256]{1,0:T(8,128)S(1)}, f32[16,256]{1,0:T(8,128)S(1)}, u32[]{:S(2)}, u32[]{:S(2)}) collective-permute-start(f32[16,256]{1,0:T(8,128)S(1)} %get-tuple-element.106.refs_10_), channel_id=1, source_target_pairs={{0,1},{1,0},{2,3},{3,2},{4,5},{5,4},{6,7},{7,6},{8,9},{9,8},{10,11... | collective-permute-start | bytes 49160 | tf_op jit(solution)/shard_map/ppermute | solution.py:494
